TPU v7x, 32 devices: a whole 2x2x4 slice. The times are simulated.
32 devices in a mesh: space: 8 (over z, y), tile: 4 (over x, core).
Axes of the slice: x: 2, y: 2, z: 4, core: 2. Of those that a mesh axis runs over, the one named last changes fastest.
Arguments:
- features: bfloat16 [8, 4, 64, 8, 8, 256], P('space', 'tile'), may hold values from -6 to 6
- weight: bfloat16 [3, 3, 3, 32, 32], replicated, may hold values from -0.21875 to 0.21875
- bias_vector: float32 [32], replicated, may hold values from -4 to 4
- cotangent: bfloat16 [8, 4, 64, 8, 8, 256], P('space', 'tile'), may hold values from -6 to 6
- counts: int32 [8, 4], P('space', 'tile'), may hold values from 8 to 64, as said below
- send_slots: int32 [8, 4, 8, 16], P('space', 'tile'), may hold values from 0 to 63
- neighbours: int32 [8, 4, 64, 26], P('space', 'tile'), may hold values from 0 to 192, as said below
Outputs:
- output: bfloat16 [8, 4, 64, 8, 8, 256], P('space', 'tile')
- input_grad: bfloat16 [8, 4, 64, 8, 8, 256], P('space', 'tile')
- weight_grad: float32 [3, 3, 3, 32, 32], replicated
- bias_grad: float32 [32], replicated
Inputs may be any that keep to these rules, and one draw needn't show every extreme that they name: `counts`: some device has all 64 slots active in every draw. `send_slots`: slots may repeat and may name inactive slots. `neighbours`: indices below 64 are the device's own slots, the next 128 its imported bricks in direction order, and 192 the zero brick, which some entry names in every draw.
All inputs are finite; a program needn't handle non-finite values.
Results may differ from a plain program's by a relative error of at most 0.0019.
Values may be sent and summed in bfloat16 or wider, within the bound.
No kernel may reach another device: no remote copies, remote signals or barrier semaphores. Data moves between devices by JAX's collectives and lax.ppermute only.
A program may use at most 256 MiB of HBM per device.

v0:
```python
import jax
import jax.numpy as jnp
import numpy as np
from jax import lax
from jax.sharding import PartitionSpec as P

NEIGHBOUR_SIDES = [
    (x_side, y_side, z_side)
    for x_side in (-1, 0, 1)
    for y_side in (-1, 0, 1)
    for z_side in (-1, 0, 1)
    if (x_side, y_side, z_side) != (0, 0, 0)
]


def from_behind(value, axis, by):
    devices = lax.axis_size(axis)
    pairs = [(i, i + by) for i in range(devices) if 0 <= i + by < devices]
    return lax.ppermute(value, axis, pairs)


def for_sending(value):
    return jax.tree.map(lambda a: a.astype(jnp.bfloat16) if a.dtype == jnp.float32 else a, value)


def side_ranges(side_value):
    if side_value < 0:
        return (7, 8)
    if side_value > 0:
        return (0, 1)
    return (0, 8)


def face_cut(table, sides, channels):
    x_start, x_stop = side_ranges(sides[0])
    y_start, y_stop = side_ranges(sides[1])
    z_start, z_stop = side_ranges(sides[2])
    return table[:, x_start:x_stop, y_start:y_stop, z_start * channels : z_stop * channels]


def assemble_faces(own_bricks, near_faces):
    rows_x = []
    for x_side in (-1, 0, 1):
        rows_y = []
        for y_side in (-1, 0, 1):
            pieces = []
            for z_side in (-1, 0, 1):
                if (x_side, y_side, z_side) == (0, 0, 0):
                    pieces.append(own_bricks)
                else:
                    pieces.append(near_faces[NEIGHBOUR_SIDES.index((x_side, y_side, z_side))])
            rows_y.append(jnp.concatenate(pieces, axis=3))
        rows_x.append(jnp.concatenate(rows_y, axis=2))
    return jnp.concatenate(rows_x, axis=1)


def columns_faces(own_bricks, near_faces, channels):
    volume = assemble_faces(own_bricks, near_faces)
    shifted = [
        volume[:, x_shift : x_shift + 8, y_shift : y_shift + 8, :]
        for x_shift in range(3)
        for y_shift in range(3)
    ]
    stacked = jnp.stack(shifted, axis=3)
    return stacked.reshape(own_bricks.shape[0] * 64, 90 * channels)


def band_weights(weight_wide, channels):
    selector = np.zeros((3, 10, 8), np.float32)
    for depth_step in range(3):
        for plane_index in range(8):
            selector[depth_step, plane_index + depth_step, plane_index] = 1.0
    band_matrix = jnp.einsum(
        "kpq,abkio->abpiqo",
        jnp.asarray(selector, weight_wide.dtype),
        weight_wide,
        precision=lax.Precision.HIGHEST,
    )
    return band_matrix.reshape(90 * channels, 8 * channels)


def to_grid(by_side):
    center = jnp.zeros((1,) + by_side.shape[1:], by_side.dtype)
    joined = jnp.concatenate([by_side[:4], center, by_side[4:]], axis=0)
    return joined.reshape((3, 3) + by_side.shape[1:])


def from_grid(side_grid):
    flat_grid = side_grid.reshape((9,) + side_grid.shape[2:])
    return jnp.concatenate([flat_grid[:4], flat_grid[5:]], axis=0)


def tile_out(side_grid):
    received = [from_behind(side_grid[:, 1 + shift_by], "tile", shift_by) for shift_by in (-1, 1)]
    return jnp.stack([received[0], side_grid[:, 1], received[1]], axis=1)


def space_out(side_grid):
    received = [from_behind(side_grid[1 + shift_by], "space", shift_by) for shift_by in (-1, 1)]
    return jnp.stack([received[0], side_grid[1], received[1]], axis=0)


def tile_back(side_grid):
    received = [
        from_behind(side_grid[:, 1 + shift_by].astype(jnp.bfloat16), "tile", -shift_by).astype(
            jnp.float32
        )
        for shift_by in (-1, 1)
    ]
    return jnp.stack([received[0], side_grid[:, 1], received[1]], axis=1)


def space_back(side_grid):
    received = [
        from_behind(for_sending(side_grid[1 + shift_by]), "space", -shift_by)
        for shift_by in (-1, 1)
    ]
    return jnp.stack([received[0], side_grid[1], received[1]], axis=0)


def route_out(by_side):
    result = from_grid(space_out(tile_out(to_grid(by_side))))
    return result


def route_back(by_side):
    result = from_grid(space_back(tile_back(to_grid(by_side))))
    return result


def local(features, weight, bias_vector, cotangent, counts, send_slots, neighbours):
    channels = weight.shape[-1]
    slot_count = features.shape[2]
    per_side = send_slots.shape[-1]
    row_width = 8 * channels
    table_rows = slot_count + 8 * per_side + 1
    block_size = min(16, slot_count)
    count_here = counts[0, 0]
    active = (jnp.arange(slot_count, dtype=jnp.int32) < count_here).astype(jnp.bfloat16)[
        :, None, None, None
    ]
    masked = features[0, 0] * active
    grads_in = cotangent[0, 0] * active
    slot_list = send_slots[0, 0].reshape(-1)
    outgoing = masked[slot_list].reshape(8, per_side, 8, 8, row_width)
    arrived = route_out(outgoing).reshape(8 * per_side, 8, 8, row_width)
    zero_brick = jnp.zeros((1, 8, 8, row_width), jnp.bfloat16)
    brick_table = jnp.concatenate([masked, arrived, zero_brick], axis=0)
    face_tables = [face_cut(brick_table, sides, channels) for sides in NEIGHBOUR_SIDES]
    band_matrix = band_weights(weight.astype(jnp.float32), channels).astype(jnp.bfloat16)
    bias_row = jnp.tile(bias_vector, 8)
    near_index = neighbours[0, 0]

    def column_map(own_bricks, near_faces):
        return columns_faces(own_bricks, near_faces, channels)

    def step_block(turn_index, state_now):
        outputs, own_sum, face_sums, band_grad, bias_grad = state_now
        first_slot = turn_index * block_size
        own_bricks = lax.dynamic_slice_in_dim(masked, first_slot, block_size, 0)
        near_rows = lax.dynamic_slice_in_dim(near_index, first_slot, block_size, 0)
        near_faces = tuple(
            (face_tables[side_index][near_rows[:, side_index]] for side_index in range(26))
        )
        column_rows = column_map(own_bricks, near_faces)
        live_mask = lax.dynamic_slice_in_dim(active, first_slot, block_size, 0).astype(jnp.float32)
        out_sums = jnp.dot(column_rows, band_matrix, preferred_element_type=jnp.float32) + bias_row
        out_rows = (out_sums.reshape(block_size, 8, 8, row_width) * live_mask).astype(jnp.bfloat16)
        outputs = lax.dynamic_update_slice_in_dim(outputs, out_rows, first_slot, 0)
        g_rows = lax.dynamic_slice_in_dim(grads_in, first_slot, block_size, 0).reshape(
            block_size * 64, row_width
        )
        col_grads = lax.dot_general(
            g_rows, band_matrix, (((1,), (1,)), ((), ())), preferred_element_type=jnp.float32
        )
        band_grad = band_grad + lax.dot_general(
            column_rows, g_rows, (((0,), (0,)), ((), ())), preferred_element_type=jnp.float32
        )
        bias_grad = bias_grad + jnp.sum(g_rows.astype(jnp.float32), axis=0)
        own_zero = jnp.zeros(own_bricks.shape, jnp.float32)
        face_zero = tuple((jnp.zeros(piece.shape, jnp.float32) for piece in near_faces))
        unused, pull_back = jax.vjp(column_map, own_zero, face_zero)
        own_grad, face_grads = pull_back(col_grads)
        face_sums = tuple(
            (
                face_sums[side_index].at[near_rows[:, side_index]].add(face_grads[side_index])
                for side_index in range(26)
            )
        )
        current = lax.dynamic_slice_in_dim(own_sum, first_slot, block_size, 0)
        own_sum = lax.dynamic_update_slice_in_dim(own_sum, current + own_grad, first_slot, 0)
        return (outputs, own_sum, face_sums, band_grad, bias_grad)

    initial = (
        jnp.zeros((slot_count, 8, 8, row_width), jnp.bfloat16),
        jnp.zeros((slot_count, 8, 8, row_width), jnp.float32),
        tuple((jnp.zeros(piece.shape, jnp.float32) for piece in face_tables)),
        jnp.zeros((90 * channels, row_width), jnp.float32),
        jnp.zeros((row_width,), jnp.float32),
    )
    turn_count = slot_count // block_size
    outputs, own_sum, face_sums, band_grad, bias_grad = lax.fori_loop(
        0, turn_count, step_block, initial
    )
    table_grad = jnp.zeros((table_rows, 8, 8, row_width), jnp.float32)
    for side_index, sides in enumerate(NEIGHBOUR_SIDES):
        x_start, x_stop = side_ranges(sides[0])
        y_start, y_stop = side_ranges(sides[1])
        z_start, z_stop = side_ranges(sides[2])
        table_grad = table_grad.at[
            :, x_start:x_stop, y_start:y_stop, z_start * channels : z_stop * channels
        ].add(face_sums[side_index])
    returning = table_grad[slot_count : slot_count + 8 * per_side].reshape(
        8, per_side, 8, 8, row_width
    )
    back_rows = route_back(returning).reshape(8 * per_side, 64 * row_width)
    chooser = (jnp.arange(slot_count, dtype=jnp.int32)[:, None] == slot_list[None, :]).astype(
        jnp.float32
    )
    returned = jnp.dot(
        chooser, back_rows, precision=lax.Precision.HIGHEST, preferred_element_type=jnp.float32
    )
    summed = table_grad[:slot_count] + own_sum + returned.reshape(slot_count, 8, 8, row_width)
    input_grad = (summed * active.astype(jnp.float32)).astype(jnp.bfloat16)

    def band_map(weight_wide):
        return band_weights(weight_wide, channels)

    unused, pull_weight = jax.vjp(band_map, jnp.zeros(weight.shape, jnp.float32))
    weight_local = pull_weight(band_grad)[0]
    bias_local = jnp.sum(bias_grad.reshape(8, channels), axis=0)
    weight_total, bias_total = lax.psum((weight_local, bias_local), ("space", "tile"))
    grad_scale = float(lax.axis_size("space") * lax.axis_size("tile") * slot_count * 512) ** (-0.5)
    return (
        outputs[None, None],
        input_grad[None, None],
        weight_total * grad_scale,
        bias_total * grad_scale,
    )


def solution(mesh):
    placed = (
        P("space", "tile", None, None, None, None),
        P(),
        P(),
        P("space", "tile", None, None, None, None),
        P("space", "tile"),
        P("space", "tile", None, None),
        P("space", "tile", None, None),
    )
    return jax.shard_map(
        local,
        mesh=mesh,
        in_specs=placed,
        out_specs=(
            P("space", "tile", None, None, None, None),
            P("space", "tile", None, None, None, None),
            P(),
            P(),
        ),
        check_vma=False,
    )
```

profile of v0, /device:TPU:0, one launch (start us, length us, event | category | flops | bytes accessed | tf_op | source)
XLA Modules:
  0.0 1470.7 jit_solution(11683220474337546024)
XLA Ops:
  31.4 7.1 collective-permute-start.3
  41.1 8.5 convert_bitcast_fusion
  49.6 6.8 copy.233
  56.4 8.1 convert_element_type.81
  70.3 34.2 %collective-permute-done.3 = bf16[3,16,8,8,256]{4,3,2,1,0:T(8,128)(2,1)} collective-permute-done((bf16[3,16,8,8,256]{4,3,2,1,0:T(8,128)(2,1)}, bf16[3,16,8,8,256]{4,3,2,1,0:T(8,128)(2,1)}, u32[]{:S(2)}, u32[]{:S(2)}) %collective-permute-start.3) | collective-permute-done | bytes 1572896 | tf_op jit(solution)/shard_map/ppermute | solution.py:19
  120.4 4.2 fusion.94
  136.2 4.6 copy.240
  179.2 840.2 %while.98 = (s32[]{:T(128)}, bf16[64,8,8,256]{3,2,1,0:T(8,128)(2,1)}, f32[64,8,8,256]{3,0,2,1:T(8,128)}, f32[193,1,1,32]{3,0,2,1:T(8,128)}, f32[193,1,1,256]{3,0...) while((s32[]{:T(128)}, ...), condition=%wide.region_28.0_spmd.clone, body=%wide.region_0.0_spmd.clone.sunk | while | flops 4560350720 | bytes 173589968 | solution.py:202
  202.7 7.6 fusion.160
  210.2 9.4 slice_bitcast_fusion.34
  219.6 5.2 pad_add_fusion.5
  286.0 20.7 %copy.393 = bf16[16,8,8,9,320]{4,3,2,1,0:T(8,128)(2,1)} copy(bf16[16,8,8,9,320]{4,2,1,0,3:T(8,128)(2,1)S(1)} %fusion.157) | data formatting | bytes 11796480 | tf_op jit(solution)/shard_map/while/body/eval_jaxpr/stack | solution.py:64
  306.7 15.3 %reshape.2170 = bf16[1024,2880]{1,0:T(8,128)(2,1)} reshape(bf16[16,8,8,9,320]{4,3,2,1,0:T(8,128)(2,1)} %copy.393) | data formatting | bytes 11796480 | tf_op jit(solution)/shard_map/while/body/eval_jaxpr/reshape | solution.py:65
  322.1 6.1 convolution_add_fusion.5
  329.0 4.5 convolution_add_fusion.4
  405.1 7.6 fusion.160
  412.7 9.4 slice_bitcast_fusion.34
  422.1 5.2 pad_add_fusion.5
  480.1 4.2 pad_maximum_fusion.34
  488.4 20.7 %copy.393 = bf16[16,8,8,9,320]{4,3,2,1,0:T(8,128)(2,1)} copy(bf16[16,8,8,9,320]{4,2,1,0,3:T(8,128)(2,1)S(1)} %fusion.157) | data formatting | bytes 11796480 | tf_op jit(solution)/shard_map/while/body/eval_jaxpr/stack | solution.py:64
  509.1 15.3 %reshape.2170 = bf16[1024,2880]{1,0:T(8,128)(2,1)} reshape(bf16[16,8,8,9,320]{4,3,2,1,0:T(8,128)(2,1)} %copy.393) | data formatting | bytes 11796480 | tf_op jit(solution)/shard_map/while/body/eval_jaxpr/reshape | solution.py:65
  524.4 7.0 convolution_add_fusion.5
  532.2 4.5 convolution_add_fusion.4
  608.4 7.6 fusion.160
  616.0 9.4 slice_bitcast_fusion.34
  625.4 5.2 pad_add_fusion.5
  683.4 4.2 pad_maximum_fusion.34
  691.7 20.7 %copy.393 = bf16[16,8,8,9,320]{4,3,2,1,0:T(8,128)(2,1)} copy(bf16[16,8,8,9,320]{4,2,1,0,3:T(8,128)(2,1)S(1)} %fusion.157) | data formatting | bytes 11796480 | tf_op jit(solution)/shard_map/while/body/eval_jaxpr/stack | solution.py:64
  712.4 15.3 %reshape.2170 = bf16[1024,2880]{1,0:T(8,128)(2,1)} reshape(bf16[16,8,8,9,320]{4,3,2,1,0:T(8,128)(2,1)} %copy.393) | data formatting | bytes 11796480 | tf_op jit(solution)/shard_map/while/body/eval_jaxpr/reshape | solution.py:65
  727.7 7.0 convolution_add_fusion.5
  735.5 4.5 convolution_add_fusion.4
  811.7 7.6 fusion.160
  819.2 9.4 slice_bitcast_fusion.34
  828.7 5.2 pad_add_fusion.5
  886.7 4.2 pad_maximum_fusion.34
  894.9 20.7 %copy.393 = bf16[16,8,8,9,320]{4,3,2,1,0:T(8,128)(2,1)} copy(bf16[16,8,8,9,320]{4,2,1,0,3:T(8,128)(2,1)S(1)} %fusion.157) | data formatting | bytes 11796480 | tf_op jit(solution)/shard_map/while/body/eval_jaxpr/stack | solution.py:64
  915.7 15.3 %reshape.2170 = bf16[1024,2880]{1,0:T(8,128)(2,1)} reshape(bf16[16,8,8,9,320]{4,3,2,1,0:T(8,128)(2,1)} %copy.393) | data formatting | bytes 11796480 | tf_op jit(solution)/shard_map/while/body/eval_jaxpr/reshape | solution.py:65
  931.0 7.0 convolution_add_fusion.5
  938.8 4.5 convolution_add_fusion.4
  1019.4 7.0 scatter-add.416
  1031.3 5.6 scatter-add.419
  1040.5 5.0 scatter-add.421
  1053.0 5.6 scatter-add.425
  1062.1 4.9 scatter-add.427
  1067.0 11.3 slice_add_fusion.2
  1078.2 38.5 %scatter-add.428 = f32[193,8,8,256]{3,0,2,1:T(8,128)} dynamic-update-slice(f32[193,8,8,256]{3,0,2,1:T(8,128)} %scatter-add.427, f32[193,8,8,32]{3,0,2,1:T(8,128)} %slice_add_fusion.2, s32[]{:T(128)} %constant.809.clone.1, s32[]{:T(128)} %constant.809.clone.1, s32[]{:T(128)} %constant.809.clone.1, s32[]{:T(128)} %constant.814.clone.1) | dynamic-update-slice | bytes 3162116 | tf_op jit(solution)/shard_map/scatter-add | solution.py:212
  1116.7 11.1 slice_add_fusion.1
  1127.8 31.8 %scatter-add.429 = f32[193,8,8,256]{3,0,2,1:T(8,128)} dynamic-update-slice(f32[193,8,8,256]{3,0,2,1:T(8,128)} %scatter-add.428, f32[193,8,8,32]{3,0,2,1:T(8,128)} %slice_add_fusion.1, s32[]{:T(128)} %constant.809.clone.1, s32[]{:T(128)} %constant.809.clone.1, s32[]{:T(128)} %constant.809.clone.1, s32[]{:T(128)} %constant.809.clone.1) | dynamic-update-slice | bytes 3162116 | tf_op jit(solution)/shard_map/scatter-add | solution.py:212
  1163.1 6.9 scatter-add.430
  1173.4 4.9 scatter-add.432
  1190.4 6.8 scatter-add.436
  1200.8 4.9 scatter-add.438
  1216.2 4.4 copy.263
  1220.6 4.4 copy.264
  1225.0 4.5 pad_maximum_fusion.13
  1243.8 8.1 reshape.1114
  1252.0 6.2 collective-permute-start.6
  1258.3 9.9 fusion.63
  1268.2 82.8 %psum.15 = f32[32]{0:T(128)S(1)} all-reduce(f32[32]{0:T(128)S(1)} %reduce_sum.22), channel_id=1, replica_groups=mesh['space'=8,'tile'=4] {'space','tile'}, use_global_device_ids=true, to_apply=%region_34.0 | all-reduce | flops 32 | bytes 256 | tf_op jit(solution)/shard_map/psum | solution.py:232
  1351.5 62.2 %all-reduce.12.cloned.1.call-done = f32[3,3,3,32,32]{4,2,3,1,0:T(4,128)} async-done(((f32[3,3,3,32,32]{4,2,3,1,0:T(4,128)}), f32[3,3,3,32,32]{4,2,3,1,0:T(4,128)}) %all-reduce.12.cloned.1.call-update) | async-done | bytes 110608 | tf_op jit(solution)/shard_map/psum | solution.py:232
  1427.5 4.2 pad_maximum_fusion.16
  1431.7 9.5 reshape.1113
  1441.2 9.0 copy.267
  1450.2 11.0 fusion.62
  (890 shorter events, 699.5 us)
Async XLA Ops:
  7.2 1406.5 %all-reduce.12.cloned.1.call-start = ((), (), s32[]{:S(2)}) async-start(), calls=%async_computation | async-start | bytes 1179648 | tf_op jit(solution)/shard_map/psum | solution.py:232
  19.8 5.3 collective-permute-start
  21.1 6.1 collective-permute-start.1
  29.9 40.4 %collective-permute-start.2 = (bf16[3,16,8,8,256]{4,3,2,1,0:T(8,128)(2,1)}, bf16[3,16,8,8,256]{4,3,2,1,0:T(8,128)(2,1)}, u32[]{:S(2)}, u32[]{:S(2)}) collective-permute-start(bf16[3,16,8,8,256]{4,3,2,1,0:T(8,128)(2,1)} %get-tuple-element.2071), channel_id=1, source_target_pairs={{4,0},{8,4},{12,8},{16,12},{20,16},{24,20},{28,24},{5,1},{9,5},{13... | collective-permute-start | bytes 4718600 | tf_op jit(solution)/shard_map/ppermute | solution.py:19
  31.4 73.2 %collective-permute-start.3 = (bf16[3,16,8,8,256]{4,3,2,1,0:T(8,128)(2,1)}, bf16[3,16,8,8,256]{4,3,2,1,0:T(8,128)(2,1)}, u32[]{:S(2)}, u32[]{:S(2)}) collective-permute-start(bf16[3,16,8,8,256]{4,3,2,1,0:T(8,128)(2,1)} %get-tuple-element.2072), channel_id=1, source_target_pairs={{0,4},{4,8},{8,12},{12,16},{16,20},{20,24},{24,28},{1,5},{5,9},{9,... | collective-permute-start | bytes 4718600 | tf_op jit(solution)/shard_map/ppermute | solution.py:19
  228.6 26.5 %copy-start.42 = (s32[16]{0:T(128)}, s32[16]{0:T(128)S(1)}, u32[]{:S(2)}) copy-start(s32[16]{0:T(128)S(1)} %get-tuple-element.2585) | copy-start | bytes 196 | tf_op jit(solution)/shard_map/while
  228.6 26.5 %copy-start.43 = (s32[16]{0:T(128)}, s32[16]{0:T(128)S(1)}, u32[]{:S(2)}) copy-start(s32[16]{0:T(128)S(1)} %get-tuple-element.2588) | copy-start | bytes 196 | tf_op jit(solution)/shard_map/while
  241.6 20.8 %copy-start.50 = (s32[16]{0:T(128)}, s32[16]{0:T(128)S(1)}, u32[]{:S(2)}) copy-start(s32[16]{0:T(128)S(1)} %get-tuple-element.2598) | copy-start | bytes 196 | tf_op jit(solution)/shard_map/while
  241.6 20.8 %copy-start.51 = (s32[16]{0:T(128)}, s32[16]{0:T(128)S(1)}, u32[]{:S(2)}) copy-start(s32[16]{0:T(128)S(1)} %get-tuple-element.2606) | copy-start | bytes 196 | tf_op jit(solution)/shard_map/while
  241.6 33.4 %copy-start.44 = (s32[16]{0:T(128)}, s32[16]{0:T(128)S(1)}, u32[]{:S(2)}) copy-start(s32[16]{0:T(128)S(1)} %get-tuple-element.2602) | copy-start | bytes 196 | tf_op jit(solution)/shard_map/while
  241.6 33.4 %copy-start.46 = (s32[16]{0:T(128)}, s32[16]{0:T(128)S(1)}, u32[]{:S(2)}) copy-start(s32[16]{0:T(128)S(1)} %get-tuple-element.2601) | copy-start | bytes 196 | tf_op jit(solution)/shard_map/while
  241.6 33.4 %copy-start.53 = (s32[16]{0:T(128)}, s32[16]{0:T(128)S(1)}, u32[]{:S(2)}) copy-start(s32[16]{0:T(128)S(1)} %get-tuple-element.2597) | copy-start | bytes 196 | tf_op jit(solution)/shard_map/while
  333.5 30.1 %copy-start.37 = (f32[193,1,1,256]{3,0,2,1:T(8,128)S(1)}, f32[193,1,1,256]{3,0,2,1:T(8,128)}, u32[]{:S(2)}) copy-start(f32[193,1,1,256]{3,0,2,1:T(8,128)} %get-tuple-element.2767) | copy-start | bytes 592900 | tf_op jit(solution)/shard_map/while
  333.5 30.8 %copy-start.34 = (f32[193,1,1,256]{3,0,2,1:T(8,128)S(1)}, f32[193,1,1,256]{3,0,2,1:T(8,128)}, u32[]{:S(2)}) copy-start(f32[193,1,1,256]{3,0,2,1:T(8,128)} %get-tuple-element.2773) | copy-start | bytes 592900 | tf_op jit(solution)/shard_map/while
  370.9 31.2 %copy-start.2 = (bf16[64,8,8,256]{3,2,1,0:T(8,128)(2,1)S(1)}, bf16[64,8,8,256]{3,2,1,0:T(8,128)(2,1)}, u32[]{:S(2)}) copy-start(bf16[64,8,8,256]{3,2,1,0:T(8,128)(2,1)} %copy-done.1) | copy-start | bytes 6291460 | tf_op jit(solution)/shard_map/while
  375.7 22.7 %copy-start.32 = (f32[193,1,1,256]{3,0,2,1:T(8,128)S(1)}, f32[193,1,1,256]{3,0,2,1:T(8,128)}, u32[]{:S(2)}) copy-start(f32[193,1,1,256]{3,0,2,1:T(8,128)} %get-tuple-element.2756) | copy-start | bytes 592900 | tf_op jit(solution)/shard_map/while
  375.7 23.6 %copy-start.45 = (s32[16]{0:T(128)S(1)}, s32[16]{0:T(128)}, u32[]{:S(2)}) copy-start(s32[16]{0:T(128)} %copy-done.44) | copy-start | bytes 196 | tf_op jit(solution)/shard_map/while
  375.7 25.9 %copy-start.52 = (f32[256]{0:T(256)S(1)}, f32[256]{0:T(256)}, u32[]{:S(2)}) copy-start(f32[256]{0:T(256)} %get-tuple-element.2653) | copy-start | bytes 3076 | tf_op jit(solution)/shard_map/while
  375.7 25.9 %copy-start.55 = (f32[256]{0:T(256)S(1)}, f32[256]{0:T(256)}, u32[]{:S(2)}) copy-start(f32[256]{0:T(256)} %get-tuple-element.2776) | copy-start | bytes 3076 | tf_op jit(solution)/shard_map/while
  431.0 26.5 %copy-start.42 = (s32[16]{0:T(128)}, s32[16]{0:T(128)S(1)}, u32[]{:S(2)}) copy-start(s32[16]{0:T(128)S(1)} %get-tuple-element.2585) | copy-start | bytes 196 | tf_op jit(solution)/shard_map/while
  431.0 26.5 %copy-start.43 = (s32[16]{0:T(128)}, s32[16]{0:T(128)S(1)}, u32[]{:S(2)}) copy-start(s32[16]{0:T(128)S(1)} %get-tuple-element.2588) | copy-start | bytes 196 | tf_op jit(solution)/shard_map/while
  444.0 20.8 %copy-start.50 = (s32[16]{0:T(128)}, s32[16]{0:T(128)S(1)}, u32[]{:S(2)}) copy-start(s32[16]{0:T(128)S(1)} %get-tuple-element.2598) | copy-start | bytes 196 | tf_op jit(solution)/shard_map/while
  444.0 20.8 %copy-start.51 = (s32[16]{0:T(128)}, s32[16]{0:T(128)S(1)}, u32[]{:S(2)}) copy-start(s32[16]{0:T(128)S(1)} %get-tuple-element.2606) | copy-start | bytes 196 | tf_op jit(solution)/shard_map/while
  444.0 33.4 %copy-start.44 = (s32[16]{0:T(128)}, s32[16]{0:T(128)S(1)}, u32[]{:S(2)}) copy-start(s32[16]{0:T(128)S(1)} %get-tuple-element.2602) | copy-start | bytes 196 | tf_op jit(solution)/shard_map/while
  444.0 33.4 %copy-start.46 = (s32[16]{0:T(128)}, s32[16]{0:T(128)S(1)}, u32[]{:S(2)}) copy-start(s32[16]{0:T(128)S(1)} %get-tuple-element.2601) | copy-start | bytes 196 | tf_op jit(solution)/shard_map/while
  444.0 33.4 %copy-start.53 = (s32[16]{0:T(128)}, s32[16]{0:T(128)S(1)}, u32[]{:S(2)}) copy-start(s32[16]{0:T(128)S(1)} %get-tuple-element.2597) | copy-start | bytes 196 | tf_op jit(solution)/shard_map/while
  536.7 30.1 %copy-start.37 = (f32[193,1,1,256]{3,0,2,1:T(8,128)S(1)}, f32[193,1,1,256]{3,0,2,1:T(8,128)}, u32[]{:S(2)}) copy-start(f32[193,1,1,256]{3,0,2,1:T(8,128)} %get-tuple-element.2767) | copy-start | bytes 592900 | tf_op jit(solution)/shard_map/while
  536.7 30.8 %copy-start.34 = (f32[193,1,1,256]{3,0,2,1:T(8,128)S(1)}, f32[193,1,1,256]{3,0,2,1:T(8,128)}, u32[]{:S(2)}) copy-start(f32[193,1,1,256]{3,0,2,1:T(8,128)} %get-tuple-element.2773) | copy-start | bytes 592900 | tf_op jit(solution)/shard_map/while
  574.2 31.3 %copy-start.2 = (bf16[64,8,8,256]{3,2,1,0:T(8,128)(2,1)S(1)}, bf16[64,8,8,256]{3,2,1,0:T(8,128)(2,1)}, u32[]{:S(2)}) copy-start(bf16[64,8,8,256]{3,2,1,0:T(8,128)(2,1)} %copy-done.1) | copy-start | bytes 6291460 | tf_op jit(solution)/shard_map/while
  578.9 22.8 %copy-start.32 = (f32[193,1,1,256]{3,0,2,1:T(8,128)S(1)}, f32[193,1,1,256]{3,0,2,1:T(8,128)}, u32[]{:S(2)}) copy-start(f32[193,1,1,256]{3,0,2,1:T(8,128)} %get-tuple-element.2756) | copy-start | bytes 592900 | tf_op jit(solution)/shard_map/while
  578.9 23.6 %copy-start.45 = (s32[16]{0:T(128)S(1)}, s32[16]{0:T(128)}, u32[]{:S(2)}) copy-start(s32[16]{0:T(128)} %copy-done.44) | copy-start | bytes 196 | tf_op jit(solution)/shard_map/while
  578.9 26.0 %copy-start.52 = (f32[256]{0:T(256)S(1)}, f32[256]{0:T(256)}, u32[]{:S(2)}) copy-start(f32[256]{0:T(256)} %get-tuple-element.2653) | copy-start | bytes 3076 | tf_op jit(solution)/shard_map/while
  578.9 26.0 %copy-start.55 = (f32[256]{0:T(256)S(1)}, f32[256]{0:T(256)}, u32[]{:S(2)}) copy-start(f32[256]{0:T(256)} %get-tuple-element.2776) | copy-start | bytes 3076 | tf_op jit(solution)/shard_map/while
  634.3 26.5 %copy-start.42 = (s32[16]{0:T(128)}, s32[16]{0:T(128)S(1)}, u32[]{:S(2)}) copy-start(s32[16]{0:T(128)S(1)} %get-tuple-element.2585) | copy-start | bytes 196 | tf_op jit(solution)/shard_map/while
  634.3 26.5 %copy-start.43 = (s32[16]{0:T(128)}, s32[16]{0:T(128)S(1)}, u32[]{:S(2)}) copy-start(s32[16]{0:T(128)S(1)} %get-tuple-element.2588) | copy-start | bytes 196 | tf_op jit(solution)/shard_map/while
  647.3 20.8 %copy-start.50 = (s32[16]{0:T(128)}, s32[16]{0:T(128)S(1)}, u32[]{:S(2)}) copy-start(s32[16]{0:T(128)S(1)} %get-tuple-element.2598) | copy-start | bytes 196 | tf_op jit(solution)/shard_map/while
  647.3 33.4 %copy-start.44 = (s32[16]{0:T(128)}, s32[16]{0:T(128)S(1)}, u32[]{:S(2)}) copy-start(s32[16]{0:T(128)S(1)} %get-tuple-element.2602) | copy-start | bytes 196 | tf_op jit(solution)/shard_map/while
  647.3 33.4 %copy-start.46 = (s32[16]{0:T(128)}, s32[16]{0:T(128)S(1)}, u32[]{:S(2)}) copy-start(s32[16]{0:T(128)S(1)} %get-tuple-element.2601) | copy-start | bytes 196 | tf_op jit(solution)/shard_map/while
  647.3 33.4 %copy-start.53 = (s32[16]{0:T(128)}, s32[16]{0:T(128)S(1)}, u32[]{:S(2)}) copy-start(s32[16]{0:T(128)S(1)} %get-tuple-element.2597) | copy-start | bytes 196 | tf_op jit(solution)/shard_map/while
  740.0 30.1 %copy-start.37 = (f32[193,1,1,256]{3,0,2,1:T(8,128)S(1)}, f32[193,1,1,256]{3,0,2,1:T(8,128)}, u32[]{:S(2)}) copy-start(f32[193,1,1,256]{3,0,2,1:T(8,128)} %get-tuple-element.2767) | copy-start | bytes 592900 | tf_op jit(solution)/shard_map/while
  740.0 30.8 %copy-start.34 = (f32[193,1,1,256]{3,0,2,1:T(8,128)S(1)}, f32[193,1,1,256]{3,0,2,1:T(8,128)}, u32[]{:S(2)}) copy-start(f32[193,1,1,256]{3,0,2,1:T(8,128)} %get-tuple-element.2773) | copy-start | bytes 592900 | tf_op jit(solution)/shard_map/while
  777.5 31.3 %copy-start.2 = (bf16[64,8,8,256]{3,2,1,0:T(8,128)(2,1)S(1)}, bf16[64,8,8,256]{3,2,1,0:T(8,128)(2,1)}, u32[]{:S(2)}) copy-start(bf16[64,8,8,256]{3,2,1,0:T(8,128)(2,1)} %copy-done.1) | copy-start | bytes 6291460 | tf_op jit(solution)/shard_map/while
  782.2 22.8 %copy-start.32 = (f32[193,1,1,256]{3,0,2,1:T(8,128)S(1)}, f32[193,1,1,256]{3,0,2,1:T(8,128)}, u32[]{:S(2)}) copy-start(f32[193,1,1,256]{3,0,2,1:T(8,128)} %get-tuple-element.2756) | copy-start | bytes 592900 | tf_op jit(solution)/shard_map/while
  782.2 23.7 %copy-start.45 = (s32[16]{0:T(128)S(1)}, s32[16]{0:T(128)}, u32[]{:S(2)}) copy-start(s32[16]{0:T(128)} %copy-done.44) | copy-start | bytes 196 | tf_op jit(solution)/shard_map/while
  782.2 26.0 %copy-start.52 = (f32[256]{0:T(256)S(1)}, f32[256]{0:T(256)}, u32[]{:S(2)}) copy-start(f32[256]{0:T(256)} %get-tuple-element.2653) | copy-start | bytes 3076 | tf_op jit(solution)/shard_map/while
  782.2 26.0 %copy-start.55 = (f32[256]{0:T(256)S(1)}, f32[256]{0:T(256)}, u32[]{:S(2)}) copy-start(f32[256]{0:T(256)} %get-tuple-element.2776) | copy-start | bytes 3076 | tf_op jit(solution)/shard_map/while
  837.6 26.5 %copy-start.42 = (s32[16]{0:T(128)}, s32[16]{0:T(128)S(1)}, u32[]{:S(2)}) copy-start(s32[16]{0:T(128)S(1)} %get-tuple-element.2585) | copy-start | bytes 196 | tf_op jit(solution)/shard_map/while
  837.6 26.5 %copy-start.43 = (s32[16]{0:T(128)}, s32[16]{0:T(128)S(1)}, u32[]{:S(2)}) copy-start(s32[16]{0:T(128)S(1)} %get-tuple-element.2588) | copy-start | bytes 196 | tf_op jit(solution)/shard_map/while
  850.6 33.4 %copy-start.44 = (s32[16]{0:T(128)}, s32[16]{0:T(128)S(1)}, u32[]{:S(2)}) copy-start(s32[16]{0:T(128)S(1)} %get-tuple-element.2602) | copy-start | bytes 196 | tf_op jit(solution)/shard_map/while
  850.6 33.4 %copy-start.46 = (s32[16]{0:T(128)}, s32[16]{0:T(128)S(1)}, u32[]{:S(2)}) copy-start(s32[16]{0:T(128)S(1)} %get-tuple-element.2601) | copy-start | bytes 196 | tf_op jit(solution)/shard_map/while
  850.6 33.4 %copy-start.53 = (s32[16]{0:T(128)}, s32[16]{0:T(128)S(1)}, u32[]{:S(2)}) copy-start(s32[16]{0:T(128)S(1)} %get-tuple-element.2597) | copy-start | bytes 196 | tf_op jit(solution)/shard_map/while
  943.3 30.0 %copy-start.37 = (f32[193,1,1,256]{3,0,2,1:T(8,128)S(1)}, f32[193,1,1,256]{3,0,2,1:T(8,128)}, u32[]{:S(2)}) copy-start(f32[193,1,1,256]{3,0,2,1:T(8,128)} %get-tuple-element.2767) | copy-start | bytes 592900 | tf_op jit(solution)/shard_map/while
  943.3 30.7 %copy-start.34 = (f32[193,1,1,256]{3,0,2,1:T(8,128)S(1)}, f32[193,1,1,256]{3,0,2,1:T(8,128)}, u32[]{:S(2)}) copy-start(f32[193,1,1,256]{3,0,2,1:T(8,128)} %get-tuple-element.2773) | copy-start | bytes 592900 | tf_op jit(solution)/shard_map/while
  980.6 31.3 %copy-start.2 = (bf16[64,8,8,256]{3,2,1,0:T(8,128)(2,1)S(1)}, bf16[64,8,8,256]{3,2,1,0:T(8,128)(2,1)}, u32[]{:S(2)}) copy-start(bf16[64,8,8,256]{3,2,1,0:T(8,128)(2,1)} %copy-done.1) | copy-start | bytes 6291460 | tf_op jit(solution)/shard_map/while
  985.4 22.8 %copy-start.32 = (f32[193,1,1,256]{3,0,2,1:T(8,128)S(1)}, f32[193,1,1,256]{3,0,2,1:T(8,128)}, u32[]{:S(2)}) copy-start(f32[193,1,1,256]{3,0,2,1:T(8,128)} %get-tuple-element.2756) | copy-start | bytes 592900 | tf_op jit(solution)/shard_map/while
  985.4 23.6 %copy-start.45 = (s32[16]{0:T(128)S(1)}, s32[16]{0:T(128)}, u32[]{:S(2)}) copy-start(s32[16]{0:T(128)} %copy-done.44) | copy-start | bytes 196 | tf_op jit(solution)/shard_map/while
  985.4 26.0 %copy-start.52 = (f32[256]{0:T(256)S(1)}, f32[256]{0:T(256)}, u32[]{:S(2)}) copy-start(f32[256]{0:T(256)} %get-tuple-element.2653) | copy-start | bytes 3076 | tf_op jit(solution)/shard_map/while
  985.4 26.0 %copy-start.55 = (f32[256]{0:T(256)S(1)}, f32[256]{0:T(256)}, u32[]{:S(2)}) copy-start(f32[256]{0:T(256)} %get-tuple-element.2776) | copy-start | bytes 3076 | tf_op jit(solution)/shard_map/while
  1127.8 31.8 %copy-start.17 = (f32[193,8,1,32]{3,1,0,2:T(8,128)S(1)}, f32[193,8,1,32]{3,1,0,2:T(8,128)}, u32[]{:S(2)}) copy-start(f32[193,8,1,32]{3,1,0,2:T(8,128)} %get-tuple-element.1324) | copy-start | bytes 592900
  1173.4 23.8 %copy-start.12 = (f32[193,1,8,256]{3,2,0,1:T(8,128)S(1)}, f32[193,1,8,256]{3,2,0,1:T(8,128)}, u32[]{:S(2)}) copy-start(f32[193,1,8,256]{3,2,0,1:T(8,128)} %get-tuple-element.1331) | copy-start | bytes 4743172
  1230.0 6.5 collective-permute-start.4
  1233.1 5.3 collective-permute-start.5
  1242.4 176.7 %collective-permute-start.7 = (bf16[3,16,8,8,256]{4,3,2,1,0:T(8,128)(2,1)}, bf16[3,16,8,8,256]{4,3,2,1,0:T(8,128)(2,1)}, u32[]{:S(2)}, u32[]{:S(2)}) collective-permute-start(bf16[3,16,8,8,256]{4,3,2,1,0:T(8,128)(2,1)} %get-tuple-element.2066), channel_id=1, source_target_pairs={{4,0},{8,4},{12,8},{16,12},{20,16},{24,20},{28,24},{5,1},{9,5},{13... | collective-permute-start | bytes 4718600 | tf_op jit(solution)/shard_map/ppermute | solution.py:19
  1252.0 170.8 %collective-permute-start.6 = (bf16[3,16,8,8,256]{4,3,2,1,0:T(8,128)(2,1)}, bf16[3,16,8,8,256]{4,3,2,1,0:T(8,128)(2,1)}, u32[]{:S(2)}, u32[]{:S(2)}) collective-permute-start(bf16[3,16,8,8,256]{4,3,2,1,0:T(8,128)(2,1)} %get-tuple-element.2065), channel_id=1, source_target_pairs={{0,4},{4,8},{8,12},{12,16},{16,20},{20,24},{24,28},{1,5},{5,9},{9,... | collective-permute-start | bytes 4718600 | tf_op jit(solution)/shard_map/ppermute | solution.py:19
  (97 other events, 757.9 us)
Sparse Core Ops, SparseCore 0:
  1268.3 145.3 all-reduce.11
where the time goes:
time: 1490 us; the launch traced here: 1470 us
  local copies, waits for them, and re-layouts  709 us (48%)
  other arithmetic  403 us (27%)
  matrix products  105 us (7%)
  waiting for transfers between devices  101 us (7%)
  blocking collectives  82.8 us (6%)
  loops' own time  30.7 us (2%)
  starting transfers between devices  24.2 us (2%)
  between operations  15.4 us (1%)
    scatter-add x104, other arithmetic, step_block(): face_sums[side_index].at[near_rows[:, side_index]]  220 us
    gather x104, local copies, waits for them, and re-layouts, step_block(): face_tables[side_index][near_rows[:, side_index]]  149 us
    scatter-add x18, local copies, waits for them, and re-layouts, local(): table_grad = table_grad.at[:, x_start:x_stop, y_start:y_stop, z_start * c...  134 us
    another operation x12, local copies, waits for them, and re-layouts, columns_faces(): stacked = jnp.stack(shifted, axis=3)  122 us
    psum x1, blocking collectives, local(): lax.psum((weight_local, bias_local), ('space', 'tile'))  82.8 us
    psum x1, waiting for transfers between devices, local(): lax.psum((weight_local, bias_local), ('space', 'tile'))  62.2 us
    reshape x4, local copies, waits for them, and re-layouts, columns_faces(): return stacked.reshape(own_bricks.shape[0] * 64, 90 * channels)  61.4 us
    split x28, local copies, waits for them, and re-layouts, assemble_faces(): rows_y.append(jnp.concatenate(pieces, axis=3))  43 us
  transfers between devices with their start and end apart: 9, of which 5 were waited for; matrix products, arithmetic and copies ran while one was open for 4% of the time, Pallas kernels for 0%

commit v1 on v0

v1 whole, which is shorter than its diff:
```python
import jax
import jax.numpy as jnp
from jax import lax
from jax.experimental import pallas as pl
from jax.experimental.pallas import tpu as pltpu
from jax.sharding import PartitionSpec as P

F32 = jnp.float32
BF16 = jnp.bfloat16
DEVICE_SIDES = [(s, t) for s in (-1, 0, 1) for t in (-1, 0, 1) if (s, t) != (0, 0)]
SHELL = (
    [(0, y) for y in range(8)]
    + [(7, y) for y in range(8)]
    + [(x, 0) for x in range(1, 7)]
    + [(x, 7) for x in range(1, 7)]
)
ROWS = len(SHELL) + 9
VMEM = pl.BlockSpec(memory_space=pltpu.VMEM)
SMEM = pl.BlockSpec(memory_space=pltpu.SMEM)
PARAMS = pltpu.CompilerParams(vmem_limit_bytes=56 * 1024 * 1024)


def dot(a, b):
    return jnp.dot(a, b, preferred_element_type=F32)


def dot_nt(a, b):
    return lax.dot_general(a, b, (((1,), (1,)), ((), ())), preferred_element_type=F32)


def dot_tn(a, b):
    return lax.dot_general(a, b, (((0,), (0,)), ((), ())), preferred_element_type=F32)


def roll(v, by):
    by = by % 128
    return v if by == 0 else pltpu.roll(v, by, axis=1)


def lanes(n, width=128):
    return lax.broadcasted_iota(jnp.int32, (n, width), 1)


def one_hot(test):
    return jnp.where(test, 1.0, 0.0).astype(BF16)


def halves(h):
    return slice(128 * h, 128 * h + 128)


def pack_z(load, top, n, ys=range(8)):
    sub = lanes(n) // 32
    out = []
    for h in (0, 1):
        acc = None
        for k in range(4):
            y = 4 * h + k
            if y not in ys:
                continue
            v = load(y, halves(1 if top else 0)).astype(F32)
            v = roll(v, 32 * k - (96 if top else 0))
            acc = v if acc is None else jnp.where(sub == k, v, acc)
        out.append(acc)
    return out


def unpack_z(low, high, y, n):
    k = y % 4
    lane = lanes(n)
    zero = jnp.zeros((n, 128), F32)
    first = jnp.where(lane < 32, roll(low(halves(y // 4)), -32 * k), zero)
    second = jnp.where(lane >= 96, roll(high(halves(y // 4)), 96 - 32 * k), zero)
    return first, second


def squeeze(piece, g, k, h, n):
    lane = lanes(n)
    last = piece(4 * g + 3, h)
    if h == 0:
        return jnp.where(lane < 32, roll(last, -32 * (k + 1)), piece(4 * g + k, h))
    return jnp.where(lane >= 96, roll(last, 96 - 32 * k), piece(4 * g + k, h))


def unsqueeze(row, p, h, n):
    g, k = p // 4, p % 4
    if k < 3:
        return row(3 * g + k, h)
    sub = lanes(n) // 32
    acc = None
    for j in range(3):
        v = roll(row(3 * g + j, h), 32 * (j + 1) if h == 0 else 32 * j - 96)
        acc = v if acc is None else jnp.where(sub == (j + 1 if h == 0 else j), v, acc)
    return acc


def pack_kernel(count_ref, f_ref, slots_ref, fm_ref, *refs):
    outs, zp = refs[:8], refs[8]
    count = count_ref[0, 0]
    live = (lax.broadcasted_iota(jnp.int32, (64, 256), 0) < count).astype(F32)

    def mask_rows(r, _):
        fm_ref[r] = (f_ref[r].astype(F32) * live).astype(BF16)
        return _

    lax.fori_loop(0, 64, mask_rows, 0)
    chosen = one_hot(slots_ref[...] == lax.broadcasted_iota(jnp.int32, (128, 64), 1))

    def send(row, value):
        value = value.astype(BF16)
        for d in range(8):
            outs[d][row] = value[16 * d : 16 * d + 16]

    for row, (x, y) in enumerate(SHELL):
        send(row, dot(chosen, fm_ref[8 * x + y]))
    for x in range(1, 7):
        for s in (0, 1):
            h0, h1 = pack_z(lambda y, h: fm_ref[8 * x + y, :, h], s == 0, 64, range(1, 7))
            z = jnp.concatenate([h0, h1], axis=1).astype(BF16)
            zp[2 * (x - 1) + s] = dot(chosen, z)
    for g in range(3):
        for k in range(3):
            parts = [
                squeeze(lambda p, hh: zp[p, :, halves(hh)], g, k, h, 128) for h in (0, 1)
            ]
            send(28 + 3 * g + k, jnp.concatenate(parts, axis=1))


def pack(count, f_rows, slots_col):
    return pl.pallas_call(
        pack_kernel,
        out_shape=[jax.ShapeDtypeStruct((64, 64, 256), BF16)]
        + [jax.ShapeDtypeStruct((ROWS, 16, 256), BF16)] * 8,
        in_specs=[SMEM, VMEM, VMEM],
        out_specs=[VMEM] * 9,
        scratch_shapes=[pltpu.VMEM((12, 128, 256), F32)],
        compiler_params=PARAMS,
        name="pack",
    )(count, f_rows, slots_col)


def build_bands(wt_ref, bm_ref, bym_ref, bye_ref):
    blk = lanes(32, 256) // 32
    zero = jnp.zeros((32, 256), F32)

    def banded(w0, w1, w2, i):
        row = jnp.where(blk == i - 1, w2, zero)
        row = jnp.where(blk == i, w1, row)
        return jnp.where(blk == i + 1, w0, row).astype(BF16)

    def one(aq, _):
        w0, w1, w2 = (wt_ref[3 * aq + r].astype(F32) for r in range(3))
        for i in range(8):
            bm_ref[aq, 32 * i : 32 * i + 32, :] = banded(w0, w1, w2, i)
        return _

    lax.fori_loop(0, 9, one, 0)

    def side(a, _):
        for s in (0, 1):
            w0, w1, w2 = (wt_ref[9 * a + 3 * q + 2 * s].astype(F32) for q in range(3))
            k = 2 * a + s
            for i in range(8):
                bym_ref[k, 32 * i : 32 * i + 32, :] = banded(w0, w1, w2, i)
            bye_ref[k] = jnp.zeros((256, 256), BF16)
            bye_ref[k, 0:32, :] = jnp.where(blk == 7, w2, zero).astype(BF16)
            bye_ref[k, 224:256, :] = jnp.where(blk == 0, w0, zero).astype(BF16)
        return _

    lax.fori_loop(0, 3, side, 0)


def high_low(v):
    high = v.astype(BF16)
    return high, (v - high.astype(F32)).astype(BF16)


def dgrad_kernel(
    count_ref, g_ref, wt_ref, rows3_ref, rows2_ref,
    own_ref, gm_ref, gz_ref, bm_ref, bym_ref, bye_ref, *refs
):
    outs = refs[:8]
    gpad, gzpad, pg, ag, agx, xf, yf, tz, oht3, oht2 = refs[8:]
    count = count_ref[0, 0]
    build_bands(wt_ref, bm_ref, bym_ref, bye_ref)
    live = (lax.broadcasted_iota(jnp.int32, (64, 256), 0) < count).astype(F32)
    for i in (0, 1, 10, 11):
        gpad[i] = jnp.zeros((8, 64, 256), BF16)
        gzpad[0, i] = jnp.zeros((64, 256), BF16)
        gzpad[1, i] = jnp.zeros((64, 256), BF16)
    pg[:, 0] = jnp.zeros((10, 64, 256), F32)
    pg[:, 9] = jnp.zeros((10, 64, 256), F32)

    def load_g(x, _):
        for y in range(8):
            v = (g_ref[8 * x + y].astype(F32) * live).astype(BF16)
            gpad[x + 2, y] = v
            gm_ref[8 * x + y] = v
        for s in (0, 1):
            parts = pack_z(lambda y, h: gpad[x + 2, y, :, h], s == 1, 64)
            z = jnp.concatenate(parts, axis=1).astype(BF16)
            gzpad[s, x + 2] = z
            gz_ref[s, x] = z
        return _

    lax.fori_loop(0, 8, load_g, 0)
    tsub = lax.broadcasted_iota(jnp.int32, (192, 192), 0)
    tsub2 = lax.broadcasted_iota(jnp.int32, (192, 128), 0)
    for k in range(9):
        oht3[k] = one_hot(rows3_ref[k : k + 1, :] == tsub)
        oht2[k] = one_hot(rows2_ref[k : k + 1, :] == tsub2)

    def plane(u, _):
        for q in (1, 0, 2):
            acc = None
            for a in range(3):
                part = dot_nt(gpad[u + 2 - a].reshape(512, 256), bm_ref[3 * a + q])
                acc = part if acc is None else acc + part
            acc = acc.reshape(8, 64, 256)
            if q == 1:
                pg[u, 1:9] = acc
            elif q == 0:
                pg[u, 0:8] = pg[u, 0:8] + acc
            else:
                pg[u, 2:10] = pg[u, 2:10] + acc
        return _

    lax.fori_loop(0, 10, plane, 0)
    for s in (0, 1):
        main, extra = None, None
        for a in range(3):
            z = gzpad[s, 2 - a : 12 - a].reshape(640, 256)
            pm = dot_nt(z, bym_ref[2 * a + s])
            pe = dot_nt(z, bye_ref[2 * a + s])
            main = pm if main is None else main + pm
            extra = pe if extra is None else extra + pe
        ag[s] = main.reshape(10, 64, 256)
        agx[s] = extra.reshape(10, 64, 256)

    def spread(k, v):
        high, low = high_low(v)
        return dot(oht2[k], jnp.concatenate([high, low], axis=0))

    lane = lanes(64, 256)

    def spread_z(k, s, u):
        m, e = ag[s, u], agx[s, u]
        zero = jnp.zeros_like(e)
        v = jnp.concatenate(
            [jnp.where(lane >= 224, e, zero), m, jnp.where(lane < 32, e, zero)], axis=0
        )
        high, low = high_low(v)
        return dot(oht3[k], high) + dot(oht3[k], low)

    def inner(x, _):
        yf[0, x] = spread(3, pg[x + 1, 0])
        yf[1, x] = spread(5, pg[x + 1, 9])
        for s in (0, 1):
            tz[s, x] = spread_z(3 + 2 * s, s, x + 1)
        return _

    lax.fori_loop(0, 8, inner, 0)
    for i, (u, x, ex) in enumerate(((0, 7, 0), (9, 0, 2))):
        def along(y, _, i=i, u=u, ex=ex):
            xf[i, y] = spread(3 * ex + 1, pg[u, y + 1])
            return _

        lax.fori_loop(0, 8, along, 0)
        yf[0, x] = yf[0, x] + spread(3 * ex, pg[u, 0])
        yf[1, x] = yf[1, x] + spread(3 * ex + 2, pg[u, 9])
        for s in (0, 1):
            tz[s, x] = tz[s, x] + spread_z(3 * ex + 2 * s, s, u)

    def own(x, _):
        for y in range(8):
            first, second = unpack_z(
                lambda h: tz[1, x, 0:64, h], lambda h: tz[0, x, 0:64, h], y, 64
            )
            extra = jnp.concatenate([first, second], axis=1)
            v = pg[x + 1, y + 1] + extra
            if y == 7:
                v = v + yf[0, x, 0:64, :]
            if y == 0:
                v = v + yf[1, x, 0:64, :]
            own_ref[8 * x + y] = v
        return _

    lax.fori_loop(0, 8, own, 0)
    for i, x in enumerate((7, 0)):
        for y in range(8):
            own_ref[8 * x + y] = own_ref[8 * x + y] + xf[i, y, 0:64, :]

    def give(row, value):
        value = value.astype(BF16)
        for d in range(8):
            outs[d][row] = value[16 * d : 16 * d + 16]

    far = slice(64, 192)
    for row, (x, y) in enumerate(SHELL):
        first, second = unpack_z(lambda h: tz[1, x, far, h], lambda h: tz[0, x, far, h], y, 128)
        v = jnp.concatenate([first, second], axis=1)
        if x in (0, 7):
            v = v + xf[0 if x == 7 else 1, y, far, :]
        if y in (0, 7):
            v = v + yf[0 if y == 7 else 1, x, far, :]
        give(row, v)
    for g in range(3):
        for k in range(3):
            parts = [
                squeeze(lambda p, hh: tz[p % 2, 1 + p // 2, far, halves(hh)], g, k, h, 128)
                for h in (0, 1)
            ]
            give(28 + 3 * g + k, jnp.concatenate(parts, axis=1))


def dgrad(count, g_rows, wt, rows3, rows2):
    sd = jax.ShapeDtypeStruct
    return pl.pallas_call(
        dgrad_kernel,
        out_shape=[
            sd((64, 64, 256), F32),
            sd((64, 64, 256), BF16),
            sd((2, 8, 64, 256), BF16),
            sd((9, 256, 256), BF16),
            sd((6, 256, 256), BF16),
            sd((6, 256, 256), BF16),
        ]
        + [sd((ROWS, 16, 256), BF16)] * 8,
        in_specs=[SMEM] + [VMEM] * 4,
        out_specs=[VMEM] * 14,
        scratch_shapes=[
            pltpu.VMEM((12, 8, 64, 256), BF16),
            pltpu.VMEM((2, 12, 64, 256), BF16),
            pltpu.VMEM((10, 10, 64, 256), F32),
            pltpu.VMEM((2, 10, 64, 256), F32),
            pltpu.VMEM((2, 10, 64, 256), F32),
            pltpu.VMEM((2, 8, 192, 256), F32),
            pltpu.VMEM((2, 8, 192, 256), F32),
            pltpu.VMEM((2, 8, 192, 256), F32),
            pltpu.VMEM((9, 192, 192), BF16),
            pltpu.VMEM((9, 192, 128), BF16),
        ],
        compiler_params=PARAMS,
        name="dgrad",
    )(count, g_rows, wt, rows3, rows2)


def wgrad_kernel(fm_ref, gm_ref, gz_ref, cols_ref, *refs):
    ins = refs[:8]
    vm_ref, a_ref, ax_ref, dw_ref = refs[8:12]
    xt, yt, tz, oh3, acc, fold = refs[12:]
    far = slice(64, 192)
    tl = lanes(192, 192)
    for k in range(9):
        oh3[k] = one_hot(cols_ref[:, k : k + 1] == tl)
    for row, (x, y) in enumerate(SHELL):
        places = []
        if x in (0, 7):
            places.append((xt, 0 if x == 7 else 1, y))
        if y in (0, 7):
            places.append((yt, 0 if y == 7 else 1, x))
        for ref, i, j in places:
            ref[i, j, 0:64, :] = fm_ref[8 * x + y]
            for d in range(8):
                ref[i, j, 64 + 16 * d : 80 + 16 * d, :] = ins[d][row]

    def own_z(x, _):
        for s in (0, 1):
            parts = pack_z(lambda y, h: fm_ref[8 * x + y, :, h], s == 0, 64)
            tz[s, x, 0:64, :] = jnp.concatenate(parts, axis=1).astype(BF16)
        return _

    lax.fori_loop(0, 8, own_z, 0)
    for i, x in enumerate((7, 0)):
        for s in (0, 1):
            parts = pack_z(lambda y, h: xt[i, y, far, h], s == 0, 128)
            tz[s, x, far, :] = jnp.concatenate(parts, axis=1).astype(BF16)

    def compact(row, h):
        return jnp.concatenate([ins[d][28 + row, :, halves(h)] for d in range(8)], axis=0).astype(F32)

    sub = lanes(128) // 32
    for x in range(1, 7):
        for s in (0, 1):
            top = s == 0
            src = halves(1 if top else 0)
            first = unsqueeze(compact, 2 * (x - 1) + s, 0, 128)
            second = unsqueeze(compact, 2 * (x - 1) + s, 1, 128)
            y0 = roll(yt[1, x, far, src].astype(F32), -96 if top else 0)
            y7 = roll(yt[0, x, far, src].astype(F32), 96 - (96 if top else 0))
            first = jnp.where(sub == 0, y0, first)
            second = jnp.where(sub == 3, y7, second)
            tz[s, x, far, :] = jnp.concatenate([first, second], axis=1).astype(BF16)

    lane = lanes(64, 256)

    def halo_z(k, s, x, u):
        v = dot(oh3[k], tz[s, x])
        zero = jnp.zeros((64, 256), F32)
        a_ref[s, u] = v[64:128].astype(BF16)
        ax_ref[s, u] = jnp.where(
            lane >= 224, v[0:64], jnp.where(lane < 32, v[128:192], zero)
        ).astype(BF16)

    def fill(x, _):
        for y in range(8):
            vm_ref[x + 1, y + 1] = fm_ref[8 * x + y]
        vm_ref[x + 1, 0] = dot(oh3[4, 0:64, :], yt[0, x]).astype(BF16)
        vm_ref[x + 1, 9] = dot(oh3[4, 128:192, :], yt[1, x]).astype(BF16)
        for s in (0, 1):
            halo_z(3 + 2 * s, s, x, x + 1)
        return _

    lax.fori_loop(0, 8, fill, 0)
    for i, (u, x, ex) in enumerate(((0, 7, 0), (9, 0, 2))):
        def along(y, _, i=i, u=u, ex=ex):
            vm_ref[u, y + 1] = dot(oh3[3 * ex + 1, 64:128, :], xt[i, y]).astype(BF16)
            return _

        lax.fori_loop(0, 8, along, 0)
        vm_ref[u, 0] = dot(oh3[3 * ex + 1, 0:64, :], xt[i, 7]).astype(BF16)
        vm_ref[u, 9] = dot(oh3[3 * ex + 1, 128:192, :], xt[i, 0]).astype(BF16)
        for s in (0, 1):
            halo_z(3 * ex + 2 * s, s, x, u)

    def column(x, a, q):
        return vm_ref[x + a, q : q + 8].reshape(512, 256)

    def sums(x, bias):
        g = gm_ref[pl.ds(8 * x, 8)].reshape(512, 256)
        cols = jnp.concatenate([column(x, a, q) for a in range(3) for q in range(3)], axis=1)
        part = dot_tn(g, cols)

        @pl.when(x == 0)
        def _():
            acc[:, 0:2304] = part

        @pl.when(x != 0)
        def _():
            acc[:, 0:2304] = acc[:, 0:2304] + part

        return bias + jnp.sum(g.astype(F32).reshape(64, 8, 256), axis=0)

    bias = lax.fori_loop(0, 8, sums, jnp.zeros((8, 256), F32))
    for s in (0, 1):
        z = gz_ref[s].reshape(512, 256)
        cols = jnp.concatenate(
            [r[s, a : a + 8].reshape(512, 256) for a in range(3) for r in (a_ref, ax_ref)], axis=1
        )
        acc[:, 2304 + 1536 * s : 3840 + 1536 * s] = dot_tn(z, cols)

    blk = lanes(32, 256) // 32

    def band_sum(start, r):
        total = None
        for i in range(8):
            if not 0 <= i + r - 1 < 8:
                continue
            v = acc[32 * i : 32 * i + 32, start : start + 256]
            v = jnp.where(blk == i + r - 1, v, jnp.zeros_like(v))
            total = v if total is None else total + v
        return total

    def fold_lanes(total):
        v = total[:, 0:128] + total[:, 128:256]
        v = v + pltpu.roll(v, 64, axis=1)
        return v + pltpu.roll(v, 32, axis=1)

    for a in range(3):
        for q in range(3):
            for r in range(3):
                total = band_sum(256 * (3 * a + q), r)
                if r != 1:
                    s = r // 2
                    base = 2304 + 1536 * s + 512 * a
                    total = total + band_sum(base, q)
                    if q == 0:
                        v = acc[0:32, base + 256 : base + 512]
                        total = total + jnp.where(blk == 7, v, jnp.zeros_like(v))
                    if q == 2:
                        v = acc[224:256, base + 256 : base + 512]
                        total = total + jnp.where(blk == 0, v, jnp.zeros_like(v))
                t = 9 * a + 3 * q + r
                fold[32 * t : 32 * t + 32, :] = fold_lanes(total)
    quarter = lanes(216) // 32
    v = fold[0:216, :]
    for k in range(1, 4):
        v = jnp.where(quarter == k, fold[216 * k : 216 * k + 216, :], v)
    dw_ref[0:216, :] = v
    dw_ref[216:224, :] = fold_lanes(bias)


def wgrad(fm, gm, gz, cols3, arrived):
    sd = jax.ShapeDtypeStruct
    return pl.pallas_call(
        wgrad_kernel,
        out_shape=[
            sd((10, 10, 64, 256), BF16),
            sd((2, 10, 64, 256), BF16),
            sd((2, 10, 64, 256), BF16),
            sd((224, 128), F32),
        ],
        in_specs=[VMEM] * 12,
        out_specs=[VMEM] * 4,
        scratch_shapes=[
            pltpu.VMEM((2, 8, 192, 256), BF16),
            pltpu.VMEM((2, 8, 192, 256), BF16),
            pltpu.VMEM((2, 8, 192, 256), BF16),
            pltpu.VMEM((9, 192, 192), BF16),
            pltpu.VMEM((256, 5376), F32),
            pltpu.VMEM((864, 128), F32),
        ],
        compiler_params=PARAMS,
        name="wgrad",
    )(fm, gm, gz, cols3, *arrived)


def forward_kernel(count_ref, vm_ref, a_ref, ax_ref, bm_ref, bym_ref, bye_ref, bias_ref, out_ref, es):
    count = count_ref[0, 0]
    live = (lax.broadcasted_iota(jnp.int32, (64, 256), 0) < count).astype(F32)
    for s in (0, 1):
        total = None
        for a in range(3):
            for ref, band in ((a_ref, bym_ref), (ax_ref, bye_ref)):
                part = dot(ref[s, a : a + 8].reshape(512, 256), band[2 * a + s])
                total = part if total is None else total + part
        es[s] = total.reshape(8, 64, 256)
    bias = bias_ref[...]

    def plane(x, _):
        cols = jnp.concatenate(
            [vm_ref[x + a, q : q + 8].reshape(512, 256) for a in range(3) for q in range(3)], axis=1
        )
        total = dot(cols, bm_ref[...].reshape(2304, 256)).reshape(8, 64, 256)
        for y in range(8):
            first, second = unpack_z(lambda h: es[0, x, :, h], lambda h: es[1, x, :, h], y, 64)
            v = total[y] + jnp.concatenate([first, second], axis=1) + bias
            out_ref[8 * x + y] = (v * live).astype(BF16)
        return _

    lax.fori_loop(0, 8, plane, 0)


def forward(count, vm, a, ax, bm, bym, bye, bias_row):
    return pl.pallas_call(
        forward_kernel,
        out_shape=jax.ShapeDtypeStruct((64, 64, 256), BF16),
        in_specs=[SMEM] + [VMEM] * 7,
        out_specs=VMEM,
        scratch_shapes=[pltpu.VMEM((2, 8, 64, 256), F32)],
        compiler_params=PARAMS,
        name="forward",
    )(count, vm, a, ax, bm, bym, bye, bias_row)


def finish_kernel(count_ref, own_ref, slots_ref, *refs):
    ins, out_ref, zp = refs[:8], refs[8], refs[9]
    count = count_ref[0, 0]
    live = (lax.broadcasted_iota(jnp.int32, (64, 256), 0) < count).astype(F32)
    chosen = one_hot(slots_ref[...] == lax.broadcasted_iota(jnp.int32, (64, 128), 0))

    def back(row):
        return dot(chosen, jnp.concatenate([r[row] for r in ins], axis=0))

    for row, (x, y) in enumerate(SHELL):
        v = own_ref[8 * x + y] + back(row)
        out_ref[8 * x + y] = (v * live).astype(BF16)
    for k in range(9):
        zp[k] = back(28 + k)

    def piece(x, s, h):
        return unsqueeze(lambda row, hh: zp[row, :, halves(hh)], 2 * (x - 1) + s, h, 64)

    for x in range(1, 7):
        parts = {(s, h): piece(x, s, h) for s in (0, 1) for h in (0, 1)}
        for y in range(1, 7):
            first, second = unpack_z(
                lambda h: parts[1, h.start // 128], lambda h: parts[0, h.start // 128], y, 64
            )
            v = own_ref[8 * x + y] + jnp.concatenate([first, second], axis=1)
            out_ref[8 * x + y] = (v * live).astype(BF16)


def finish(count, own, slots_row, returned):
    return pl.pallas_call(
        finish_kernel,
        out_shape=jax.ShapeDtypeStruct((64, 64, 256), BF16),
        in_specs=[SMEM] + [VMEM] * 10,
        out_specs=VMEM,
        scratch_shapes=[pltpu.VMEM((9, 64, 256), F32)],
        compiler_params=PARAMS,
        name="finish",
    )(count, own, slots_row, *returned)


def side_pairs(ds, dt):
    spaces, tiles = lax.axis_size("space"), lax.axis_size("tile")
    return [
        (s * tiles + t, (s + ds) * tiles + t + dt)
        for s in range(spaces)
        for t in range(tiles)
        if 0 <= s + ds < spaces and 0 <= t + dt < tiles
    ]


def send_out(blocks):
    return [
        lax.ppermute(b, ("space", "tile"), side_pairs(ds, dt))
        for b, (ds, dt) in zip(blocks, DEVICE_SIDES)
    ]


def send_back(blocks):
    return [
        lax.ppermute(b, ("space", "tile"), side_pairs(-ds, -dt))
        for b, (ds, dt) in zip(blocks, DEVICE_SIDES)
    ]


def sum_all(value):
    for axis in ("tile", "space"):
        n = lax.axis_size(axis)
        if n & (n - 1):
            value = lax.psum(value, axis)
            continue
        by = 1
        while by < n:
            value = value + lax.ppermute(value, axis, [(i, i ^ by) for i in range(n)])
            by *= 2
    return value


def to_rows(v):
    return jnp.transpose(v[0, 0].reshape(64, 64, 256), (1, 0, 2))


def from_rows(v):
    return jnp.transpose(v, (1, 0, 2)).reshape(1, 1, 64, 8, 8, 256)


def local(features, weight, bias_vector, cotangent, counts, send_slots, neighbours):
    slots = send_slots[0, 0].reshape(1, 128)
    near = neighbours[0, 0]
    full = jnp.concatenate(
        [near[:, :13], jnp.full((64, 1), 192, jnp.int32), near[:, 13:]], axis=1
    ).reshape(64, 3, 3, 3)
    cols3 = jnp.transpose(full, (2, 0, 1, 3)).reshape(192, 9)
    rows3 = cols3.T
    rows2 = full[:, :, :, 1].reshape(64, 9).T
    rows2 = jnp.concatenate([rows2, rows2], axis=1)
    wt = jnp.tile(weight.reshape(27, 32, 32), (1, 1, 8))
    bias_row = jnp.tile(bias_vector, 8).reshape(1, 256)

    fm, *outgoing = pack(counts, to_rows(features), slots.reshape(128, 1))
    arrived = send_out(outgoing)
    own, gm, gz, bm, bym, bye, *back = dgrad(counts, to_rows(cotangent), wt, rows3, rows2)
    returned = send_back(back)
    vm, a, ax, dw = wgrad(fm, gm, gz, cols3, arrived)
    out = forward(counts, vm, a, ax, bm, bym, bye, bias_row)
    total = sum_all(dw)
    grad_in = finish(counts, own, slots, returned)

    scale = float(lax.axis_size("space") * lax.axis_size("tile") * 64 * 512) ** (-0.5)
    total = total * scale
    weight_grad = jnp.transpose(total[:216].reshape(216, 4, 32), (1, 0, 2)).reshape(27, 32, 32)
    weight_grad = jnp.transpose(weight_grad, (0, 2, 1)).reshape(3, 3, 3, 32, 32)
    bias_grad = jnp.sum(total[216:224, :32], axis=0)
    return from_rows(out), from_rows(grad_in), weight_grad, bias_grad


def solution(mesh):
    wide = P("space", "tile", None, None, None, None)
    return jax.shard_map(
        local,
        mesh=mesh,
        in_specs=(wide, P(), P(), wide, P("space", "tile"), P("space", "tile", None, None), P("space", "tile", None, None)),
        out_specs=(wide, wide, P(), P()),
        check_vma=False,
    )
```

time: 1490 us -> 183 us (0.12); the launches traced: 1470 us -> 183 us
  local copies, waits for them, and re-layouts: 709 us -> 24.7 us
  other arithmetic: 403 us -> 2.25 us
  matrix products: 105 us -> 0 us
  blocking collectives: 82.8 us -> 0 us
  waiting for transfers between devices: 101 us -> 27.7 us
  Pallas kernels: 0 us -> 67.2 us
  starting transfers between devices: 24.2 us -> 59.1 us
  loops' own time: 30.7 us -> 0 us
    scatter-add x112 -> x0, other arithmetic: 242 us -> none  [the longest x104 220 us: step_block(): face_sums[side_index].at[near_rows[:, side_index]]]
    another operation x62 -> x7, local copies, waits for them, and re-layouts: 169 us -> 4.28 us  [the longest x2 2.31 us: local(): wt = jnp.tile(weight.reshape(27, 32, 32), (1, 1, 8))]
    gather x105 -> x0, local copies, waits for them, and re-layouts: 152 us -> none  [the longest x104 149 us: step_block(): face_tables[side_index][near_rows[:, side_index]]]
    scatter-add x18 -> x0, local copies, waits for them, and re-layouts: 134 us -> none  [local(): table_grad = table_grad.at[:, x_start:x_stop, y_start:y_stop, z_start * c...]
    dot_general x15 -> x0, matrix products: 105 us -> none  [the longest x4 30.3 us: step_block(): lax.dot_general(g_rows, band_matrix, (((1,), (1,)), ((), ())), preferred_...]
    psum x1 -> x0, blocking collectives: 82.8 us -> none  [local(): lax.psum((weight_local, bias_local), ('space', 'tile'))]
    reshape x7 -> x5, local copies, waits for them, and re-layouts: 79 us -> 1.25 us  [the longest x2 0.81 us: local(): cols3 = jnp.transpose(full, (2, 0, 1, 3)).reshape(192, 9)]
    pallas_call x0 -> x5, Pallas kernels: none -> 67.2 us  [the longest x1 24.5 us: dgrad(): pl.pallas_call(dgrad_kernel, out_shape=[sd((64, 64, 256), F32), sd((64, 6...]
  transfers between devices with their start and end apart: 9 -> 21, of which waited for: 5 -> 8; matrix products, arithmetic and copies ran while one was open for 4% -> 10% of each run, Pallas kernels for 0% -> 23%
where the time goes in v1:
time: 183 us
  Pallas kernels  67.2 us (37%)
  starting transfers between devices  59.1 us (32%)
  waiting for transfers between devices  27.7 us (15%)
  local copies, waits for them, and re-layouts  24.7 us (13%)
  other arithmetic  2.25 us (1%)
    ppermute x8, starting transfers between devices, send_out(): lax.ppermute(b, ('space', 'tile'), side_pairs(ds, dt))  30.2 us
    pallas_call x1, Pallas kernels, dgrad(): pl.pallas_call(dgrad_kernel, out_shape=[sd((64, 64, 256), F32), sd((64, 6...  24.5 us
    pallas_call x1, Pallas kernels, wgrad(): pl.pallas_call(wgrad_kernel, out_shape=[sd((10, 10, 64, 256), BF16), sd((...  21.1 us
    ppermute x8, starting transfers between devices, send_back(): lax.ppermute(b, ('space', 'tile'), side_pairs(-ds, -dt))  20.4 us
    unnamed x50, local copies, waits for them, and re-layouts  17.8 us
    ppermute x8, waiting for transfers between devices, send_back(): lax.ppermute(b, ('space', 'tile'), side_pairs(-ds, -dt))  15.5 us
    pallas_call x1, Pallas kernels, forward(): pl.pallas_call(forward_kernel, out_shape=jax.ShapeDtypeStruct((64, 64, 25...  11.7 us
    ppermute x5, starting transfers between devices, sum_all(): value = value + lax.ppermute(value, axis, [(i, i ^ by) for i in range(n)])  8.52 us
  transfers between devices with their start and end apart: 21, of which 8 were waited for; matrix products, arithmetic and copies ran while one was open for 10% of the time, Pallas kernels for 23%

profile of v1, /device:TPU:0, one launch (start us, length us, event | category | flops | bytes accessed | tf_op | source)
XLA Modules:
  0.0 182.6 jit_solution(8752037440874918167)
XLA Ops:
  1.3 4.1 %copy.30 = bf16[1,1,64,8,8,256]{5,2,4,3,1,0:T(8,128)(2,1)} copy(bf16[1,1,64,8,8,256]{5,4,3,2,1,0:T(8,128)(2,1)} %param.7) | data formatting | bytes 4194304 | tf_op args[0]
  5.4 0.7 reshape_reshape_squeeze.4.slots_ref
  6.1 4.6 %pack.1 = (bf16[64,64,256]{2,1,0:T(8,128)(2,1)}, bf16[37,16,256]{2,1,0:T(8,128)(2,1)}, bf16[37,16,256]{2,1,0:T(8,128)(2,1)}, bf16[37,16,256]{2,1,0:T(8,128)(2,1)...) custom-call(s32[1,1]{1,0:T(1,128)S(6)} %copy.47.count_ref, ...), custom_call_target="tpu_custom_call" | custom-call | tf_op jit(solution)/shard_map/pack/pallas_call | solution.py:130
  10.7 1.3 collective-permute-start
  11.9 1.3 collective-permute-start.1
  13.2 0.7 collective-permute-start.2
  13.9 1.3 collective-permute-start.3
  15.2 3.6 %collective-permute-start.4 = (bf16[37,16,256]{2,1,0:T(8,128)(2,1)}, bf16[37,16,256]{2,1,0:T(8,128)(2,1)S(1)}, u32[]{:S(2)}, u32[]{:S(2)}) collective-permute-start(bf16[37,16,256]{2,1,0:T(8,128)(2,1)} %get-tuple-element.38), channel_id=1, source_target_pairs={{0,1},{1,2},{2,3},{4,5},{5,6},{6,7},{8,9},{9,10},{10,11},{12,13},{... | collective-permute-start | bytes 909320 | tf_op jit(solution)/shard_map/ppermute | solution.py:608
  18.9 0.1 pad.3.clone
  19.0 5.2 %collective-permute-done.refs_0_ = bf16[37,16,256]{2,1,0:T(8,128)(2,1)S(1)} collective-permute-done((bf16[37,16,256]{2,1,0:T(8,128)(2,1)}, bf16[37,16,256]{2,1,0:T(8,128)(2,1)S(1)}, u32[]{:S(2)}, u32[]{:S(2)}) %collective-permute-start) | collective-permute-done | bytes 303136 | tf_op jit(solution)/shard_map/ppermute | solution.py:608
  24.2 1.4 collective-permute-start.5
  25.6 2.5 %collective-permute-done.1.refs_1_ = bf16[37,16,256]{2,1,0:T(8,128)(2,1)S(1)} collective-permute-done((bf16[37,16,256]{2,1,0:T(8,128)(2,1)}, bf16[37,16,256]{2,1,0:T(8,128)(2,1)S(1)}, u32[]{:S(2)}, u32[]{:S(2)}) %collective-permute-start.1) | collective-permute-done | bytes 303136 | tf_op jit(solution)/shard_map/ppermute | solution.py:608
  28.1 5.8 %collective-permute-start.6 = (bf16[37,16,256]{2,1,0:T(8,128)(2,1)}, bf16[37,16,256]{2,1,0:T(8,128)(2,1)}, u32[]{:S(2)}, u32[]{:S(2)}) collective-permute-start(bf16[37,16,256]{2,1,0:T(8,128)(2,1)} %get-tuple-element.40), channel_id=1, source_target_pairs={{0,4},{1,5},{2,6},{3,7},{4,8},{5,9},{6,10},{7,11},{8,12},{9,13},{1... | collective-permute-start | bytes 909320 | tf_op jit(solution)/shard_map/ppermute | solution.py:608
  33.9 14.8 %collective-permute-start.7 = (bf16[37,16,256]{2,1,0:T(8,128)(2,1)}, bf16[37,16,256]{2,1,0:T(8,128)(2,1)}, u32[]{:S(2)}, u32[]{:S(2)}) collective-permute-start(bf16[37,16,256]{2,1,0:T(8,128)(2,1)} %get-tuple-element.41), channel_id=1, source_target_pairs={{0,5},{1,6},{2,7},{4,9},{5,10},{6,11},{8,13},{9,14},{10,15},{12,17... | collective-permute-start | bytes 909320 | tf_op jit(solution)/shard_map/ppermute | solution.py:608
  48.8 0.1 pad_add_fusion
  48.9 0.1 reshape.35
  49.0 0.4 tile.17
  49.4 1.9 %tile.18.wt_ref = bf16[27,32,256]{2,1,0:T(8,128)(2,1)} reshape(bf16[27,32,8,32]{3,2,1,0:T(8,128)(2,1)S(1)} %tile.17) | data formatting | bytes 884736 | tf_op jit(solution)/shard_map/tile | solution.py:651
  51.3 4.1 %copy.32 = bf16[1,1,64,8,8,256]{5,2,4,3,1,0:T(8,128)(2,1)} copy(bf16[1,1,64,8,8,256]{5,4,3,2,1,0:T(8,128)(2,1)} %param.10) | data formatting | bytes 4194304 | tf_op args[3]
  55.4 0.7 copy.35.cols_ref
  56.1 0.7 pad_add_fusion.1.rows2_ref
  56.8 24.5 %dgrad.1 = (f32[64,64,256]{2,1,0:T(8,128)}, bf16[64,64,256]{2,1,0:T(8,128)(2,1)}, bf16[2,8,64,256]{3,2,1,0:T(8,128)(2,1)}, bf16[9,256,256]{2,1,0:T(8,128)(2,1)},...) custom-call(s32[1,1]{1,0:T(1,128)S(6)} %copy.47.count_ref, ...), custom_call_target="tpu_custom_call" | custom-call | tf_op jit(solution)/shard_map/dgrad/pallas_call | solution.py:318
  81.3 0.0 collective-permute-done.3.refs_3_
  81.3 0.0 copy-start.3
  81.4 0.0 copy-start.4
  81.4 0.0 collective-permute-done.5.refs_5_
  81.4 0.7 copy-done.3
  82.1 0.1 copy-done.4
  82.2 0.0 copy-start.17
  82.2 21.1 %wgrad.1 = (bf16[10,10,64,256]{3,2,1,0:T(8,128)(2,1)}, bf16[2,10,64,256]{3,2,1,0:T(8,128)(2,1)}, bf16[2,10,64,256]{3,2,1,0:T(8,128)(2,1)}, f32[224,128]{1,0:T(8,128)}) custom-call(bf16[64,64,256]{2,1,0:T(8,128)(2,1)} %get-tuple-element.31.fm_ref, bf16[64,64,256]{2,1,0:T(8,128)(2,1)} %get-tuple-element.32.gm_ref, ...), custom_call_target="tpu_custom_call" | custom-call | tf_op jit(solution)/shard_map/wgrad/pallas_call | solution.py:495
  103.3 1.5 collective-permute-done.16
  104.8 0.9 add.15
  105.8 0.1 collective-permute-start.17
  105.9 0.7 collective-permute-start.10
  106.5 3.6 %collective-permute-start.11 = (bf16[37,16,256]{2,1,0:T(8,128)(2,1)S(1)}, bf16[37,16,256]{2,1,0:T(8,128)(2,1)S(1)}, u32[]{:S(2)}, u32[]{:S(2)}) collective-permute-start(bf16[37,16,256]{2,1,0:T(8,128)(2,1)S(1)} %copy-done.20), channel_id=1, source_target_pairs={{0,1},{1,2},{2,3},{4,5},{5,6},{6,7},{8,9},{9,10},{10,11},{12,13},{... | collective-permute-start | bytes 909320 | tf_op jit(solution)/shard_map/ppermute | solution.py:615
  110.1 1.3 collective-permute-start.12
  111.4 0.0 collective-permute-done.17
  111.5 2.8 %collective-permute-start.18 = (f32[224,128]{1,0:T(8,128)S(1)}, f32[224,128]{1,0:T(8,128)S(1)}, u32[]{:S(2)}, u32[]{:S(2)}) collective-permute-start(f32[224,128]{1,0:T(8,128)S(1)} %add.16), channel_id=1, source_target_pairs={{0,4},{4,0},{8,12},{12,8},{16,20},{20,16},{24,28},{28,24},{1,5},{5... | collective-permute-start | bytes 344072 | tf_op jit(solution)/shard_map/ppermute | solution.py:628
  114.3 2.8 %collective-permute-done.18 = f32[224,128]{1,0:T(8,128)S(1)} collective-permute-done((f32[224,128]{1,0:T(8,128)S(1)}, f32[224,128]{1,0:T(8,128)S(1)}, u32[]{:S(2)}, u32[]{:S(2)}) %collective-permute-start.18) | collective-permute-done | bytes 114720 | tf_op jit(solution)/shard_map/ppermute | solution.py:628
  117.1 5.0 %collective-permute-start.19 = (f32[224,128]{1,0:T(8,128)S(1)}, f32[224,128]{1,0:T(8,128)S(1)}, u32[]{:S(2)}, u32[]{:S(2)}) collective-permute-start(f32[224,128]{1,0:T(8,128)S(1)} %add.17), channel_id=1, source_target_pairs={{0,8},{4,12},{8,0},{12,4},{16,24},{20,28},{24,16},{28,20},{1,9},{5... | collective-permute-start | bytes 344072 | tf_op jit(solution)/shard_map/ppermute | solution.py:628
  122.1 0.7 collective-permute-start.13
  122.8 1.3 collective-permute-start.14
  124.2 1.3 collective-permute-start.15
  125.5 0.0 collective-permute-done.12.refs_4_
  125.5 6.8 %collective-permute-start.8 = (bf16[37,16,256]{2,1,0:T(8,128)(2,1)}, bf16[37,16,256]{2,1,0:T(8,128)(2,1)S(1)}, u32[]{:S(2)}, u32[]{:S(2)}) collective-permute-start(bf16[37,16,256]{2,1,0:T(8,128)(2,1)} %get-tuple-element.49), channel_id=1, source_target_pairs={{0,5},{1,6},{2,7},{4,9},{5,10},{6,11},{8,13},{9,14},{10,15},{12,17... | collective-permute-start | bytes 909320 | tf_op jit(solution)/shard_map/ppermute | solution.py:615
  132.3 0.0 collective-permute-done.19
  132.3 4.8 %collective-permute-start.9 = (bf16[37,16,256]{2,1,0:T(8,128)(2,1)}, bf16[37,16,256]{2,1,0:T(8,128)(2,1)S(1)}, u32[]{:S(2)}, u32[]{:S(2)}) collective-permute-start(bf16[37,16,256]{2,1,0:T(8,128)(2,1)} %get-tuple-element.50), channel_id=1, source_target_pairs={{0,4},{1,5},{2,6},{3,7},{4,8},{5,9},{6,10},{7,11},{8,12},{9,13},{1... | collective-permute-start | bytes 909320 | tf_op jit(solution)/shard_map/ppermute | solution.py:615
  137.1 0.6 collective-permute-start.20
  137.8 0.6 reshape_squeeze.15.slots_ref
  138.3 0.7 reshape_tile.3.bias_ref
  139.0 1.4 collective-permute-done.14.refs_6_
  140.4 2.9 %collective-permute-done.15.refs_7_ = bf16[37,16,256]{2,1,0:T(8,128)(2,1)S(1)} collective-permute-done((bf16[37,16,256]{2,1,0:T(8,128)(2,1)}, bf16[37,16,256]{2,1,0:T(8,128)(2,1)S(1)}, u32[]{:S(2)}, u32[]{:S(2)}) %collective-permute-start.15) | collective-permute-done | bytes 303136 | tf_op jit(solution)/shard_map/ppermute | solution.py:615
  143.3 7.9 %collective-permute-done.8.refs_0_ = bf16[37,16,256]{2,1,0:T(8,128)(2,1)S(1)} collective-permute-done((bf16[37,16,256]{2,1,0:T(8,128)(2,1)}, bf16[37,16,256]{2,1,0:T(8,128)(2,1)S(1)}, u32[]{:S(2)}, u32[]{:S(2)}) %collective-permute-start.8) | collective-permute-done | bytes 303136 | tf_op jit(solution)/shard_map/ppermute | solution.py:615
  151.2 3.3 %collective-permute-done.9.refs_1_ = bf16[37,16,256]{2,1,0:T(8,128)(2,1)S(1)} collective-permute-done((bf16[37,16,256]{2,1,0:T(8,128)(2,1)}, bf16[37,16,256]{2,1,0:T(8,128)(2,1)S(1)}, u32[]{:S(2)}, u32[]{:S(2)}) %collective-permute-start.9) | collective-permute-done | bytes 303136 | tf_op jit(solution)/shard_map/ppermute | solution.py:615
  154.6 0.7 copy-done.12
  155.2 5.4 %finish.1 = bf16[64,64,256]{2,1,0:T(8,128)(2,1)} custom-call(s32[1,1]{1,0:T(1,128)S(6)} %copy.47.count_ref, f32[64,64,256]{2,1,0:T(8,128)} %get-tuple-element.48.own_ref, s32[1,128]{1,0:T(1,128)} %reshape_squeeze.15.slots_ref, bf16[37,16,256]{2,1,0:T(8,128)(2,1)} %copy-done.11, bf16[37,16,256]{2,1,0:T(8,128)(2,1)} %copy-done.12, ...), custom_call_target="tpu_custom_call" | custom-call | tf_op jit(solution)/shard_map/finish/pallas_call | solution.py:585
  160.6 4.1 %copy.40 = bf16[1,1,64,8,8,256]{5,4,3,2,1,0:T(8,128)(2,1)} copy(bf16[1,1,64,8,8,256]{5,2,4,3,1,0:T(8,128)(2,1)} %bitcast.41) | data formatting | bytes 4194304
  164.7 11.7 %forward.1 = bf16[64,64,256]{2,1,0:T(8,128)(2,1)} custom-call(s32[1,1]{1,0:T(1,128)S(6)} %copy.47.count_ref, bf16[10,10,64,256]{3,2,1,0:T(8,128)(2,1)} %get-tuple-element.42.vm_ref, bf16[2,10,64,256]{3,2,1,0:T(8,128)(2,1)} %get-tuple-element.43.a_ref, bf16[2,10,64,256]{3,2,1,0:T(8,128)(2,1)} %get-tuple-element.44.ax_ref, ...), custom_call_target="tpu_custom_call" | custom-call | tf_op jit(solution)/shard_map/forward/pallas_call | solution.py:545
  176.3 4.1 %copy.39 = bf16[1,1,64,8,8,256]{5,4,3,2,1,0:T(8,128)(2,1)} copy(bf16[1,1,64,8,8,256]{5,2,4,3,1,0:T(8,128)(2,1)} %bitcast.42) | data formatting | bytes 4194304
  180.5 0.5 slice_reduce_fusion
  181.0 0.1 copy.36
  181.1 0.1 copy.37
  181.2 0.4 reshape.39
  181.6 1.0 copy.38
  (60 shorter events, 0.2 us)
Async XLA Ops:
  1.3 4.1 %copy-start.15 = (s32[1,1,8,16]{3,2,1,0:T(8,128)S(1)}, s32[1,1,8,16]{3,2,1,0:T(8,128)}, u32[]{:S(2)}) copy-start(s32[1,1,8,16]{3,2,1,0:T(8,128)} %param.12) | copy-start | bytes 1540
  5.4 13.5 %copy-start.16 = (s32[1,1,64,26]{2,1,3,0:T(1,128)S(1)}, s32[1,1,64,26]{2,1,3,0:T(1,128)}, u32[]{:S(2)}) copy-start(s32[1,1,64,26]{2,1,3,0:T(1,128)} %param.13) | copy-start | bytes 19972
  5.4 43.6 %copy-start.13 = (bf16[3,3,3,32,32]{4,3,2,1,0:T(8,128)(2,1)S(1)}, bf16[3,3,3,32,32]{4,3,2,1,0:T(8,128)(2,1)}, u32[]{:S(2)}) copy-start(bf16[3,3,3,32,32]{4,3,2,1,0:T(8,128)(2,1)} %param.8) | copy-start | bytes 165892
  10.7 13.5 %collective-permute-start = (bf16[37,16,256]{2,1,0:T(8,128)(2,1)}, bf16[37,16,256]{2,1,0:T(8,128)(2,1)S(1)}, u32[]{:S(2)}, u32[]{:S(2)}) collective-permute-start(bf16[37,16,256]{2,1,0:T(8,128)(2,1)} %get-tuple-element.34), channel_id=1, source_target_pairs={{5,0},{6,1},{7,2},{9,4},{10,5},{11,6},{13,8},{14,9},{15,10},{17,12... | collective-permute-start | bytes 909320 | tf_op jit(solution)/shard_map/ppermute | solution.py:608
  11.9 16.2 %collective-permute-start.1 = (bf16[37,16,256]{2,1,0:T(8,128)(2,1)}, bf16[37,16,256]{2,1,0:T(8,128)(2,1)S(1)}, u32[]{:S(2)}, u32[]{:S(2)}) collective-permute-start(bf16[37,16,256]{2,1,0:T(8,128)(2,1)} %get-tuple-element.35), channel_id=1, source_target_pairs={{4,0},{5,1},{6,2},{7,3},{8,4},{9,5},{10,6},{11,7},{12,8},{13,9},{1... | collective-permute-start | bytes 909320 | tf_op jit(solution)/shard_map/ppermute | solution.py:608
  13.2 20.7 %collective-permute-start.2 = (bf16[37,16,256]{2,1,0:T(8,128)(2,1)}, bf16[37,16,256]{2,1,0:T(8,128)(2,1)S(1)}, u32[]{:S(2)}, u32[]{:S(2)}) collective-permute-start(bf16[37,16,256]{2,1,0:T(8,128)(2,1)} %get-tuple-element.36), channel_id=1, source_target_pairs={{4,1},{5,2},{6,3},{8,5},{9,6},{10,7},{12,9},{13,10},{14,11},{16,13... | collective-permute-start | bytes 909320 | tf_op jit(solution)/shard_map/ppermute | solution.py:608
  13.9 67.4 %collective-permute-start.3 = (bf16[37,16,256]{2,1,0:T(8,128)(2,1)}, bf16[37,16,256]{2,1,0:T(8,128)(2,1)S(1)}, u32[]{:S(2)}, u32[]{:S(2)}) collective-permute-start(bf16[37,16,256]{2,1,0:T(8,128)(2,1)} %get-tuple-element.37), channel_id=1, source_target_pairs={{1,0},{2,1},{3,2},{5,4},{6,5},{7,6},{9,8},{10,9},{11,10},{13,12},{... | collective-permute-start | bytes 909320 | tf_op jit(solution)/shard_map/ppermute | solution.py:608
  15.2 66.1 %collective-permute-start.4 = (bf16[37,16,256]{2,1,0:T(8,128)(2,1)}, bf16[37,16,256]{2,1,0:T(8,128)(2,1)S(1)}, u32[]{:S(2)}, u32[]{:S(2)}) collective-permute-start(bf16[37,16,256]{2,1,0:T(8,128)(2,1)} %get-tuple-element.38), channel_id=1, source_target_pairs={{0,1},{1,2},{2,3},{4,5},{5,6},{6,7},{8,9},{9,10},{10,11},{12,13},{... | collective-permute-start | bytes 909320 | tf_op jit(solution)/shard_map/ppermute | solution.py:608
  24.2 27.1 %copy-start = (bf16[37,16,256]{2,1,0:T(8,128)(2,1)}, bf16[37,16,256]{2,1,0:T(8,128)(2,1)S(1)}, u32[]{:S(2)}) copy-start(bf16[37,16,256]{2,1,0:T(8,128)(2,1)S(1)} %collective-permute-done.refs_0_) | copy-start | bytes 909316
  24.2 57.2 %collective-permute-start.5 = (bf16[37,16,256]{2,1,0:T(8,128)(2,1)}, bf16[37,16,256]{2,1,0:T(8,128)(2,1)}, u32[]{:S(2)}, u32[]{:S(2)}) collective-permute-start(bf16[37,16,256]{2,1,0:T(8,128)(2,1)} %get-tuple-element.39), channel_id=1, source_target_pairs={{1,4},{2,5},{3,6},{5,8},{6,9},{7,10},{9,12},{10,13},{11,14},{13,16... | collective-permute-start | bytes 909320 | tf_op jit(solution)/shard_map/ppermute | solution.py:608
  28.1 23.2 %copy-start.1 = (bf16[37,16,256]{2,1,0:T(8,128)(2,1)}, bf16[37,16,256]{2,1,0:T(8,128)(2,1)S(1)}, u32[]{:S(2)}) copy-start(bf16[37,16,256]{2,1,0:T(8,128)(2,1)S(1)} %collective-permute-done.1.refs_1_) | copy-start | bytes 909316
  28.1 53.3 %collective-permute-start.6 = (bf16[37,16,256]{2,1,0:T(8,128)(2,1)}, bf16[37,16,256]{2,1,0:T(8,128)(2,1)}, u32[]{:S(2)}, u32[]{:S(2)}) collective-permute-start(bf16[37,16,256]{2,1,0:T(8,128)(2,1)} %get-tuple-element.40), channel_id=1, source_target_pairs={{0,4},{1,5},{2,6},{3,7},{4,8},{5,9},{6,10},{7,11},{8,12},{9,13},{1... | collective-permute-start | bytes 909320 | tf_op jit(solution)/shard_map/ppermute | solution.py:608
  33.9 17.4 %copy-start.2 = (bf16[37,16,256]{2,1,0:T(8,128)(2,1)}, bf16[37,16,256]{2,1,0:T(8,128)(2,1)S(1)}, u32[]{:S(2)}) copy-start(bf16[37,16,256]{2,1,0:T(8,128)(2,1)S(1)} %collective-permute-done.2.refs_2_) | copy-start | bytes 909316
  33.9 47.5 %collective-permute-start.7 = (bf16[37,16,256]{2,1,0:T(8,128)(2,1)}, bf16[37,16,256]{2,1,0:T(8,128)(2,1)}, u32[]{:S(2)}, u32[]{:S(2)}) collective-permute-start(bf16[37,16,256]{2,1,0:T(8,128)(2,1)} %get-tuple-element.41), channel_id=1, source_target_pairs={{0,5},{1,6},{2,7},{4,9},{5,10},{6,11},{8,13},{9,14},{10,15},{12,17... | collective-permute-start | bytes 909320 | tf_op jit(solution)/shard_map/ppermute | solution.py:608
  48.9 6.4 %copy-start.14 = (s32[192,9]{0,1:T(8,128)}, s32[192,9]{0,1:T(8,128)S(1)}, u32[]{:S(2)}) copy-start(s32[192,9]{0,1:T(8,128)S(1)} %reshape.35) | copy-start | bytes 20740
  81.3 0.7 copy-start.3
  81.4 0.8 copy-start.4
  82.2 23.7 %copy-start.21 = (bf16[37,16,256]{2,1,0:T(8,128)(2,1)S(1)}, bf16[37,16,256]{2,1,0:T(8,128)(2,1)}, u32[]{:S(2)}) copy-start(bf16[37,16,256]{2,1,0:T(8,128)(2,1)} %get-tuple-element.51) | copy-start | bytes 909316
  82.2 24.4 %copy-start.20 = (bf16[37,16,256]{2,1,0:T(8,128)(2,1)S(1)}, bf16[37,16,256]{2,1,0:T(8,128)(2,1)}, u32[]{:S(2)}) copy-start(bf16[37,16,256]{2,1,0:T(8,128)(2,1)} %get-tuple-element.52) | copy-start | bytes 909316
  82.2 28.0 %copy-start.19 = (bf16[37,16,256]{2,1,0:T(8,128)(2,1)S(1)}, bf16[37,16,256]{2,1,0:T(8,128)(2,1)}, u32[]{:S(2)}) copy-start(bf16[37,16,256]{2,1,0:T(8,128)(2,1)} %get-tuple-element.53) | copy-start | bytes 909316
  82.2 40.0 %copy-start.18 = (bf16[37,16,256]{2,1,0:T(8,128)(2,1)S(1)}, bf16[37,16,256]{2,1,0:T(8,128)(2,1)}, u32[]{:S(2)}) copy-start(bf16[37,16,256]{2,1,0:T(8,128)(2,1)} %get-tuple-element.54) | copy-start | bytes 909316
  82.2 56.2 %copy-start.17 = (f32[32]{0:T(128)S(1)}, f32[32]{0:T(128)}, u32[]{:S(2)}) copy-start(f32[32]{0:T(128)} %param.9) | copy-start | bytes 388
  103.3 1.5 collective-permute-start.16
  105.8 5.7 %collective-permute-start.17 = (f32[224,128]{1,0:T(8,128)S(1)}, f32[224,128]{1,0:T(8,128)S(1)}, u32[]{:S(2)}, u32[]{:S(2)}) collective-permute-start(f32[224,128]{1,0:T(8,128)S(1)} %add.15), channel_id=1, source_target_pairs={{0,2},{1,3},{2,0},{3,1},{4,6},{5,7},{6,4},{7,5},{8,10},{9,11},{10,... | collective-permute-start | bytes 344072 | tf_op jit(solution)/shard_map/ppermute | solution.py:628
  105.9 17.0 %collective-permute-start.10 = (bf16[37,16,256]{2,1,0:T(8,128)(2,1)S(1)}, bf16[37,16,256]{2,1,0:T(8,128)(2,1)S(1)}, u32[]{:S(2)}, u32[]{:S(2)}) collective-permute-start(bf16[37,16,256]{2,1,0:T(8,128)(2,1)S(1)} %copy-done.21), channel_id=1, source_target_pairs={{1,4},{2,5},{3,6},{5,8},{6,9},{7,10},{9,12},{10,13},{11,14},{13,16... | collective-permute-start | bytes 909320 | tf_op jit(solution)/shard_map/ppermute | solution.py:615
  106.5 17.6 %collective-permute-start.11 = (bf16[37,16,256]{2,1,0:T(8,128)(2,1)S(1)}, bf16[37,16,256]{2,1,0:T(8,128)(2,1)S(1)}, u32[]{:S(2)}, u32[]{:S(2)}) collective-permute-start(bf16[37,16,256]{2,1,0:T(8,128)(2,1)S(1)} %copy-done.20), channel_id=1, source_target_pairs={{0,1},{1,2},{2,3},{4,5},{5,6},{6,7},{8,9},{9,10},{10,11},{12,13},{... | collective-permute-start | bytes 909320 | tf_op jit(solution)/shard_map/ppermute | solution.py:615
  110.1 15.3 %collective-permute-start.12 = (bf16[37,16,256]{2,1,0:T(8,128)(2,1)S(1)}, bf16[37,16,256]{2,1,0:T(8,128)(2,1)S(1)}, u32[]{:S(2)}, u32[]{:S(2)}) collective-permute-start(bf16[37,16,256]{2,1,0:T(8,128)(2,1)S(1)} %copy-done.19), channel_id=1, source_target_pairs={{1,0},{2,1},{3,2},{5,4},{6,5},{7,6},{9,8},{10,9},{11,10},{13,12},{... | collective-permute-start | bytes 909320 | tf_op jit(solution)/shard_map/ppermute | solution.py:615
  111.5 5.6 %collective-permute-start.18 = (f32[224,128]{1,0:T(8,128)S(1)}, f32[224,128]{1,0:T(8,128)S(1)}, u32[]{:S(2)}, u32[]{:S(2)}) collective-permute-start(f32[224,128]{1,0:T(8,128)S(1)} %add.16), channel_id=1, source_target_pairs={{0,4},{4,0},{8,12},{12,8},{16,20},{20,16},{24,28},{28,24},{1,5},{5... | collective-permute-start | bytes 344072 | tf_op jit(solution)/shard_map/ppermute | solution.py:628
  117.1 15.2 %collective-permute-start.19 = (f32[224,128]{1,0:T(8,128)S(1)}, f32[224,128]{1,0:T(8,128)S(1)}, u32[]{:S(2)}, u32[]{:S(2)}) collective-permute-start(f32[224,128]{1,0:T(8,128)S(1)} %add.17), channel_id=1, source_target_pairs={{0,8},{4,12},{8,0},{12,4},{16,24},{20,28},{24,16},{28,20},{1,9},{5... | collective-permute-start | bytes 344072 | tf_op jit(solution)/shard_map/ppermute | solution.py:628
  122.1 15.0 %collective-permute-start.13 = (bf16[37,16,256]{2,1,0:T(8,128)(2,1)S(1)}, bf16[37,16,256]{2,1,0:T(8,128)(2,1)S(1)}, u32[]{:S(2)}, u32[]{:S(2)}) collective-permute-start(bf16[37,16,256]{2,1,0:T(8,128)(2,1)S(1)} %copy-done.18), channel_id=1, source_target_pairs={{4,1},{5,2},{6,3},{8,5},{9,6},{10,7},{12,9},{13,10},{14,11},{16,13... | collective-permute-start | bytes 909320 | tf_op jit(solution)/shard_map/ppermute | solution.py:615
  122.8 31.7 %copy-start.5 = (bf16[37,16,256]{2,1,0:T(8,128)(2,1)}, bf16[37,16,256]{2,1,0:T(8,128)(2,1)S(1)}, u32[]{:S(2)}) copy-start(bf16[37,16,256]{2,1,0:T(8,128)(2,1)S(1)} %collective-permute-done.10.refs_2_) | copy-start | bytes 909316
  122.8 17.6 %collective-permute-start.14 = (bf16[37,16,256]{2,1,0:T(8,128)(2,1)}, bf16[37,16,256]{2,1,0:T(8,128)(2,1)S(1)}, u32[]{:S(2)}, u32[]{:S(2)}) collective-permute-start(bf16[37,16,256]{2,1,0:T(8,128)(2,1)} %get-tuple-element.55), channel_id=1, source_target_pairs={{4,0},{5,1},{6,2},{7,3},{8,4},{9,5},{10,6},{11,7},{12,8},{13,9},{1... | collective-permute-start | bytes 909320 | tf_op jit(solution)/shard_map/ppermute | solution.py:615
  124.2 30.4 %copy-start.6 = (bf16[37,16,256]{2,1,0:T(8,128)(2,1)}, bf16[37,16,256]{2,1,0:T(8,128)(2,1)S(1)}, u32[]{:S(2)}) copy-start(bf16[37,16,256]{2,1,0:T(8,128)(2,1)S(1)} %collective-permute-done.11.refs_3_) | copy-start | bytes 909316
  124.2 19.1 %collective-permute-start.15 = (bf16[37,16,256]{2,1,0:T(8,128)(2,1)}, bf16[37,16,256]{2,1,0:T(8,128)(2,1)S(1)}, u32[]{:S(2)}, u32[]{:S(2)}) collective-permute-start(bf16[37,16,256]{2,1,0:T(8,128)(2,1)} %get-tuple-element.56), channel_id=1, source_target_pairs={{5,0},{6,1},{7,2},{9,4},{10,5},{11,6},{13,8},{14,9},{15,10},{17,12... | collective-permute-start | bytes 909320 | tf_op jit(solution)/shard_map/ppermute | solution.py:615
  125.5 29.1 %copy-start.7 = (bf16[37,16,256]{2,1,0:T(8,128)(2,1)}, bf16[37,16,256]{2,1,0:T(8,128)(2,1)S(1)}, u32[]{:S(2)}) copy-start(bf16[37,16,256]{2,1,0:T(8,128)(2,1)S(1)} %collective-permute-done.12.refs_4_) | copy-start | bytes 909316
  125.5 25.7 %collective-permute-start.8 = (bf16[37,16,256]{2,1,0:T(8,128)(2,1)}, bf16[37,16,256]{2,1,0:T(8,128)(2,1)S(1)}, u32[]{:S(2)}, u32[]{:S(2)}) collective-permute-start(bf16[37,16,256]{2,1,0:T(8,128)(2,1)} %get-tuple-element.49), channel_id=1, source_target_pairs={{0,5},{1,6},{2,7},{4,9},{5,10},{6,11},{8,13},{9,14},{10,15},{12,17... | collective-permute-start | bytes 909320 | tf_op jit(solution)/shard_map/ppermute | solution.py:615
  132.3 22.2 %collective-permute-start.9 = (bf16[37,16,256]{2,1,0:T(8,128)(2,1)}, bf16[37,16,256]{2,1,0:T(8,128)(2,1)S(1)}, u32[]{:S(2)}, u32[]{:S(2)}) collective-permute-start(bf16[37,16,256]{2,1,0:T(8,128)(2,1)} %get-tuple-element.50), channel_id=1, source_target_pairs={{0,4},{1,5},{2,6},{3,7},{4,8},{5,9},{6,10},{7,11},{8,12},{9,13},{1... | collective-permute-start | bytes 909320 | tf_op jit(solution)/shard_map/ppermute | solution.py:615
  137.1 17.4 %copy-start.8 = (bf16[37,16,256]{2,1,0:T(8,128)(2,1)}, bf16[37,16,256]{2,1,0:T(8,128)(2,1)S(1)}, u32[]{:S(2)}) copy-start(bf16[37,16,256]{2,1,0:T(8,128)(2,1)S(1)} %collective-permute-done.13.refs_5_) | copy-start | bytes 909316
  137.1 43.3 %collective-permute-start.20 = (f32[224,128]{1,0:T(8,128)S(1)}, f32[224,128]{1,0:T(8,128)S(1)}, u32[]{:S(2)}, u32[]{:S(2)}) collective-permute-start(f32[224,128]{1,0:T(8,128)S(1)} %add.18), channel_id=1, source_target_pairs={{0,16},{4,20},{8,24},{12,28},{16,0},{20,4},{24,8},{28,12},{1,17},{... | collective-permute-start | bytes 344072 | tf_op jit(solution)/shard_map/ppermute | solution.py:628
  140.4 14.1 %copy-start.9 = (bf16[37,16,256]{2,1,0:T(8,128)(2,1)}, bf16[37,16,256]{2,1,0:T(8,128)(2,1)S(1)}, u32[]{:S(2)}) copy-start(bf16[37,16,256]{2,1,0:T(8,128)(2,1)S(1)} %collective-permute-done.14.refs_6_) | copy-start | bytes 909316
  143.3 11.3 %copy-start.10 = (bf16[37,16,256]{2,1,0:T(8,128)(2,1)}, bf16[37,16,256]{2,1,0:T(8,128)(2,1)S(1)}, u32[]{:S(2)}) copy-start(bf16[37,16,256]{2,1,0:T(8,128)(2,1)S(1)} %collective-permute-done.15.refs_7_) | copy-start | bytes 909316
  151.2 3.4 %copy-start.11 = (bf16[37,16,256]{2,1,0:T(8,128)(2,1)}, bf16[37,16,256]{2,1,0:T(8,128)(2,1)S(1)}, u32[]{:S(2)}) copy-start(bf16[37,16,256]{2,1,0:T(8,128)(2,1)S(1)} %collective-permute-done.8.refs_0_) | copy-start | bytes 909316
  154.5 0.7 copy-start.12

commit v2 on v1

--- a/solution.py
+++ b/solution.py
@@ -1,3 +1,5 @@
+import functools
+
 import jax
 import jax.numpy as jnp
 from jax import lax
@@ -15,9 +17,17 @@
     + [(x, 7) for x in range(1, 7)]
 )
 ROWS = len(SHELL) + 9
+UNROLL = 8
+XS = 4
 VMEM = pl.BlockSpec(memory_space=pltpu.VMEM)
 SMEM = pl.BlockSpec(memory_space=pltpu.SMEM)
+ANY = pl.BlockSpec(memory_space=pl.ANY)
+DMA = pltpu.SemaphoreType.DMA
 PARAMS = pltpu.CompilerParams(vmem_limit_bytes=56 * 1024 * 1024)
+
+
+def cost(us):
+    return pl.CostEstimate(flops=us * 10**6, bytes_accessed=us * 10**3, transcendentals=0)
 
 
 def dot(a, b):
@@ -94,22 +104,24 @@
     return acc
 
 
-def pack_kernel(count_ref, f_ref, slots_ref, fm_ref, *refs):
-    outs, zp = refs[:8], refs[8]
+def pack_kernel(count_ref, f_ref, slots_ref, fm_ref, right, left, down, up, zp):
     count = count_ref[0, 0]
     live = (lax.broadcasted_iota(jnp.int32, (64, 256), 0) < count).astype(F32)
 
-    def mask_rows(r, _):
-        fm_ref[r] = (f_ref[r].astype(F32) * live).astype(BF16)
-        return _
-
-    lax.fori_loop(0, 64, mask_rows, 0)
+    def mask_rows(i, _):
+        rows = pl.ds(16 * i, 16)
+        v = jnp.transpose(f_ref[:, rows, :], (1, 0, 2))
+        fm_ref[rows] = v * live[None].astype(BF16)
+        return _
+
+    lax.fori_loop(0, 4, mask_rows, 0)
     chosen = one_hot(slots_ref[...] == lax.broadcasted_iota(jnp.int32, (128, 64), 1))
 
     def send(row, value):
         value = value.astype(BF16)
-        for d in range(8):
-            outs[d][row] = value[16 * d : 16 * d + 16]
+        for ref, order in ((right, (4, 7, 2)), (left, (3, 5, 0)), (down, (1,)), (up, (6,))):
+            for i, d in enumerate(order):
+                ref[row, 16 * i : 16 * i + 16, :] = value[16 * d : 16 * d + 16]
 
     for row, (x, y) in enumerate(SHELL):
         send(row, dot(chosen, fm_ref[8 * x + y]))
@@ -130,11 +142,12 @@
     return pl.pallas_call(
         pack_kernel,
         out_shape=[jax.ShapeDtypeStruct((64, 64, 256), BF16)]
-        + [jax.ShapeDtypeStruct((ROWS, 16, 256), BF16)] * 8,
+        + [jax.ShapeDtypeStruct((ROWS, n, 256), BF16) for n in (48, 48, 16, 16)],
         in_specs=[SMEM, VMEM, VMEM],
-        out_specs=[VMEM] * 9,
+        out_specs=[VMEM] * 5,
         scratch_shapes=[pltpu.VMEM((12, 128, 256), F32)],
         compiler_params=PARAMS,
+        cost_estimate=cost(5),
         name="pack",
     )(count, f_rows, slots_col)
 
@@ -177,12 +190,27 @@
 
 def dgrad_kernel(
     count_ref, g_ref, wt_ref, rows3_ref, rows2_ref,
-    own_ref, gm_ref, gz_ref, bm_ref, bym_ref, bye_ref, *refs
+    own_hbm, gm_hbm, gz_hbm, bm_hbm, bym_hbm, bye_hbm, bias_ref, *refs
 ):
-    outs = refs[:8]
-    gpad, gzpad, pg, ag, agx, xf, yf, tz, oht3, oht2 = refs[8:]
+    to_left, to_right, below, above = refs[:4]
+    own_ref, bm_ref, bym_ref, bye_ref, gt, gzt, gpad, gzpad, pg, ag, agx, xf, yf, tz, oht3, oht2, sems = refs[4:]
     count = count_ref[0, 0]
     build_bands(wt_ref, bm_ref, bym_ref, bye_ref)
+    stores = [
+        pltpu.make_async_copy(src, dst, sems.at[i])
+        for i, (src, dst) in enumerate(
+            (
+                (bm_ref, bm_hbm),
+                (bym_ref, bym_hbm),
+                (bye_ref, bye_hbm),
+                (gt, gm_hbm),
+                (gzt, gz_hbm),
+                (own_ref, own_hbm),
+            )
+        )
+    ]
+    for c in stores[:3]:
+        c.start()
     live = (lax.broadcasted_iota(jnp.int32, (64, 256), 0) < count).astype(F32)
     for i in (0, 1, 10, 11):
         gpad[i] = jnp.zeros((8, 64, 256), BF16)
@@ -192,18 +220,26 @@
     pg[:, 9] = jnp.zeros((10, 64, 256), F32)
 
     def load_g(x, _):
-        for y in range(8):
-            v = (g_ref[8 * x + y].astype(F32) * live).astype(BF16)
-            gpad[x + 2, y] = v
-            gm_ref[8 * x + y] = v
-        for s in (0, 1):
-            parts = pack_z(lambda y, h: gpad[x + 2, y, :, h], s == 1, 64)
-            z = jnp.concatenate(parts, axis=1).astype(BF16)
-            gzpad[s, x + 2] = z
-            gz_ref[s, x] = z
-        return _
-
-    lax.fori_loop(0, 8, load_g, 0)
+        both = jnp.transpose(g_ref[:, pl.ds(16 * x, 16), :], (1, 0, 2)) * live[None].astype(BF16)
+        gpad[pl.ds(2 * x + 2, 2)] = both.reshape(2, 8, 64, 256)
+        for i in (0, 1):
+            for s in (0, 1):
+                parts = pack_z(lambda y, h: gpad[2 * x + i + 2, y, :, h], s == 1, 64)
+                z = jnp.concatenate(parts, axis=1).astype(BF16)
+                gzpad[s, 2 * x + i + 2] = z
+        return _
+
+    lax.fori_loop(0, 4, load_g, 0)
+    bias = jnp.zeros((8, 256), F32)
+    for x in range(8):
+        g = gpad[x + 2].reshape(512, 256)
+        gt[:, 512 * x : 512 * x + 512] = g.T
+        bias = bias + jnp.sum(g.astype(F32).reshape(64, 8, 256), axis=0)
+    bias_ref[...] = bias
+    for s in (0, 1):
+        gzt[s] = gzpad[s, 2:10].reshape(512, 256).T
+    for c in stores[3:5]:
+        c.start()
     tsub = lax.broadcasted_iota(jnp.int32, (192, 192), 0)
     tsub2 = lax.broadcasted_iota(jnp.int32, (192, 128), 0)
     for k in range(9):
@@ -259,13 +295,13 @@
             tz[s, x] = spread_z(3 + 2 * s, s, x + 1)
         return _
 
-    lax.fori_loop(0, 8, inner, 0)
+    lax.fori_loop(0, 8, inner, 0, unroll=UNROLL)
     for i, (u, x, ex) in enumerate(((0, 7, 0), (9, 0, 2))):
         def along(y, _, i=i, u=u, ex=ex):
             xf[i, y] = spread(3 * ex + 1, pg[u, y + 1])
             return _
 
-        lax.fori_loop(0, 8, along, 0)
+        lax.fori_loop(0, 8, along, 0, unroll=UNROLL)
         yf[0, x] = yf[0, x] + spread(3 * ex, pg[u, 0])
         yf[1, x] = yf[1, x] + spread(3 * ex + 2, pg[u, 9])
         for s in (0, 1):
@@ -290,10 +326,13 @@
         for y in range(8):
             own_ref[8 * x + y] = own_ref[8 * x + y] + xf[i, y, 0:64, :]
 
+    stores[5].start()
+
     def give(row, value):
         value = value.astype(BF16)
-        for d in range(8):
-            outs[d][row] = value[16 * d : 16 * d + 16]
+        for ref, order in ((to_left, (4, 7, 2)), (to_right, (3, 5, 0)), (below, (6,)), (above, (1,))):
+            for i, d in enumerate(order):
+                ref[row, 16 * i : 16 * i + 16, :] = value[16 * d : 16 * d + 16]
 
     far = slice(64, 192)
     for row, (x, y) in enumerate(SHELL):
@@ -311,6 +350,8 @@
                 for h in (0, 1)
             ]
             give(28 + 3 * g + k, jnp.concatenate(parts, axis=1))
+    for c in stores:
+        c.wait()
 
 
 def dgrad(count, g_rows, wt, rows3, rows2):
@@ -319,16 +360,23 @@
         dgrad_kernel,
         out_shape=[
             sd((64, 64, 256), F32),
-            sd((64, 64, 256), BF16),
-            sd((2, 8, 64, 256), BF16),
+            sd((256, 4096), BF16),
+            sd((2, 256, 512), BF16),
             sd((9, 256, 256), BF16),
             sd((6, 256, 256), BF16),
             sd((6, 256, 256), BF16),
+            sd((8, 256), F32),
         ]
-        + [sd((ROWS, 16, 256), BF16)] * 8,
+        + [sd((ROWS, n, 256), BF16) for n in (48, 48, 16, 16)],
         in_specs=[SMEM] + [VMEM] * 4,
-        out_specs=[VMEM] * 14,
+        out_specs=[ANY] * 6 + [VMEM] * 5,
         scratch_shapes=[
+            pltpu.VMEM((64, 64, 256), F32),
+            pltpu.VMEM((9, 256, 256), BF16),
+            pltpu.VMEM((6, 256, 256), BF16),
+            pltpu.VMEM((6, 256, 256), BF16),
+            pltpu.VMEM((256, 4096), BF16),
+            pltpu.VMEM((2, 256, 512), BF16),
             pltpu.VMEM((12, 8, 64, 256), BF16),
             pltpu.VMEM((2, 12, 64, 256), BF16),
             pltpu.VMEM((10, 10, 64, 256), F32),
@@ -339,20 +387,51 @@
             pltpu.VMEM((2, 8, 192, 256), F32),
             pltpu.VMEM((9, 192, 192), BF16),
             pltpu.VMEM((9, 192, 128), BF16),
+            DMA((6,)),
         ],
         compiler_params=PARAMS,
+        cost_estimate=cost(20000),
         name="dgrad",
     )(count, g_rows, wt, rows3, rows2)
 
 
-def wgrad_kernel(fm_ref, gm_ref, gz_ref, cols_ref, *refs):
-    ins = refs[:8]
-    vm_ref, a_ref, ax_ref, dw_ref = refs[8:12]
-    xt, yt, tz, oh3, acc, fold = refs[12:]
+def wgrad_kernel(fm_hbm, gm_hbm, gz_hbm, cols_ref, bias_ref, mark_hbm, *refs):
+    far_hbm, (vm_hbm, a_hbm, ax_hbm, dw_ref) = refs[:4], refs[4:8]
+    fm_ref, gm_ref, gz_ref, vm_ref, a_ref, ax_ref = refs[8:14]
+    fars, (xt, yt, tz, oh3, acc, fold, sems) = refs[14:18], refs[18:]
+    from_left, from_right, from_below, from_above = fars
+    loads = [
+        pltpu.make_async_copy(src, dst, sems.at[i])
+        for i, (src, dst) in enumerate(
+            zip((fm_hbm, *far_hbm, gm_hbm, gz_hbm), (fm_ref, *fars, gm_ref, gz_ref))
+        )
+    ]
+    for c in loads:
+        c.start()
+    ins = (
+        (from_above, 0), (from_above, 16), (from_above, 32), (from_right, 0),
+        (from_left, 0), (from_below, 0), (from_below, 16), (from_below, 32),
+    )
+
+    def imported(d, row, h=slice(None)):
+        ref, at = ins[d]
+        return ref[row, at : at + 16, h]
+
     far = slice(64, 192)
     tl = lanes(192, 192)
     for k in range(9):
         oh3[k] = one_hot(cols_ref[:, k : k + 1] == tl)
+    loads[0].wait()
+
+    def own_z(x, _):
+        for s in (0, 1):
+            parts = pack_z(lambda y, h: fm_ref[8 * x + y, :, h], s == 0, 64)
+            tz[s, x, 0:64, :] = jnp.concatenate(parts, axis=1).astype(BF16)
+        return _
+
+    lax.fori_loop(0, 8, own_z, 0, unroll=2)
+    for c in loads[1:5]:
+        c.wait()
     for row, (x, y) in enumerate(SHELL):
         places = []
         if x in (0, 7):
@@ -362,22 +441,14 @@
         for ref, i, j in places:
             ref[i, j, 0:64, :] = fm_ref[8 * x + y]
             for d in range(8):
-                ref[i, j, 64 + 16 * d : 80 + 16 * d, :] = ins[d][row]
-
-    def own_z(x, _):
-        for s in (0, 1):
-            parts = pack_z(lambda y, h: fm_ref[8 * x + y, :, h], s == 0, 64)
-            tz[s, x, 0:64, :] = jnp.concatenate(parts, axis=1).astype(BF16)
-        return _
-
-    lax.fori_loop(0, 8, own_z, 0)
+                ref[i, j, 64 + 16 * d : 80 + 16 * d, :] = imported(d, row)
     for i, x in enumerate((7, 0)):
         for s in (0, 1):
             parts = pack_z(lambda y, h: xt[i, y, far, h], s == 0, 128)
             tz[s, x, far, :] = jnp.concatenate(parts, axis=1).astype(BF16)
 
     def compact(row, h):
-        return jnp.concatenate([ins[d][28 + row, :, halves(h)] for d in range(8)], axis=0).astype(F32)
+        return jnp.concatenate([imported(d, 28 + row, halves(h)) for d in range(8)], axis=0).astype(F32)
 
     sub = lanes(128) // 32
     for x in range(1, 7):
@@ -411,52 +482,46 @@
             halo_z(3 + 2 * s, s, x, x + 1)
         return _
 
-    lax.fori_loop(0, 8, fill, 0)
+    lax.fori_loop(0, 8, fill, 0, unroll=UNROLL)
     for i, (u, x, ex) in enumerate(((0, 7, 0), (9, 0, 2))):
         def along(y, _, i=i, u=u, ex=ex):
             vm_ref[u, y + 1] = dot(oh3[3 * ex + 1, 64:128, :], xt[i, y]).astype(BF16)
             return _
 
-        lax.fori_loop(0, 8, along, 0)
+        lax.fori_loop(0, 8, along, 0, unroll=UNROLL)
         vm_ref[u, 0] = dot(oh3[3 * ex + 1, 0:64, :], xt[i, 7]).astype(BF16)
         vm_ref[u, 9] = dot(oh3[3 * ex + 1, 128:192, :], xt[i, 0]).astype(BF16)
         for s in (0, 1):
             halo_z(3 * ex + 2 * s, s, x, u)
 
-    def column(x, a, q):
-        return vm_ref[x + a, q : q + 8].reshape(512, 256)
-
-    def sums(x, bias):
-        g = gm_ref[pl.ds(8 * x, 8)].reshape(512, 256)
-        cols = jnp.concatenate([column(x, a, q) for a in range(3) for q in range(3)], axis=1)
-        part = dot_tn(g, cols)
-
-        @pl.when(x == 0)
-        def _():
-            acc[:, 0:2304] = part
-
-        @pl.when(x != 0)
-        def _():
-            acc[:, 0:2304] = acc[:, 0:2304] + part
-
-        return bias + jnp.sum(g.astype(F32).reshape(64, 8, 256), axis=0)
-
-    bias = lax.fori_loop(0, 8, sums, jnp.zeros((8, 256), F32))
+    stores = [
+        pltpu.make_async_copy(src, dst, sems.at[7 + i])
+        for i, (src, dst) in enumerate(zip((vm_ref, a_ref, ax_ref), (vm_hbm, a_hbm, ax_hbm)))
+    ]
+    for c in stores:
+        c.start()
+    for c in loads[5:]:
+        c.wait()
+
+    def tap(k, _):
+        cols = vm_ref[pl.ds(k // 3, 8), pl.ds(k % 3, 8)].reshape(4096, 256)
+        acc[k] = dot(gm_ref[...], cols)
+        return _
+
+    lax.fori_loop(0, 9, tap, 0)
     for s in (0, 1):
-        z = gz_ref[s].reshape(512, 256)
-        cols = jnp.concatenate(
-            [r[s, a : a + 8].reshape(512, 256) for a in range(3) for r in (a_ref, ax_ref)], axis=1
-        )
-        acc[:, 2304 + 1536 * s : 3840 + 1536 * s] = dot_tn(z, cols)
+        for a in range(3):
+            for i, r in enumerate((a_ref, ax_ref)):
+                acc[9 + 6 * s + 2 * a + i] = dot(gz_ref[s], r[s, a : a + 8].reshape(512, 256))
 
     blk = lanes(32, 256) // 32
 
-    def band_sum(start, r):
+    def band_sum(k, r):
         total = None
         for i in range(8):
             if not 0 <= i + r - 1 < 8:
                 continue
-            v = acc[32 * i : 32 * i + 32, start : start + 256]
+            v = acc[k, 32 * i : 32 * i + 32, :]
             v = jnp.where(blk == i + r - 1, v, jnp.zeros_like(v))
             total = v if total is None else total + v
         return total
@@ -469,16 +534,16 @@
     for a in range(3):
         for q in range(3):
             for r in range(3):
-                total = band_sum(256 * (3 * a + q), r)
+                total = band_sum(3 * a + q, r)
                 if r != 1:
                     s = r // 2
-                    base = 2304 + 1536 * s + 512 * a
+                    base = 9 + 6 * s + 2 * a
                     total = total + band_sum(base, q)
                     if q == 0:
-                        v = acc[0:32, base + 256 : base + 512]
+                        v = acc[base + 1, 0:32, :]
                         total = total + jnp.where(blk == 7, v, jnp.zeros_like(v))
                     if q == 2:
-                        v = acc[224:256, base + 256 : base + 512]
+                        v = acc[base + 1, 224:256, :]
                         total = total + jnp.where(blk == 0, v, jnp.zeros_like(v))
                 t = 9 * a + 3 * q + r
                 fold[32 * t : 32 * t + 32, :] = fold_lanes(total)
@@ -487,10 +552,12 @@
     for k in range(1, 4):
         v = jnp.where(quarter == k, fold[216 * k : 216 * k + 216, :], v)
     dw_ref[0:216, :] = v
-    dw_ref[216:224, :] = fold_lanes(bias)
-
-
-def wgrad(fm, gm, gz, cols3, arrived):
+    dw_ref[216:224, :] = fold_lanes(bias_ref[...])
+    for c in stores:
+        c.wait()
+
+
+def wgrad(fm, gm, gz, cols3, bias_sum, mark, arrived):
     sd = jax.ShapeDtypeStruct
     return pl.pallas_call(
         wgrad_kernel,
@@ -500,32 +567,58 @@
             sd((2, 10, 64, 256), BF16),
             sd((224, 128), F32),
         ],
-        in_specs=[VMEM] * 12,
-        out_specs=[VMEM] * 4,
-        scratch_shapes=[
+        in_specs=[ANY] * 3 + [VMEM] * 2 + [ANY] * 5,
+        out_specs=[ANY] * 3 + [VMEM],
+        scratch_shapes=[pltpu.VMEM(v.shape, v.dtype) for v in (fm, gm, gz)]
+        + [
+            pltpu.VMEM((10, 10, 64, 256), BF16),
+            pltpu.VMEM((2, 10, 64, 256), BF16),
+            pltpu.VMEM((2, 10, 64, 256), BF16),
+        ]
+        + [pltpu.VMEM(v.shape, v.dtype) for v in arrived]
+        + [
             pltpu.VMEM((2, 8, 192, 256), BF16),
             pltpu.VMEM((2, 8, 192, 256), BF16),
             pltpu.VMEM((2, 8, 192, 256), BF16),
             pltpu.VMEM((9, 192, 192), BF16),
-            pltpu.VMEM((256, 5376), F32),
+            pltpu.VMEM((21, 256, 256), F32),
             pltpu.VMEM((864, 128), F32),
+            DMA((10,)),
         ],
         compiler_params=PARAMS,
+        cost_estimate=cost(16),
         name="wgrad",
-    )(fm, gm, gz, cols3, *arrived)
-
-
-def forward_kernel(count_ref, vm_ref, a_ref, ax_ref, bm_ref, bym_ref, bye_ref, bias_ref, out_ref, es):
+    )(fm, gm, gz, cols3, bias_sum, mark, *arrived)
+
+
+def forward_kernel(first, count_ref, vm_hbm, a_hbm, ax_hbm, bm_hbm, bym_hbm, bye_hbm, bias_ref, *refs):
+    out_hbm, vm_ref, a_ref, ax_ref, bm_ref, bym_ref, bye_ref, es, os, ob, sems = refs[-11:]
+    n = os.shape[0] // 8
+    planes = pl.ds(first, n + 2)
+    loads = [
+        pltpu.make_async_copy(a_hbm.at[:, planes], a_ref, sems.at[0]),
+        pltpu.make_async_copy(ax_hbm.at[:, planes], ax_ref, sems.at[1]),
+        pltpu.make_async_copy(bym_hbm, bym_ref, sems.at[2]),
+        pltpu.make_async_copy(bye_hbm, bye_ref, sems.at[3]),
+        pltpu.make_async_copy(bm_hbm, bm_ref, sems.at[4]),
+        pltpu.make_async_copy(vm_hbm.at[planes], vm_ref, sems.at[5]),
+    ]
+    for c in loads:
+        c.start()
     count = count_ref[0, 0]
     live = (lax.broadcasted_iota(jnp.int32, (64, 256), 0) < count).astype(F32)
+    for c in loads[:4]:
+        c.wait()
     for s in (0, 1):
         total = None
         for a in range(3):
             for ref, band in ((a_ref, bym_ref), (ax_ref, bye_ref)):
-                part = dot(ref[s, a : a + 8].reshape(512, 256), band[2 * a + s])
+                part = dot(ref[s, a : a + n].reshape(64 * n, 256), band[2 * a + s])
                 total = part if total is None else total + part
-        es[s] = total.reshape(8, 64, 256)
+        es[s] = total.reshape(n, 64, 256)
     bias = bias_ref[...]
+    for c in loads[4:]:
+        c.wait()
 
     def plane(x, _):
         cols = jnp.concatenate(
@@ -533,38 +626,84 @@
         )
         total = dot(cols, bm_ref[...].reshape(2304, 256)).reshape(8, 64, 256)
         for y in range(8):
-            first, second = unpack_z(lambda h: es[0, x, :, h], lambda h: es[1, x, :, h], y, 64)
-            v = total[y] + jnp.concatenate([first, second], axis=1) + bias
-            out_ref[8 * x + y] = (v * live).astype(BF16)
-        return _
-
-    lax.fori_loop(0, 8, plane, 0)
-
-
-def forward(count, vm, a, ax, bm, bym, bye, bias_row):
+            low, high = unpack_z(lambda h: es[0, x, :, h], lambda h: es[1, x, :, h], y, 64)
+            v = total[y] + jnp.concatenate([low, high], axis=1) + bias
+            os[8 * x + y] = (v * live).astype(BF16)
+        return _
+
+    def store(i):
+        rows = pl.ds(16 * i + 8 * first, 16)
+        return pltpu.make_async_copy(ob.at[:, pl.ds(16 * i, 16)], out_hbm.at[:, rows], sems.at[6 + i])
+
+    def two(i, _):
+        plane(2 * i, 0)
+        plane(2 * i + 1, 0)
+        ob[:, pl.ds(pl.multiple_of(16 * i, 16), 16), :] = jnp.transpose(
+            os[pl.ds(pl.multiple_of(16 * i, 16), 16)], (1, 0, 2)
+        )
+        return _
+
+    for i in range(n // 2):
+        two(i, 0)
+        store(i).start()
+    for i in range(n // 2):
+        store(i).wait()
+
+
+def forward(first, n, count, vm, a, ax, bm, bym, bye, bias_row, before=None):
+    more = [] if before is None else [before]
     return pl.pallas_call(
-        forward_kernel,
+        functools.partial(forward_kernel, first),
         out_shape=jax.ShapeDtypeStruct((64, 64, 256), BF16),
-        in_specs=[SMEM] + [VMEM] * 7,
-        out_specs=VMEM,
-        scratch_shapes=[pltpu.VMEM((2, 8, 64, 256), F32)],
+        in_specs=[SMEM] + [ANY] * 6 + [VMEM] + [ANY] * len(more),
+        out_specs=ANY,
+        input_output_aliases={8: 0} if more else {},
+        scratch_shapes=[
+            pltpu.VMEM((n + 2, 10, 64, 256), BF16),
+            pltpu.VMEM((2, n + 2, 64, 256), BF16),
+            pltpu.VMEM((2, n + 2, 64, 256), BF16),
+            pltpu.VMEM(bm.shape, BF16),
+            pltpu.VMEM(bym.shape, BF16),
+            pltpu.VMEM(bye.shape, BF16),
+            pltpu.VMEM((2, n, 64, 256), F32),
+            pltpu.VMEM((8 * n, 64, 256), BF16),
+            pltpu.VMEM((64, 8 * n, 256), BF16),
+            DMA((6 + n // 2,)),
+        ],
         compiler_params=PARAMS,
+        cost_estimate=cost(1),
         name="forward",
-    )(count, vm, a, ax, bm, bym, bye, bias_row)
-
-
-def finish_kernel(count_ref, own_ref, slots_ref, *refs):
-    ins, out_ref, zp = refs[:8], refs[8], refs[9]
+    )(count, vm, a, ax, bm, bym, bye, bias_row, *more)
+
+
+def finish_kernel(count_ref, own_hbm, slots_ref, *refs):
+    hbm, out_hbm, (zp, os, ob, own_ref) = refs[:4], refs[4], refs[5:9]
+    far, sems = refs[9:13], refs[13]
+    from_left, from_right, from_below, from_above = far
+    loads = [
+        pltpu.make_async_copy(src, dst, sems.at[i])
+        for i, (src, dst) in enumerate(zip((*hbm, own_hbm), (*far, own_ref)))
+    ]
+    for c in loads:
+        c.start()
     count = count_ref[0, 0]
     live = (lax.broadcasted_iota(jnp.int32, (64, 256), 0) < count).astype(F32)
     chosen = one_hot(slots_ref[...] == lax.broadcasted_iota(jnp.int32, (64, 128), 0))
 
     def back(row):
-        return dot(chosen, jnp.concatenate([r[row] for r in ins], axis=0))
-
+        return dot(
+            chosen,
+            jnp.concatenate(
+                [from_below[row], from_left[row, 0:16], from_right[row, 0:16], from_above[row]],
+                axis=0,
+            ),
+        )
+
+    for c in loads:
+        c.wait()
     for row, (x, y) in enumerate(SHELL):
         v = own_ref[8 * x + y] + back(row)
-        out_ref[8 * x + y] = (v * live).astype(BF16)
+        os[8 * x + y] = (v * live).astype(BF16)
     for k in range(9):
         zp[k] = back(28 + k)
 
@@ -578,64 +717,58 @@
                 lambda h: parts[1, h.start // 128], lambda h: parts[0, h.start // 128], y, 64
             )
             v = own_ref[8 * x + y] + jnp.concatenate([first, second], axis=1)
-            out_ref[8 * x + y] = (v * live).astype(BF16)
+            os[8 * x + y] = (v * live).astype(BF16)
+    stores = []
+    for i in range(4):
+        rows = slice(16 * i, 16 * i + 16)
+        ob[:, rows, :] = jnp.transpose(os[rows], (1, 0, 2))
+        stores.append(pltpu.make_async_copy(ob.at[:, rows], out_hbm.at[:, rows], sems.at[5 + i]))
+        stores[-1].start()
+    for c in stores:
+        c.wait()
 
 
 def finish(count, own, slots_row, returned):
     return pl.pallas_call(
         finish_kernel,
         out_shape=jax.ShapeDtypeStruct((64, 64, 256), BF16),
-        in_specs=[SMEM] + [VMEM] * 10,
-        out_specs=VMEM,
-        scratch_shapes=[pltpu.VMEM((9, 64, 256), F32)],
+        in_specs=[SMEM, ANY, VMEM] + [ANY] * 4,
+        out_specs=ANY,
+        scratch_shapes=[
+            pltpu.VMEM((9, 64, 256), F32),
+            pltpu.VMEM((64, 64, 256), BF16),
+            pltpu.VMEM((64, 64, 256), BF16),
+            pltpu.VMEM((64, 64, 256), F32),
+        ]
+        + [pltpu.VMEM(v.shape, BF16) for v in returned]
+        + [DMA((9,))],
         compiler_params=PARAMS,
+        cost_estimate=cost(5),
         name="finish",
     )(count, own, slots_row, *returned)
 
 
-def side_pairs(ds, dt):
-    spaces, tiles = lax.axis_size("space"), lax.axis_size("tile")
-    return [
-        (s * tiles + t, (s + ds) * tiles + t + dt)
-        for s in range(spaces)
-        for t in range(tiles)
-        if 0 <= s + ds < spaces and 0 <= t + dt < tiles
-    ]
-
-
-def send_out(blocks):
-    return [
-        lax.ppermute(b, ("space", "tile"), side_pairs(ds, dt))
-        for b, (ds, dt) in zip(blocks, DEVICE_SIDES)
-    ]
-
-
-def send_back(blocks):
-    return [
-        lax.ppermute(b, ("space", "tile"), side_pairs(-ds, -dt))
-        for b, (ds, dt) in zip(blocks, DEVICE_SIDES)
-    ]
-
-
-def sum_all(value):
+def shift(value, axis, by):
+    n = lax.axis_size(axis)
+    return lax.ppermute(value, axis, [(i, i + by) for i in range(n) if 0 <= i + by < n])
+
+
+def group(*blocks):
+    return jnp.concatenate(blocks, axis=1)
+
+
+def sum_steps():
+    def doubling(axis, n, by):
+        return lambda v: v + lax.ppermute(v, axis, [(i, i ^ by) for i in range(n)])
+
+    found = []
     for axis in ("tile", "space"):
         n = lax.axis_size(axis)
         if n & (n - 1):
-            value = lax.psum(value, axis)
-            continue
-        by = 1
-        while by < n:
-            value = value + lax.ppermute(value, axis, [(i, i ^ by) for i in range(n)])
-            by *= 2
-    return value
-
-
-def to_rows(v):
-    return jnp.transpose(v[0, 0].reshape(64, 64, 256), (1, 0, 2))
-
-
-def from_rows(v):
-    return jnp.transpose(v, (1, 0, 2)).reshape(1, 1, 64, 8, 8, 256)
+            found.append([functools.partial(lax.psum, axis_name=axis)])
+        else:
+            found.append([doubling(axis, n, 1 << k) for k in range(n.bit_length() - 1)])
+    return found
 
 
 def local(features, weight, bias_vector, cotangent, counts, send_slots, neighbours):
@@ -651,21 +784,48 @@
     wt = jnp.tile(weight.reshape(27, 32, 32), (1, 1, 8))
     bias_row = jnp.tile(bias_vector, 8).reshape(1, 256)
 
-    fm, *outgoing = pack(counts, to_rows(features), slots.reshape(128, 1))
-    arrived = send_out(outgoing)
-    own, gm, gz, bm, bym, bye, *back = dgrad(counts, to_rows(cotangent), wt, rows3, rows2)
-    returned = send_back(back)
-    vm, a, ax, dw = wgrad(fm, gm, gz, cols3, arrived)
-    out = forward(counts, vm, a, ax, bm, bym, bye, bias_row)
-    total = sum_all(dw)
-    grad_in = finish(counts, own, slots, returned)
+    fm, right, left, down, up = pack(counts, features.reshape(64, 64, 256), slots.reshape(128, 1))
+    from_left = shift(right, "tile", 1)
+    from_right = shift(left, "tile", -1)
+    go_up = group(from_right[:, 16:32], up, from_left[:, 16:32])
+    go_down = group(from_right[:, 32:48], down, from_left[:, 32:48])
+    go_up, go_down, cotangent = lax.optimization_barrier((go_up, go_down, cotangent))
+    from_below = shift(go_up, "space", 1)
+    from_above = shift(go_down, "space", -1)
+    own, gm, gz, bm, bym, bye, bias_sum, to_left, to_right, below, above = dgrad(
+        counts, cotangent.reshape(64, 64, 256), wt, rows3, rows2
+    )
+    back_right = shift(to_left, "tile", -1)
+    back_left = shift(to_right, "tile", 1)
+    mark = from_below[0, 0:16] + from_above[0, 0:16]
+    mark, back_left, back_right = lax.optimization_barrier((mark, back_left, back_right))
+    go_down = group(back_left[:, 16:32], below, back_right[:, 16:32])
+    go_up = group(back_left[:, 32:48], above, back_right[:, 32:48])
+    go_down, go_up, from_below, from_above = lax.optimization_barrier(
+        (go_down, go_up, from_below, from_above)
+    )
+    back_above = shift(go_down, "space", -1)
+    back_below = shift(go_up, "space", 1)
+    vm, a, ax, dw = wgrad(fm, gm, gz, cols3, bias_sum, mark, (from_left, from_right, from_below, from_above))
+    args = (counts, vm, a, ax, bm, bym, bye, bias_row)
+    near, across = sum_steps()
+    total = dw
+    for step in near:
+        total = step(total)
+    out = forward(0, 8, *args)
+    total, out, back_above, back_below = lax.optimization_barrier((total, out, back_above, back_below))
+    grad_in = finish(counts, own, slots, (back_left, back_right, back_below, back_above))
+    for i, step in enumerate(across):
+        total = step(total)
+        if i == 0:
+            total, grad_in = lax.optimization_barrier((total, grad_in))
 
     scale = float(lax.axis_size("space") * lax.axis_size("tile") * 64 * 512) ** (-0.5)
     total = total * scale
     weight_grad = jnp.transpose(total[:216].reshape(216, 4, 32), (1, 0, 2)).reshape(27, 32, 32)
     weight_grad = jnp.transpose(weight_grad, (0, 2, 1)).reshape(3, 3, 3, 32, 32)
     bias_grad = jnp.sum(total[216:224, :32], axis=0)
-    return from_rows(out), from_rows(grad_in), weight_grad, bias_grad
+    return out.reshape(features.shape), grad_in.reshape(features.shape), weight_grad, bias_grad
 
 
 def solution(mesh):

time: 183 us -> 135 us (0.74)
  local copies, waits for them, and re-layouts: 24.7 us -> 9.73 us
  waiting for transfers between devices: 27.7 us -> 15.1 us
  starting transfers between devices: 59.1 us -> 47.3 us
  Pallas kernels: 67.2 us -> 56.3 us
  other arithmetic: 2.25 us -> 4.14 us
    unnamed x50 -> x34, local copies, waits for them, and re-layouts: 17.8 us -> 0.1 us
    ppermute x21 -> x13, waiting for transfers between devices: 27.7 us -> 15.1 us  [the longest x5 9.38 us: doubling(): return lambda v: v + lax.ppermute(v, axis, [(i, i ^ by) for i in range(n)])]
    ppermute x21 -> x13, starting transfers between devices: 59.1 us -> 47.3 us  [the longest x8 27.7 us: shift(): lax.ppermute(value, axis, [(i, i + by) for i in range(n) if 0 <= i + by <...]
    pallas_call x1, Pallas kernels: 21.1 us -> 13.4 us  [wgrad(): pl.pallas_call(wgrad_kernel, out_shape=[sd((10, 10, 64, 256), BF16), sd((...]
    pallas_call x2, Pallas kernels: 36.2 us -> 32 us  [the longest x1 21.8 us: dgrad(): pl.pallas_call(dgrad_kernel, out_shape=[sd((64, 64, 256), F32), sd((256,...]
  transfers between devices with their start and end apart: 21 -> 13, of which waited for: 8 -> 6; matrix products, arithmetic and copies ran while one was open for 10% -> 6% of each run, Pallas kernels for 23% -> 39%
where the time goes in v2:
time: 135 us; the launch traced here: 134 us
  Pallas kernels  56.3 us (42%)
  starting transfers between devices  47.3 us (35%)
  waiting for transfers between devices  15.1 us (11%)
  local copies, waits for them, and re-layouts  9.73 us (7%)
  other arithmetic  4.14 us (3%)
  between operations  1.67 us (1%)
    ppermute x8, starting transfers between devices, shift(): lax.ppermute(value, axis, [(i, i + by) for i in range(n) if 0 <= i + by <...  27.7 us
    pallas_call x1, Pallas kernels, dgrad(): pl.pallas_call(dgrad_kernel, out_shape=[sd((64, 64, 256), F32), sd((256,...  21.8 us
    ppermute x5, starting transfers between devices, doubling(): return lambda v: v + lax.ppermute(v, axis, [(i, i ^ by) for i in range(n)])  19.5 us
    pallas_call x1, Pallas kernels, wgrad(): pl.pallas_call(wgrad_kernel, out_shape=[sd((10, 10, 64, 256), BF16), sd((...  13.4 us
    pallas_call x1, Pallas kernels, forward(): pl.pallas_call(functools.partial(forward_kernel, first), out_shape=jax.Sh...  10.2 us
    ppermute x5, waiting for transfers between devices, doubling(): return lambda v: v + lax.ppermute(v, axis, [(i, i ^ by) for i in range(n)])  9.38 us
    pallas_call x1, Pallas kernels, finish(): pl.pallas_call(finish_kernel, out_shape=jax.ShapeDtypeStruct((64, 64, 256...  6.25 us
    ppermute x8, waiting for transfers between devices, shift(): lax.ppermute(value, axis, [(i, i + by) for i in range(n) if 0 <= i + by <...  5.68 us
  transfers between devices with their start and end apart: 13, of which 6 were waited for; matrix products, arithmetic and copies ran while one was open for 6% of the time, Pallas kernels for 39%

profile of v2, /device:TPU:0, one launch (start us, length us, event | category | flops | bytes accessed | tf_op | source)
XLA Modules:
  0.0 134.2 jit_solution(10942624762915987715)
XLA Ops:
  0.6 0.0 copy-start.14
  0.6 0.0 copy-start.11
  1.3 1.4 %reshape_reshape_squeeze.4.slots_ref = s32[128,1]{1,0:T(8,128)} reshape(s32[1,1,8,16]{3,2,1,0:T(8,128)} %param.12) | data formatting | bytes 1024 | tf_op jit(solution)/shard_map/reshape;reshape;squeeze | solution.py:787
  2.7 4.6 %pack.1 = (bf16[64,64,256]{2,1,0:T(8,128)(2,1)}, bf16[37,48,256]{2,1,0:T(8,128)(2,1)}, bf16[37,48,256]{2,1,0:T(8,128)(2,1)}, bf16[37,16,256]{2,1,0:T(8,128)(2,1)}, bf16[37,16,256]{2,1,0:T(8,128)(2,1)}) custom-call(s32[1,1]{1,0:T(1,128)S(6)} %copy.35.count_ref, bf16[64,64,256]{2,1,0:T(8,128)(2,1)} %bitcast.37, s32[128,1]{1,0:T(8,128)} %reshape_reshape_squeeze.4.slots_ref), custom_call_target="tpu_custom_call" | custom-call | flops 5000000 | bytes 5000 | tf_op jit(solution)/shard_map/pack/pallas_call | solution.py:142
  7.3 1.3 collective-permute-start
  8.6 4.0 %collective-permute-start.1 = (bf16[37,48,256]{2,1,0:T(8,128)(2,1)}, bf16[37,48,256]{2,1,0:T(8,128)(2,1)}, u32[]{:S(2)}, u32[]{:S(2)}) collective-permute-start(bf16[37,48,256]{2,1,0:T(8,128)(2,1)} %get-tuple-element.43), channel_id=1, source_target_pairs={{0,1},{1,2},{2,3},{4,5},{5,6},{6,7},{8,9},{9,10},{10,11},{12,13},{... | collective-permute-start | bytes 2727944 | tf_op jit(solution)/shard_map/ppermute | solution.py:753
  12.6 0.0 copy-done.14
  12.6 0.1 pad.9.clone
  12.7 0.1 pad_add_fusion
  12.8 0.7 reshape.44
  13.5 0.0 copy-done.11
  13.5 0.4 tile.17
  13.9 0.0 copy-start.7
  13.9 0.0 copy-start.8
  13.9 1.9 %tile.18.wt_ref = bf16[27,32,256]{2,1,0:T(8,128)(2,1)} reshape(bf16[27,32,8,32]{3,2,1,0:T(8,128)(2,1)S(1)} %tile.17) | data formatting | bytes 884736 | tf_op jit(solution)/shard_map/tile | solution.py:784
  15.8 0.7 pad_add_fusion.1.rows2_ref
  16.5 0.0 collective-permute-done.refs_1_
  16.5 0.0 collective-permute-done.1.refs_0_
  16.6 1.4 %fusion.4 = (bf16[37,16,256]{2,1,0:T(8,128)(2,1)S(1)}, bf16[37,16,256]{2,1,0:T(8,128)(2,1)S(1)}) fusion(bf16[37,48,256]{2,1,0:T(8,128)(2,1)} %collective-permute-done.1.refs_0_), kind=kLoop, calls=%fused_computation.15 | loop fusion | bytes 1212416 | tf_op jit(solution)/shard_map/slice | solution.py:791
  18.0 0.0 copy-done.7
  18.0 0.0 copy-done.8
  18.0 0.1 pad_maximum_fusion
  18.1 4.9 %collective-permute-start.2 = (bf16[37,48,256]{2,1,0:T(8,128)(2,1)S(1)}, bf16[37,48,256]{2,1,0:T(8,128)(2,1)S(1)}, u32[]{:S(2)}, u32[]{:S(2)}) collective-permute-start(bf16[37,48,256]{2,1,0:T(8,128)(2,1)S(1)} %get-tuple-element.49), channel_id=1, source_target_pairs={{0,4},{4,8},{8,12},{12,16},{16,20},{20,24},{24,28},{1,5},{5,9},{9,... | collective-permute-start | bytes 2727944 | tf_op jit(solution)/shard_map/ppermute | solution.py:753
  23.0 1.3 collective-permute-start.3
  24.3 21.8 %dgrad.1 = (f32[64,64,256]{2,1,0:T(8,128)}, bf16[256,4096]{1,0:T(8,128)(2,1)}, bf16[2,256,512]{2,1,0:T(8,128)(2,1)}, bf16[9,256,256]{2,1,0:T(8,128)(2,1)}, bf16[...) custom-call(s32[1,1]{1,0:T(1,128)S(6)} %copy.35.count_ref, ...), custom_call_target="tpu_custom_call" | custom-call | flops 20000000000 | bytes 20000000 | tf_op jit(solution)/shard_map/dgrad/pallas_call | solution.py:359
  46.2 0.0 copy-start.10
  46.2 8.3 %collective-permute-start.4 = (bf16[37,48,256]{2,1,0:T(8,128)(2,1)}, bf16[37,48,256]{2,1,0:T(8,128)(2,1)S(1)}, u32[]{:S(2)}, u32[]{:S(2)}) collective-permute-start(bf16[37,48,256]{2,1,0:T(8,128)(2,1)} %get-tuple-element.51), channel_id=1, source_target_pairs={{0,1},{1,2},{2,3},{4,5},{5,6},{6,7},{8,9},{9,10},{10,11},{12,13},{... | collective-permute-start | bytes 2727944 | tf_op jit(solution)/shard_map/ppermute | solution.py:753
  54.5 1.3 collective-permute-start.5
  55.8 2.8 %collective-permute-done.2.refs_2_ = bf16[37,48,256]{2,1,0:T(8,128)(2,1)S(1)} collective-permute-done((bf16[37,48,256]{2,1,0:T(8,128)(2,1)S(1)}, bf16[37,48,256]{2,1,0:T(8,128)(2,1)S(1)}, u32[]{:S(2)}, u32[]{:S(2)}) %collective-permute-start.2) | collective-permute-done | bytes 909344 | tf_op jit(solution)/shard_map/ppermute | solution.py:753
  58.5 0.0 collective-permute-done.3.refs_3_
  58.5 0.6 fusion.mark_hbm
  59.2 0.0 collective-permute-done.4.refs_0_
  59.2 2.0 %collective-permute-done.5.refs_1_ = bf16[37,48,256]{2,1,0:T(8,128)(2,1)S(1)} collective-permute-done((bf16[37,48,256]{2,1,0:T(8,128)(2,1)}, bf16[37,48,256]{2,1,0:T(8,128)(2,1)S(1)}, u32[]{:S(2)}, u32[]{:S(2)}) %collective-permute-start.5) | collective-permute-done | bytes 909344 | tf_op jit(solution)/shard_map/ppermute | solution.py:753
  61.4 1.1 pad_maximum_fusion.3
  62.4 0.0 copy-done.1
  62.5 0.0 copy-done.9
  62.5 0.1 pad_maximum_fusion.2
  62.5 1.3 collective-permute-start.8
  63.8 5.4 %collective-permute-start.9 = (bf16[37,48,256]{2,1,0:T(8,128)(2,1)}, bf16[37,48,256]{2,1,0:T(8,128)(2,1)S(1)}, u32[]{:S(2)}, u32[]{:S(2)}) collective-permute-start(bf16[37,48,256]{2,1,0:T(8,128)(2,1)} %pad_maximum_fusion.3), channel_id=1, source_target_pairs={{0,4},{4,8},{8,12},{12,16},{16,20},{20,24},{24,28},{1,5},{5,9},{9,... | collective-permute-start | bytes 2727944 | tf_op jit(solution)/shard_map/ppermute | solution.py:753
  69.3 0.7 copy.25.cols_ref
  70.0 13.4 %wgrad.1 = (bf16[10,10,64,256]{3,2,1,0:T(8,128)(2,1)}, bf16[2,10,64,256]{3,2,1,0:T(8,128)(2,1)}, bf16[2,10,64,256]{3,2,1,0:T(8,128)(2,1)}, f32[224,128]{1,0:T(8,128)}) custom-call(bf16[64,64,256]{2,1,0:T(8,128)(2,1)} %get-tuple-element.40.fm_hbm, bf16[256,4096]{1,0:T(8,128)(2,1)} %get-tuple-element.46.gm_hbm, bf16[2,256,512]{2,1,0:T(8,128)(2,1)} %get-tuple-element.47.gz_hbm, ...), custom_call_target="tpu_custom_call" | custom-call | flops 16000000 | bytes 16000 | tf_op jit(solution)/shard_map/wgrad/pallas_call | solution.py:562
  83.5 10.8 %collective-permute-start.6 = (f32[224,128]{1,0:T(8,128)}, f32[224,128]{1,0:T(8,128)S(1)}, u32[]{:S(2)}, u32[]{:S(2)}) collective-permute-start(f32[224,128]{1,0:T(8,128)} %get-tuple-element.60), channel_id=1, source_target_pairs={{0,1},{1,0},{2,3},{3,2},{4,5},{5,4},{6,7},{7,6},{8,9},{9,8},{10,11... | collective-permute-start | bytes 344072 | tf_op jit(solution)/shard_map/ppermute | solution.py:762
  94.3 1.2 collective-permute-done.6
  95.5 0.9 add.23
  96.4 0.2 collective-permute-start.7
  96.7 0.6 reshape_tile.3.bias_ref
  97.3 10.2 %forward.1 = bf16[64,64,256]{2,1,0:T(8,128)(2,1)} custom-call(s32[1,1]{1,0:T(1,128)S(6)} %copy.35.count_ref, bf16[10,10,64,256]{3,2,1,0:T(8,128)(2,1)} %get-tuple-element.61.vm_hbm, bf16[2,10,64,256]{3,2,1,0:T(8,128)(2,1)} %get-tuple-element.62.a_hbm, bf16[2,10,64,256]{3,2,1,0:T(8,128)(2,1)} %get-tuple-element.63.ax_hbm, ...), custom_call_target="tpu_custom_call" | custom-call | flops 1000000 | bytes 1000 | tf_op jit(solution)/shard_map/forward/pallas_call | solution.py:655
  107.5 0.0 collective-permute-done.7
  107.6 0.0 collective-permute-done.8.refs_3_
  107.6 0.8 collective-permute-done.9.refs_2_
  108.5 2.4 %collective-permute-start.10 = (f32[224,128]{1,0:T(8,128)S(1)}, f32[224,128]{1,0:T(8,128)S(1)}, u32[]{:S(2)}, u32[]{:S(2)}) collective-permute-start(f32[224,128]{1,0:T(8,128)S(1)} %add.24), channel_id=1, source_target_pairs={{0,4},{4,0},{8,12},{12,8},{16,20},{20,16},{24,28},{28,24},{1,5},{5... | collective-permute-start | bytes 344072 | tf_op jit(solution)/shard_map/ppermute | solution.py:762
  110.8 0.6 reshape_squeeze.7.slots_ref
  111.4 0.0 copy-done.5
  111.4 6.3 %finish.1 = bf16[64,64,256]{2,1,0:T(8,128)(2,1)} custom-call(s32[1,1]{1,0:T(1,128)S(6)} %copy.35.count_ref, f32[64,64,256]{2,1,0:T(8,128)} %get-tuple-element.71.own_hbm, s32[1,128]{1,0:T(1,128)} %reshape_squeeze.7.slots_ref, bf16[37,48,256]{2,1,0:T(8,128)(2,1)} %copy-done, bf16[37,48,256]{2,1,0:T(8,128)(2,1)} %copy-done.1, bf16[37,48,256]{2,1,0:T(8,128)(2,1)} %copy-done.6, ...), custom_call_target="tpu_custom_call" | custom-call | flops 5000000 | bytes 5000 | tf_op jit(solution)/shard_map/finish/pallas_call | solution.py:732
  117.7 0.0 collective-permute-done.10
  117.7 3.2 %collective-permute-start.11 = (f32[224,128]{1,0:T(8,128)S(1)}, f32[224,128]{1,0:T(8,128)S(1)}, u32[]{:S(2)}, u32[]{:S(2)}) collective-permute-start(f32[224,128]{1,0:T(8,128)S(1)} %add.25), channel_id=1, source_target_pairs={{0,8},{4,12},{8,0},{12,4},{16,24},{20,28},{24,16},{28,20},{1,9},{5... | collective-permute-start | bytes 344072 | tf_op jit(solution)/shard_map/ppermute | solution.py:762
  120.9 3.1 %collective-permute-done.11 = f32[224,128]{1,0:T(8,128)S(1)} collective-permute-done((f32[224,128]{1,0:T(8,128)S(1)}, f32[224,128]{1,0:T(8,128)S(1)}, u32[]{:S(2)}, u32[]{:S(2)}) %collective-permute-start.11) | collective-permute-done | bytes 114720 | tf_op jit(solution)/shard_map/ppermute | solution.py:762
  124.1 2.8 %collective-permute-start.12 = (f32[224,128]{1,0:T(8,128)S(1)}, f32[224,128]{1,0:T(8,128)S(1)}, u32[]{:S(2)}, u32[]{:S(2)}) collective-permute-start(f32[224,128]{1,0:T(8,128)S(1)} %add.26), channel_id=1, source_target_pairs={{0,16},{4,20},{8,24},{12,28},{16,0},{20,4},{24,8},{28,12},{1,17},{... | collective-permute-start | bytes 344072 | tf_op jit(solution)/shard_map/ppermute | solution.py:762
  126.9 5.1 %collective-permute-done.12 = f32[224,128]{1,0:T(8,128)S(1)} collective-permute-done((f32[224,128]{1,0:T(8,128)S(1)}, f32[224,128]{1,0:T(8,128)S(1)}, u32[]{:S(2)}, u32[]{:S(2)}) %collective-permute-start.12) | collective-permute-done | bytes 114720 | tf_op jit(solution)/shard_map/ppermute | solution.py:762
  132.0 0.5 slice_reduce_fusion
  132.5 0.1 copy.26
  132.6 0.1 copy.27
  132.7 0.4 reshape.48
  133.2 1.0 copy.28
  (36 shorter events, 0.3 us)
Async XLA Ops:
  0.6 12.0 %copy-start.14 = (s32[1,1,64,26]{2,1,3,0:T(1,128)S(1)}, s32[1,1,64,26]{2,1,3,0:T(1,128)}, u32[]{:S(2)}) copy-start(s32[1,1,64,26]{2,1,3,0:T(1,128)} %param.13) | copy-start | bytes 19972
  0.6 12.8 %copy-start.11 = (bf16[3,3,3,32,32]{4,3,2,1,0:T(8,128)(2,1)S(1)}, bf16[3,3,3,32,32]{4,3,2,1,0:T(8,128)(2,1)}, u32[]{:S(2)}) copy-start(bf16[3,3,3,32,32]{4,3,2,1,0:T(8,128)(2,1)} %param.8) | copy-start | bytes 165892
  7.3 9.2 %collective-permute-start = (bf16[37,48,256]{2,1,0:T(8,128)(2,1)}, bf16[37,48,256]{2,1,0:T(8,128)(2,1)S(1)}, u32[]{:S(2)}, u32[]{:S(2)}) collective-permute-start(bf16[37,48,256]{2,1,0:T(8,128)(2,1)} %get-tuple-element.41), channel_id=1, source_target_pairs={{1,0},{2,1},{3,2},{5,4},{6,5},{7,6},{9,8},{10,9},{11,10},{13,12},{... | collective-permute-start | bytes 2727944 | tf_op jit(solution)/shard_map/ppermute | solution.py:753
  8.6 7.9 %collective-permute-start.1 = (bf16[37,48,256]{2,1,0:T(8,128)(2,1)}, bf16[37,48,256]{2,1,0:T(8,128)(2,1)}, u32[]{:S(2)}, u32[]{:S(2)}) collective-permute-start(bf16[37,48,256]{2,1,0:T(8,128)(2,1)} %get-tuple-element.43), channel_id=1, source_target_pairs={{0,1},{1,2},{2,3},{4,5},{5,6},{6,7},{8,9},{9,10},{10,11},{12,13},{... | collective-permute-start | bytes 2727944 | tf_op jit(solution)/shard_map/ppermute | solution.py:753
  13.9 4.1 %copy-start.7 = (bf16[37,16,256]{2,1,0:T(8,128)(2,1)S(1)}, bf16[37,16,256]{2,1,0:T(8,128)(2,1)}, u32[]{:S(2)}) copy-start(bf16[37,16,256]{2,1,0:T(8,128)(2,1)} %get-tuple-element.44) | copy-start | bytes 909316
  13.9 4.1 %copy-start.8 = (bf16[37,16,256]{2,1,0:T(8,128)(2,1)S(1)}, bf16[37,16,256]{2,1,0:T(8,128)(2,1)}, u32[]{:S(2)}) copy-start(bf16[37,16,256]{2,1,0:T(8,128)(2,1)} %get-tuple-element.42) | copy-start | bytes 909316
  16.5 1.6 %copy-start.2 = (bf16[37,48,256]{2,1,0:T(8,128)(2,1)}, bf16[37,48,256]{2,1,0:T(8,128)(2,1)S(1)}, u32[]{:S(2)}) copy-start(bf16[37,48,256]{2,1,0:T(8,128)(2,1)S(1)} %collective-permute-done.refs_1_) | copy-start | bytes 2727940
  18.1 40.4 %collective-permute-start.2 = (bf16[37,48,256]{2,1,0:T(8,128)(2,1)S(1)}, bf16[37,48,256]{2,1,0:T(8,128)(2,1)S(1)}, u32[]{:S(2)}, u32[]{:S(2)}) collective-permute-start(bf16[37,48,256]{2,1,0:T(8,128)(2,1)S(1)} %get-tuple-element.49), channel_id=1, source_target_pairs={{0,4},{4,8},{8,12},{12,16},{16,20},{20,24},{24,28},{1,5},{5,9},{9,... | collective-permute-start | bytes 2727944 | tf_op jit(solution)/shard_map/ppermute | solution.py:753
  23.0 35.5 %collective-permute-start.3 = (bf16[37,48,256]{2,1,0:T(8,128)(2,1)S(1)}, bf16[37,48,256]{2,1,0:T(8,128)(2,1)S(1)}, u32[]{:S(2)}, u32[]{:S(2)}) collective-permute-start(bf16[37,48,256]{2,1,0:T(8,128)(2,1)S(1)} %get-tuple-element.50), channel_id=1, source_target_pairs={{4,0},{8,4},{12,8},{16,12},{20,16},{24,20},{28,24},{5,1},{9,5},{13... | collective-permute-start | bytes 2727944 | tf_op jit(solution)/shard_map/ppermute | solution.py:753
  46.2 15.2 %copy-start.10 = (bf16[37,16,256]{2,1,0:T(8,128)(2,1)S(1)}, bf16[37,16,256]{2,1,0:T(8,128)(2,1)}, u32[]{:S(2)}) copy-start(bf16[37,16,256]{2,1,0:T(8,128)(2,1)} %get-tuple-element.57) | copy-start | bytes 909316
  46.2 13.0 %collective-permute-start.4 = (bf16[37,48,256]{2,1,0:T(8,128)(2,1)}, bf16[37,48,256]{2,1,0:T(8,128)(2,1)S(1)}, u32[]{:S(2)}, u32[]{:S(2)}) collective-permute-start(bf16[37,48,256]{2,1,0:T(8,128)(2,1)} %get-tuple-element.51), channel_id=1, source_target_pairs={{0,1},{1,2},{2,3},{4,5},{5,6},{6,7},{8,9},{9,10},{10,11},{12,13},{... | collective-permute-start | bytes 2727944 | tf_op jit(solution)/shard_map/ppermute | solution.py:753
  54.5 6.8 %collective-permute-start.5 = (bf16[37,48,256]{2,1,0:T(8,128)(2,1)}, bf16[37,48,256]{2,1,0:T(8,128)(2,1)S(1)}, u32[]{:S(2)}, u32[]{:S(2)}) collective-permute-start(bf16[37,48,256]{2,1,0:T(8,128)(2,1)} %get-tuple-element.52), channel_id=1, source_target_pairs={{1,0},{2,1},{3,2},{5,4},{6,5},{7,6},{9,8},{10,9},{11,10},{13,12},{... | collective-permute-start | bytes 2727944 | tf_op jit(solution)/shard_map/ppermute | solution.py:753
  58.5 3.9 %copy-start.3 = (bf16[37,48,256]{2,1,0:T(8,128)(2,1)}, bf16[37,48,256]{2,1,0:T(8,128)(2,1)S(1)}, u32[]{:S(2)}) copy-start(bf16[37,48,256]{2,1,0:T(8,128)(2,1)S(1)} %collective-permute-done.2.refs_2_) | copy-start | bytes 2727940
  58.5 3.9 %copy-start.4 = (bf16[37,48,256]{2,1,0:T(8,128)(2,1)}, bf16[37,48,256]{2,1,0:T(8,128)(2,1)S(1)}, u32[]{:S(2)}) copy-start(bf16[37,48,256]{2,1,0:T(8,128)(2,1)S(1)} %collective-permute-done.3.refs_3_) | copy-start | bytes 2727940
  59.2 3.3 %copy-start = (bf16[37,48,256]{2,1,0:T(8,128)(2,1)}, bf16[37,48,256]{2,1,0:T(8,128)(2,1)S(1)}, u32[]{:S(2)}) copy-start(bf16[37,48,256]{2,1,0:T(8,128)(2,1)S(1)} %collective-permute-done.4.refs_0_) | copy-start | bytes 2727940
  61.2 1.2 copy-start.1
  61.3 1.2 copy-start.9
  61.3 7.9 %copy-start.12 = (s32[192,9]{0,1:T(8,128)S(1)}, s32[192,9]{0,1:T(8,128)}, u32[]{:S(2)}) copy-start(s32[192,9]{0,1:T(8,128)} %reshape.44) | copy-start | bytes 20740
  62.5 45.0 %collective-permute-start.8 = (bf16[37,48,256]{2,1,0:T(8,128)(2,1)S(1)}, bf16[37,48,256]{2,1,0:T(8,128)(2,1)S(1)}, u32[]{:S(2)}, u32[]{:S(2)}) collective-permute-start(bf16[37,48,256]{2,1,0:T(8,128)(2,1)S(1)} %pad_maximum_fusion.2), channel_id=1, source_target_pairs={{4,0},{8,4},{12,8},{16,12},{20,16},{24,20},{28,24},{5,1},{9,5},{13... | collective-permute-start | bytes 2727944 | tf_op jit(solution)/shard_map/ppermute | solution.py:753
  63.8 44.6 %collective-permute-start.9 = (bf16[37,48,256]{2,1,0:T(8,128)(2,1)}, bf16[37,48,256]{2,1,0:T(8,128)(2,1)S(1)}, u32[]{:S(2)}, u32[]{:S(2)}) collective-permute-start(bf16[37,48,256]{2,1,0:T(8,128)(2,1)} %pad_maximum_fusion.3), channel_id=1, source_target_pairs={{0,4},{4,8},{8,12},{12,16},{16,20},{20,24},{24,28},{1,5},{5,9},{9,... | collective-permute-start | bytes 2727944 | tf_op jit(solution)/shard_map/ppermute | solution.py:753
  70.0 26.6 %copy-start.15 = (f32[32]{0:T(128)S(1)}, f32[32]{0:T(128)}, u32[]{:S(2)}) copy-start(f32[32]{0:T(128)} %param.9) | copy-start | bytes 388
  83.5 12.0 %collective-permute-start.6 = (f32[224,128]{1,0:T(8,128)}, f32[224,128]{1,0:T(8,128)S(1)}, u32[]{:S(2)}, u32[]{:S(2)}) collective-permute-start(f32[224,128]{1,0:T(8,128)} %get-tuple-element.60), channel_id=1, source_target_pairs={{0,1},{1,0},{2,3},{3,2},{4,5},{5,4},{6,7},{7,6},{8,9},{9,8},{10,11... | collective-permute-start | bytes 344072 | tf_op jit(solution)/shard_map/ppermute | solution.py:762
  96.4 11.1 %collective-permute-start.7 = (f32[224,128]{1,0:T(8,128)S(1)}, f32[224,128]{1,0:T(8,128)S(1)}, u32[]{:S(2)}, u32[]{:S(2)}) collective-permute-start(f32[224,128]{1,0:T(8,128)S(1)} %add.23), channel_id=1, source_target_pairs={{0,2},{1,3},{2,0},{3,1},{4,6},{5,7},{6,4},{7,5},{8,10},{9,11},{10,... | collective-permute-start | bytes 344072 | tf_op jit(solution)/shard_map/ppermute | solution.py:762
  97.3 13.5 %copy-start.13 = (s32[1,1,8,16]{3,2,1,0:T(8,128)S(1)}, s32[1,1,8,16]{3,2,1,0:T(8,128)}, u32[]{:S(2)}) copy-start(s32[1,1,8,16]{3,2,1,0:T(8,128)} %param.12) | copy-start | bytes 1540
  107.6 3.8 %copy-start.5 = (bf16[37,48,256]{2,1,0:T(8,128)(2,1)}, bf16[37,48,256]{2,1,0:T(8,128)(2,1)S(1)}, u32[]{:S(2)}) copy-start(bf16[37,48,256]{2,1,0:T(8,128)(2,1)S(1)} %collective-permute-done.8.refs_3_) | copy-start | bytes 2727940
  108.4 3.0 %copy-start.6 = (bf16[37,48,256]{2,1,0:T(8,128)(2,1)}, bf16[37,48,256]{2,1,0:T(8,128)(2,1)S(1)}, u32[]{:S(2)}) copy-start(bf16[37,48,256]{2,1,0:T(8,128)(2,1)S(1)} %collective-permute-done.9.refs_2_) | copy-start | bytes 2727940
  108.5 9.2 %collective-permute-start.10 = (f32[224,128]{1,0:T(8,128)S(1)}, f32[224,128]{1,0:T(8,128)S(1)}, u32[]{:S(2)}, u32[]{:S(2)}) collective-permute-start(f32[224,128]{1,0:T(8,128)S(1)} %add.24), channel_id=1, source_target_pairs={{0,4},{4,0},{8,12},{12,8},{16,20},{20,16},{24,28},{28,24},{1,5},{5... | collective-permute-start | bytes 344072 | tf_op jit(solution)/shard_map/ppermute | solution.py:762
  117.7 6.4 %collective-permute-start.11 = (f32[224,128]{1,0:T(8,128)S(1)}, f32[224,128]{1,0:T(8,128)S(1)}, u32[]{:S(2)}, u32[]{:S(2)}) collective-permute-start(f32[224,128]{1,0:T(8,128)S(1)} %add.25), channel_id=1, source_target_pairs={{0,8},{4,12},{8,0},{12,4},{16,24},{20,28},{24,16},{28,20},{1,9},{5... | collective-permute-start | bytes 344072 | tf_op jit(solution)/shard_map/ppermute | solution.py:762
  124.1 7.9 %collective-permute-start.12 = (f32[224,128]{1,0:T(8,128)S(1)}, f32[224,128]{1,0:T(8,128)S(1)}, u32[]{:S(2)}, u32[]{:S(2)}) collective-permute-start(f32[224,128]{1,0:T(8,128)S(1)} %add.26), channel_id=1, source_target_pairs={{0,16},{4,20},{8,24},{12,28},{16,0},{20,4},{24,8},{28,12},{1,17},{... | collective-permute-start | bytes 344072 | tf_op jit(solution)/shard_map/ppermute | solution.py:762

commit v3 on v2

--- a/solution.py
+++ b/solution.py
@@ -395,16 +395,14 @@
     )(count, g_rows, wt, rows3, rows2)
 
 
-def wgrad_kernel(fm_hbm, gm_hbm, gz_hbm, cols_ref, bias_ref, mark_hbm, *refs):
-    far_hbm, (vm_hbm, a_hbm, ax_hbm, dw_ref) = refs[:4], refs[4:8]
-    fm_ref, gm_ref, gz_ref, vm_ref, a_ref, ax_ref = refs[8:14]
-    fars, (xt, yt, tz, oh3, acc, fold, sems) = refs[14:18], refs[18:]
+def halo_kernel(fm_hbm, cols_ref, *refs):
+    far_hbm, (vm_hbm, a_hbm, ax_hbm) = refs[:4], refs[4:7]
+    fm_ref, vm_ref, a_ref, ax_ref = refs[7:11]
+    fars, (xt, yt, tz, oh3, sems) = refs[11:15], refs[15:]
     from_left, from_right, from_below, from_above = fars
     loads = [
         pltpu.make_async_copy(src, dst, sems.at[i])
-        for i, (src, dst) in enumerate(
-            zip((fm_hbm, *far_hbm, gm_hbm, gz_hbm), (fm_ref, *fars, gm_ref, gz_ref))
-        )
+        for i, (src, dst) in enumerate(zip((fm_hbm, *far_hbm), (fm_ref, *fars)))
     ]
     for c in loads:
         c.start()
@@ -495,12 +493,43 @@
             halo_z(3 * ex + 2 * s, s, x, u)
 
     stores = [
-        pltpu.make_async_copy(src, dst, sems.at[7 + i])
+        pltpu.make_async_copy(src, dst, sems.at[5 + i])
         for i, (src, dst) in enumerate(zip((vm_ref, a_ref, ax_ref), (vm_hbm, a_hbm, ax_hbm)))
     ]
     for c in stores:
         c.start()
-    for c in loads[5:]:
+    for c in stores:
+        c.wait()
+
+
+def halo(fm, cols3, arrived):
+    sd = jax.ShapeDtypeStruct
+    edges = [(10, 10, 64, 256), (2, 10, 64, 256), (2, 10, 64, 256)]
+    return pl.pallas_call(
+        halo_kernel,
+        out_shape=[sd(v, BF16) for v in edges],
+        in_specs=[ANY, VMEM] + [ANY] * 4,
+        out_specs=[ANY] * 3,
+        scratch_shapes=[pltpu.VMEM(v, BF16) for v in [fm.shape, *edges, *(v.shape for v in arrived)]]
+        + [pltpu.VMEM((2, 8, 192, 256), BF16)] * 3
+        + [pltpu.VMEM((9, 192, 192), BF16), DMA((8,))],
+        compiler_params=PARAMS,
+        cost_estimate=cost(1),
+        name="halo",
+    )(fm, cols3, *arrived)
+
+
+def wgrad_kernel(*refs):
+    hbm, bias_ref, dw_ref = refs[:5], refs[5], refs[6]
+    vm_ref, a_ref, ax_ref, gm_ref, gz_ref = refs[7:12]
+    acc, fold, sems = refs[12:]
+    loads = [
+        pltpu.make_async_copy(src, dst, sems.at[i])
+        for i, (src, dst) in enumerate(zip(hbm, refs[7:12]))
+    ]
+    for c in loads:
+        c.start()
+    for c in (loads[0], loads[3]):
         c.wait()
 
     def tap(k, _):
@@ -509,6 +538,8 @@
         return _
 
     lax.fori_loop(0, 9, tap, 0)
+    for c in (loads[1], loads[2], loads[4]):
+        c.wait()
     for s in (0, 1):
         for a in range(3):
             for i, r in enumerate((a_ref, ax_ref)):
@@ -553,42 +584,20 @@
         v = jnp.where(quarter == k, fold[216 * k : 216 * k + 216, :], v)
     dw_ref[0:216, :] = v
     dw_ref[216:224, :] = fold_lanes(bias_ref[...])
-    for c in stores:
-        c.wait()
-
-
-def wgrad(fm, gm, gz, cols3, bias_sum, mark, arrived):
-    sd = jax.ShapeDtypeStruct
+
+
+def wgrad(vm, a, ax, gm, gz, bias_sum):
     return pl.pallas_call(
         wgrad_kernel,
-        out_shape=[
-            sd((10, 10, 64, 256), BF16),
-            sd((2, 10, 64, 256), BF16),
-            sd((2, 10, 64, 256), BF16),
-            sd((224, 128), F32),
-        ],
-        in_specs=[ANY] * 3 + [VMEM] * 2 + [ANY] * 5,
-        out_specs=[ANY] * 3 + [VMEM],
-        scratch_shapes=[pltpu.VMEM(v.shape, v.dtype) for v in (fm, gm, gz)]
-        + [
-            pltpu.VMEM((10, 10, 64, 256), BF16),
-            pltpu.VMEM((2, 10, 64, 256), BF16),
-            pltpu.VMEM((2, 10, 64, 256), BF16),
-        ]
-        + [pltpu.VMEM(v.shape, v.dtype) for v in arrived]
-        + [
-            pltpu.VMEM((2, 8, 192, 256), BF16),
-            pltpu.VMEM((2, 8, 192, 256), BF16),
-            pltpu.VMEM((2, 8, 192, 256), BF16),
-            pltpu.VMEM((9, 192, 192), BF16),
-            pltpu.VMEM((21, 256, 256), F32),
-            pltpu.VMEM((864, 128), F32),
-            DMA((10,)),
-        ],
+        out_shape=jax.ShapeDtypeStruct((224, 128), F32),
+        in_specs=[ANY] * 5 + [VMEM],
+        out_specs=VMEM,
+        scratch_shapes=[pltpu.VMEM(v.shape, v.dtype) for v in (vm, a, ax, gm, gz)]
+        + [pltpu.VMEM((21, 256, 256), F32), pltpu.VMEM((864, 128), F32), DMA((5,))],
         compiler_params=PARAMS,
-        cost_estimate=cost(16),
+        cost_estimate=cost(1),
         name="wgrad",
-    )(fm, gm, gz, cols3, bias_sum, mark, *arrived)
+    )(vm, a, ax, gm, gz, bias_sum)
 
 
 def forward_kernel(first, count_ref, vm_hbm, a_hbm, ax_hbm, bm_hbm, bym_hbm, bye_hbm, bias_ref, *refs):
@@ -761,14 +770,29 @@
     def doubling(axis, n, by):
         return lambda v: v + lax.ppermute(v, axis, [(i, i ^ by) for i in range(n)])
 
+    def fourfold(axis, n, by):
+        def step(v):
+            a, b, c = (lax.ppermute(v, axis, [(i, i ^ (k * by)) for i in range(n)]) for k in (1, 2, 3))
+            return (v + a) + (b + c)
+
+        return step
+
     found = []
     for axis in ("tile", "space"):
         n = lax.axis_size(axis)
         if n & (n - 1):
             found.append([functools.partial(lax.psum, axis_name=axis)])
         else:
-            found.append([doubling(axis, n, 1 << k) for k in range(n.bit_length() - 1)])
-    return found
+            bits = n.bit_length() - 1
+            found.append([])
+            if bits % 2 or axis == "space":
+                found[-1].append(doubling(axis, n, 1))
+            k = len(found[-1])
+            while k < bits:
+                found[-1].append((doubling if k + 1 == bits else fourfold)(axis, n, 1 << k))
+                k += 2
+    near, across = found
+    return near + across[1:], across[:1]
 
 
 def local(features, weight, bias_vector, cotangent, counts, send_slots, neighbours):
@@ -797,16 +821,14 @@
     )
     back_right = shift(to_left, "tile", -1)
     back_left = shift(to_right, "tile", 1)
-    mark = from_below[0, 0:16] + from_above[0, 0:16]
-    mark, back_left, back_right = lax.optimization_barrier((mark, back_left, back_right))
+    vm, a, ax = halo(fm, cols3, (from_left, from_right, from_below, from_above))
+    vm, back_left, back_right = lax.optimization_barrier((vm, back_left, back_right))
     go_down = group(back_left[:, 16:32], below, back_right[:, 16:32])
     go_up = group(back_left[:, 32:48], above, back_right[:, 32:48])
-    go_down, go_up, from_below, from_above = lax.optimization_barrier(
-        (go_down, go_up, from_below, from_above)
-    )
+    go_down, go_up, vm = lax.optimization_barrier((go_down, go_up, vm))
     back_above = shift(go_down, "space", -1)
     back_below = shift(go_up, "space", 1)
-    vm, a, ax, dw = wgrad(fm, gm, gz, cols3, bias_sum, mark, (from_left, from_right, from_below, from_above))
+    dw = wgrad(vm, a, ax, gm, gz, bias_sum)
     args = (counts, vm, a, ax, bm, bym, bye, bias_row)
     near, across = sum_steps()
     total = dw
@@ -815,11 +837,8 @@
     out = forward(0, 8, *args)
     total, out, back_above, back_below = lax.optimization_barrier((total, out, back_above, back_below))
     grad_in = finish(counts, own, slots, (back_left, back_right, back_below, back_above))
-    for i, step in enumerate(across):
+    for step in across:
         total = step(total)
-        if i == 0:
-            total, grad_in = lax.optimization_barrier((total, grad_in))
-
     scale = float(lax.axis_size("space") * lax.axis_size("tile") * 64 * 512) ** (-0.5)
     total = total * scale
     weight_grad = jnp.transpose(total[:216].reshape(216, 4, 32), (1, 0, 2)).reshape(27, 32, 32)

time: 135 us -> 129 us (0.956)
  waiting for transfers between devices: 15.1 us -> 7.47 us
  starting transfers between devices: 47.3 us -> 41.4 us
  Pallas kernels: 56.3 us -> 62.1 us
  local copies, waits for them, and re-layouts: 9.73 us -> 11.5 us
    ppermute x5 -> x1, starting transfers between devices: 19.5 us -> 1.91 us  [doubling(): return lambda v: v + lax.ppermute(v, axis, [(i, i ^ by) for i in range(n)])]
    ppermute x0 -> x6, starting transfers between devices: none -> 10.7 us  [step(): lax.ppermute(v, axis, [(i, i ^ k * by) for i in range(n)])]
    ppermute x5 -> x1, waiting for transfers between devices: 9.38 us -> 0.01 us  [doubling(): return lambda v: v + lax.ppermute(v, axis, [(i, i ^ by) for i in range(n)])]
    ppermute x0 -> x6, waiting for transfers between devices: none -> 5.98 us  [step(): lax.ppermute(v, axis, [(i, i ^ k * by) for i in range(n)])]
    pallas_call x1 -> x2, Pallas kernels: 13.4 us -> 19.3 us  [the longest x1 12 us: wgrad(): pl.pallas_call(wgrad_kernel, out_shape=jax.ShapeDtypeStruct((224, 128), F...]
    ppermute x8, waiting for transfers between devices: 5.68 us -> 1.49 us  [shift(): lax.ppermute(value, axis, [(i, i + by) for i in range(n) if 0 <= i + by <...]
    unnamed x34 -> x32, local copies, waits for them, and re-layouts: 0.1 us -> 2.16 us
  transfers between devices with their start and end apart: 13 -> 15, of which waited for: 6 -> 3; matrix products, arithmetic and copies ran while one was open for 6% -> 5% of each run, Pallas kernels for 39% -> 45%
where the time goes in v3:
time: 129 us
  Pallas kernels  62.1 us (48%)
  starting transfers between devices  41.4 us (32%)
  local copies, waits for them, and re-layouts  11.5 us (9%)
  waiting for transfers between devices  7.47 us (6%)
  other arithmetic  4.65 us (4%)
  between operations  1.75 us (1%)
    ppermute x8, starting transfers between devices, shift(): lax.ppermute(value, axis, [(i, i + by) for i in range(n) if 0 <= i + by <...  28.8 us
    pallas_call x1, Pallas kernels, dgrad(): pl.pallas_call(dgrad_kernel, out_shape=[sd((64, 64, 256), F32), sd((256,...  21.7 us
    pallas_call x1, Pallas kernels, wgrad(): pl.pallas_call(wgrad_kernel, out_shape=jax.ShapeDtypeStruct((224, 128), F...  12 us
    ppermute x6, starting transfers between devices, step(): lax.ppermute(v, axis, [(i, i ^ k * by) for i in range(n)])  10.7 us
    pallas_call x1, Pallas kernels, forward(): pl.pallas_call(functools.partial(forward_kernel, first), out_shape=jax.Sh...  10.2 us
    pallas_call x1, Pallas kernels, halo(): pl.pallas_call(halo_kernel, out_shape=[sd(v, BF16) for v in edges], in_sp...  7.28 us
    pallas_call x1, Pallas kernels, finish(): pl.pallas_call(finish_kernel, out_shape=jax.ShapeDtypeStruct((64, 64, 256...  6.26 us
    ppermute x6, waiting for transfers between devices, step(): lax.ppermute(v, axis, [(i, i ^ k * by) for i in range(n)])  5.98 us
  transfers between devices with their start and end apart: 15, of which 3 were waited for; matrix products, arithmetic and copies ran while one was open for 5% of the time, Pallas kernels for 45%

profile of v3, /device:TPU:0, one launch (start us, length us, event | category | flops | bytes accessed | tf_op | source)
XLA Modules:
  0.0 128.9 jit_solution(17631968659139320879)
XLA Ops:
  1.3 1.4 %reshape_reshape_squeeze.4.slots_ref = s32[128,1]{1,0:T(8,128)} reshape(s32[1,1,8,16]{3,2,1,0:T(8,128)} %param.12) | data formatting | bytes 1024 | tf_op jit(solution)/shard_map/reshape;reshape;squeeze | solution.py:811
  2.7 4.6 %pack.1 = (bf16[64,64,256]{2,1,0:T(8,128)(2,1)}, bf16[37,48,256]{2,1,0:T(8,128)(2,1)}, bf16[37,48,256]{2,1,0:T(8,128)(2,1)}, bf16[37,16,256]{2,1,0:T(8,128)(2,1)}, bf16[37,16,256]{2,1,0:T(8,128)(2,1)}) custom-call(s32[1,1]{1,0:T(1,128)S(6)} %copy.35.count_ref, bf16[64,64,256]{2,1,0:T(8,128)(2,1)} %bitcast.35, s32[128,1]{1,0:T(8,128)} %reshape_reshape_squeeze.4.slots_ref), custom_call_target="tpu_custom_call" | custom-call | flops 5000000 | bytes 5000 | tf_op jit(solution)/shard_map/pack/pallas_call | solution.py:142
  7.3 2.4 %collective-permute-start = (bf16[37,48,256]{2,1,0:T(8,128)(2,1)}, bf16[37,48,256]{2,1,0:T(8,128)(2,1)S(1)}, u32[]{:S(2)}, u32[]{:S(2)}) collective-permute-start(bf16[37,48,256]{2,1,0:T(8,128)(2,1)} %get-tuple-element.37), channel_id=1, source_target_pairs={{0,1},{1,2},{2,3},{4,5},{5,6},{6,7},{8,9},{9,10},{10,11},{12,13},{... | collective-permute-start | bytes 2727944 | tf_op jit(solution)/shard_map/ppermute | solution.py:762
  9.7 1.3 %collective-permute-start.1 = (bf16[37,48,256]{2,1,0:T(8,128)(2,1)}, bf16[37,48,256]{2,1,0:T(8,128)(2,1)}, u32[]{:S(2)}, u32[]{:S(2)}) collective-permute-start(bf16[37,48,256]{2,1,0:T(8,128)(2,1)} %get-tuple-element.38), channel_id=1, source_target_pairs={{1,0},{2,1},{3,2},{5,4},{6,5},{7,6},{9,8},{10,9},{11,10},{13,12},{... | collective-permute-start | bytes 2727944 | tf_op jit(solution)/shard_map/ppermute | solution.py:762
  11.0 0.0 copy-done.13
  11.1 0.1 pad.15.clone
  11.1 0.1 pad_add_fusion
  11.3 0.7 reshape.42
  11.9 0.0 copy-done.10
  11.9 0.4 tile.17
  12.3 1.9 %tile.18.wt_ref = bf16[27,32,256]{2,1,0:T(8,128)(2,1)} reshape(bf16[27,32,8,32]{3,2,1,0:T(8,128)(2,1)S(1)} %tile.17) | data formatting | bytes 884736 | tf_op jit(solution)/shard_map/tile | solution.py:808
  14.3 0.7 pad_add_fusion.1.rows2_ref
  15.0 0.0 collective-permute-done.refs_0_
  15.0 1.5 %collective-permute-done.1.refs_1_ = bf16[37,48,256]{2,1,0:T(8,128)(2,1)} collective-permute-done((bf16[37,48,256]{2,1,0:T(8,128)(2,1)}, bf16[37,48,256]{2,1,0:T(8,128)(2,1)}, u32[]{:S(2)}, u32[]{:S(2)}) %collective-permute-start.1) | collective-permute-done | bytes 909344 | tf_op jit(solution)/shard_map/ppermute | solution.py:762
  16.5 1.1 fusion.2
  17.6 1.4 %pad_maximum_fusion = (bf16[37,48,256]{2,1,0:T(8,128)(2,1)}, bf16[37,48,256]{2,1,0:T(8,128)(2,1)}) fusion(bf16[37,16,256]{2,1,0:T(8,128)(2,1)S(1)} %get-tuple-element.79, bf16[37,16,256]{2,1,0:T(8,128)(2,1)S(1)} %copy-done.7, bf16[37,16,256]{2,1,0:T(8,128)(2,1)S(1)} %get-tuple-element.77, bf16[37,16,256]{2,1,0:T(8,128)(2,1)S(1)} %get-tuple-element.78, ...), kind=kLoop, calls=%fused_computation | loop fusion | flops 5455872 | bytes 3637248 | tf_op jit(solution)/shard_map/concatenate | solution.py:766
  19.0 3.5 %collective-permute-start.2 = (bf16[37,48,256]{2,1,0:T(8,128)(2,1)}, bf16[37,48,256]{2,1,0:T(8,128)(2,1)S(1)}, u32[]{:S(2)}, u32[]{:S(2)}) collective-permute-start(bf16[37,48,256]{2,1,0:T(8,128)(2,1)} %get-tuple-element.41), channel_id=1, source_target_pairs={{0,4},{4,8},{8,12},{12,16},{16,20},{20,24},{24,28},{1,5},{5,9},{9,... | collective-permute-start | bytes 2727944 | tf_op jit(solution)/shard_map/ppermute | solution.py:762
  22.5 1.3 %collective-permute-start.3 = (bf16[37,48,256]{2,1,0:T(8,128)(2,1)}, bf16[37,48,256]{2,1,0:T(8,128)(2,1)}, u32[]{:S(2)}, u32[]{:S(2)}) collective-permute-start(bf16[37,48,256]{2,1,0:T(8,128)(2,1)} %get-tuple-element.42), channel_id=1, source_target_pairs={{4,0},{8,4},{12,8},{16,12},{20,16},{24,20},{28,24},{5,1},{9,5},{13... | collective-permute-start | bytes 2727944 | tf_op jit(solution)/shard_map/ppermute | solution.py:762
  23.8 21.7 %dgrad.1 = (f32[64,64,256]{2,1,0:T(8,128)}, bf16[256,4096]{1,0:T(8,128)(2,1)}, bf16[2,256,512]{2,1,0:T(8,128)(2,1)}, bf16[9,256,256]{2,1,0:T(8,128)(2,1)}, bf16[...) custom-call(s32[1,1]{1,0:T(1,128)S(6)} %copy.35.count_ref, ...), custom_call_target="tpu_custom_call" | custom-call | flops 20000000000 | bytes 20000000 | tf_op jit(solution)/shard_map/dgrad/pallas_call | solution.py:359
  45.5 12.6 %collective-permute-start.4 = (bf16[37,48,256]{2,1,0:T(8,128)(2,1)}, bf16[37,48,256]{2,1,0:T(8,128)(2,1)S(1)}, u32[]{:S(2)}, u32[]{:S(2)}) collective-permute-start(bf16[37,48,256]{2,1,0:T(8,128)(2,1)} %get-tuple-element.45), channel_id=1, source_target_pairs={{0,1},{1,2},{2,3},{4,5},{5,6},{6,7},{8,9},{9,10},{10,11},{12,13},{... | collective-permute-start | bytes 2727944 | tf_op jit(solution)/shard_map/ppermute | solution.py:762
  58.1 1.3 %collective-permute-start.5 = (bf16[37,48,256]{2,1,0:T(8,128)(2,1)}, bf16[37,48,256]{2,1,0:T(8,128)(2,1)S(1)}, u32[]{:S(2)}, u32[]{:S(2)}) collective-permute-start(bf16[37,48,256]{2,1,0:T(8,128)(2,1)} %get-tuple-element.46), channel_id=1, source_target_pairs={{1,0},{2,1},{3,2},{5,4},{6,5},{7,6},{9,8},{10,9},{11,10},{13,12},{... | collective-permute-start | bytes 2727944 | tf_op jit(solution)/shard_map/ppermute | solution.py:762
  59.4 0.8 copy.24.cols_ref
  60.2 0.0 collective-permute-done.2.refs_2_
  60.2 0.0 collective-permute-done.3.refs_3_
  60.2 0.9 copy-done.5
  61.1 7.3 %halo.1 = (bf16[10,10,64,256]{3,2,1,0:T(8,128)(2,1)}, bf16[2,10,64,256]{3,2,1,0:T(8,128)(2,1)}, bf16[2,10,64,256]{3,2,1,0:T(8,128)(2,1)}) custom-call(bf16[64,64,256]{2,1,0:T(8,128)(2,1)} %get-tuple-element.36.fm_hbm, s32[192,9]{1,0:T(8,128)} %copy.24.cols_ref, bf16[37,48,256]{2,1,0:T(8,128)(2,1)} %copy-done.2, ...), custom_call_target="tpu_custom_call" | custom-call | flops 1000000 | bytes 1000 | tf_op jit(solution)/shard_map/halo/pallas_call | solution.py:508
  68.4 0.0 collective-permute-done.4.refs_0_
  68.4 0.0 copy-start
  68.4 0.0 collective-permute-done.5.refs_1_
  68.6 0.9 copy-done.9
  69.5 0.1 pad_maximum_fusion.2
  69.6 0.1 copy-done.1
  69.7 0.1 copy-done.8
  69.8 1.0 pad_maximum_fusion.3
  70.8 1.3 collective-permute-start.12
  72.1 5.1 %collective-permute-start.13 = (bf16[37,48,256]{2,1,0:T(8,128)(2,1)}, bf16[37,48,256]{2,1,0:T(8,128)(2,1)S(1)}, u32[]{:S(2)}, u32[]{:S(2)}) collective-permute-start(bf16[37,48,256]{2,1,0:T(8,128)(2,1)} %pad_maximum_fusion.3), channel_id=1, source_target_pairs={{0,4},{4,8},{8,12},{12,16},{16,20},{20,24},{24,28},{1,5},{5,9},{9,... | collective-permute-start | bytes 2727944 | tf_op jit(solution)/shard_map/ppermute | solution.py:762
  77.2 0.0 copy-start.14
  77.3 12.0 %wgrad.1 = f32[224,128]{1,0:T(8,128)} custom-call(bf16[10,10,64,256]{3,2,1,0:T(8,128)(2,1)} %get-tuple-element.52.refs_0_.vm_hbm, bf16[2,10,64,256]{3,2,1,0:T(8,128)(2,1)} %get-tuple-element.53.refs_1_.a_hbm, bf16[2,10,64,256]{3,2,1,0:T(8,128)(2,1)} %get-tuple-element.54.refs_2_.ax_hbm, bf16[256,4096]{1,0:T(8,128)(2,1)} %get-tuple-element.55.refs_3_, ...), custom_call_target="tpu_custom_call" | custom-call | flops 1000000 | bytes 1000 | tf_op jit(solution)/shard_map/wgrad/pallas_call | solution.py:590
  89.3 5.0 %collective-permute-start.7 = (f32[224,128]{1,0:T(8,128)}, f32[224,128]{1,0:T(8,128)S(1)}, u32[]{:S(2)}, u32[]{:S(2)}) collective-permute-start(f32[224,128]{1,0:T(8,128)} %wgrad.1), channel_id=1, source_target_pairs={{0,2},{1,3},{2,0},{3,1},{4,6},{5,7},{6,4},{7,5},{8,10},{9,11},{10,... | collective-permute-start | bytes 344072 | tf_op jit(solution)/shard_map/ppermute | solution.py:775
  94.3 0.7 collective-permute-start.8
  95.0 0.0 collective-permute-start.6
  95.0 3.2 %collective-permute-done.7 = f32[224,128]{1,0:T(8,128)S(1)} collective-permute-done((f32[224,128]{1,0:T(8,128)}, f32[224,128]{1,0:T(8,128)S(1)}, u32[]{:S(2)}, u32[]{:S(2)}) %collective-permute-start.7) | collective-permute-done | bytes 114720 | tf_op jit(solution)/shard_map/ppermute | solution.py:775
  98.2 2.8 %collective-permute-done.8 = f32[224,128]{1,0:T(8,128)S(1)} collective-permute-done((f32[224,128]{1,0:T(8,128)}, f32[224,128]{1,0:T(8,128)S(1)}, u32[]{:S(2)}, u32[]{:S(2)}) %collective-permute-start.8) | collective-permute-done | bytes 114720 | tf_op jit(solution)/shard_map/ppermute | solution.py:775
  100.9 0.0 collective-permute-done.6
  100.9 0.9 add_add_fusion.1
  101.9 3.4 %collective-permute-start.10 = (f32[224,128]{1,0:T(8,128)S(1)}, f32[224,128]{1,0:T(8,128)S(1)}, u32[]{:S(2)}, u32[]{:S(2)}) collective-permute-start(f32[224,128]{1,0:T(8,128)S(1)} %add_add_fusion.1), channel_id=1, source_target_pairs={{0,16},{4,20},{8,24},{12,28},{16,0},{20,4},{24,8},{28,12},{1,17},{... | collective-permute-start | bytes 344072 | tf_op jit(solution)/shard_map/ppermute | solution.py:775
  105.3 1.3 %collective-permute-start.11 = (f32[224,128]{1,0:T(8,128)S(1)}, f32[224,128]{1,0:T(8,128)S(1)}, u32[]{:S(2)}, u32[]{:S(2)}) collective-permute-start(f32[224,128]{1,0:T(8,128)S(1)} %add_add_fusion.1), channel_id=1, source_target_pairs={{0,24},{4,28},{8,16},{12,20},{16,8},{20,12},{24,0},{28,4},{1,25},{... | collective-permute-start | bytes 344072 | tf_op jit(solution)/shard_map/ppermute | solution.py:775
  106.6 0.3 collective-permute-start.9
  106.9 0.6 reshape_tile.3.bias_ref
  107.5 10.2 %forward.1 = bf16[64,64,256]{2,1,0:T(8,128)(2,1)} custom-call(s32[1,1]{1,0:T(1,128)S(6)} %copy.35.count_ref, bf16[10,10,64,256]{3,2,1,0:T(8,128)(2,1)} %get-tuple-element.52.refs_0_.vm_hbm, bf16[2,10,64,256]{3,2,1,0:T(8,128)(2,1)} %get-tuple-element.53.refs_1_.a_hbm, bf16[2,10,64,256]{3,2,1,0:T(8,128)(2,1)} %get-tuple-element.54.refs_2_.ax_hbm, ...), custom_call_target="tpu_custom_call" | custom-call | flops 1000000 | bytes 1000 | tf_op jit(solution)/shard_map/forward/pallas_call | solution.py:664
  117.8 0.0 collective-permute-done.10
  117.8 0.0 collective-permute-done.11
  117.8 0.0 collective-permute-done.9
  117.8 0.0 collective-permute-done.12.refs_3_
  117.9 0.0 collective-permute-done.13.refs_2_
  117.9 1.9 %collective-permute-start.14 = (f32[224,128]{1,0:T(8,128)S(1)}, f32[224,128]{1,0:T(8,128)S(1)}, u32[]{:S(2)}, u32[]{:S(2)}) collective-permute-start(f32[224,128]{1,0:T(8,128)S(1)} %add_add_fusion), channel_id=1, source_target_pairs={{0,4},{4,0},{8,12},{12,8},{16,20},{20,16},{24,28},{28,24},{1,5},{5... | collective-permute-start | bytes 344072 | tf_op jit(solution)/shard_map/ppermute | solution.py:771
  119.8 0.6 reshape_squeeze.7.slots_ref
  120.4 6.3 %finish.1 = bf16[64,64,256]{2,1,0:T(8,128)(2,1)} custom-call(s32[1,1]{1,0:T(1,128)S(6)} %copy.35.count_ref, f32[64,64,256]{2,1,0:T(8,128)} %get-tuple-element.64.own_hbm, s32[1,128]{1,0:T(1,128)} %reshape_squeeze.7.slots_ref, bf16[37,48,256]{2,1,0:T(8,128)(2,1)} %copy-done, bf16[37,48,256]{2,1,0:T(8,128)(2,1)} %copy-done.1, bf16[37,48,256]{2,1,0:T(8,128)(2,1)} %copy-done.4, ...), custom_call_target="tpu_custom_call" | custom-call | flops 5000000 | bytes 5000 | tf_op jit(solution)/shard_map/finish/pallas_call | solution.py:741
  126.7 0.0 collective-permute-done.14
  126.7 0.5 slice_reduce_fusion
  127.2 0.1 copy.26
  127.3 0.1 copy.27
  127.4 0.4 reshape.47
  127.9 1.0 copy.28
  (36 shorter events, 0.3 us)
Async XLA Ops:
  0.6 10.4 %copy-start.13 = (s32[1,1,64,26]{2,1,3,0:T(1,128)S(1)}, s32[1,1,64,26]{2,1,3,0:T(1,128)}, u32[]{:S(2)}) copy-start(s32[1,1,64,26]{2,1,3,0:T(1,128)} %param.13) | copy-start | bytes 19972
  0.6 11.3 %copy-start.10 = (bf16[3,3,3,32,32]{4,3,2,1,0:T(8,128)(2,1)S(1)}, bf16[3,3,3,32,32]{4,3,2,1,0:T(8,128)(2,1)}, u32[]{:S(2)}) copy-start(bf16[3,3,3,32,32]{4,3,2,1,0:T(8,128)(2,1)} %param.8) | copy-start | bytes 165892
  7.3 7.6 %collective-permute-start = (bf16[37,48,256]{2,1,0:T(8,128)(2,1)}, bf16[37,48,256]{2,1,0:T(8,128)(2,1)S(1)}, u32[]{:S(2)}, u32[]{:S(2)}) collective-permute-start(bf16[37,48,256]{2,1,0:T(8,128)(2,1)} %get-tuple-element.37), channel_id=1, source_target_pairs={{0,1},{1,2},{2,3},{4,5},{5,6},{6,7},{8,9},{9,10},{10,11},{12,13},{... | collective-permute-start | bytes 2727944 | tf_op jit(solution)/shard_map/ppermute | solution.py:762
  9.7 6.7 %collective-permute-start.1 = (bf16[37,48,256]{2,1,0:T(8,128)(2,1)}, bf16[37,48,256]{2,1,0:T(8,128)(2,1)}, u32[]{:S(2)}, u32[]{:S(2)}) collective-permute-start(bf16[37,48,256]{2,1,0:T(8,128)(2,1)} %get-tuple-element.38), channel_id=1, source_target_pairs={{1,0},{2,1},{3,2},{5,4},{6,5},{7,6},{9,8},{10,9},{11,10},{13,12},{... | collective-permute-start | bytes 2727944 | tf_op jit(solution)/shard_map/ppermute | solution.py:762
  12.3 5.3 %copy-start.6 = (bf16[37,16,256]{2,1,0:T(8,128)(2,1)S(1)}, bf16[37,16,256]{2,1,0:T(8,128)(2,1)}, u32[]{:S(2)}) copy-start(bf16[37,16,256]{2,1,0:T(8,128)(2,1)} %get-tuple-element.40) | copy-start | bytes 909316
  12.3 5.3 %copy-start.7 = (bf16[37,16,256]{2,1,0:T(8,128)(2,1)S(1)}, bf16[37,16,256]{2,1,0:T(8,128)(2,1)}, u32[]{:S(2)}) copy-start(bf16[37,16,256]{2,1,0:T(8,128)(2,1)} %get-tuple-element.39) | copy-start | bytes 909316
  15.0 4.0 %copy-start.2 = (bf16[37,48,256]{2,1,0:T(8,128)(2,1)}, bf16[37,48,256]{2,1,0:T(8,128)(2,1)S(1)}, u32[]{:S(2)}) copy-start(bf16[37,48,256]{2,1,0:T(8,128)(2,1)S(1)} %collective-permute-done.refs_0_) | copy-start | bytes 2727940
  19.0 41.2 %collective-permute-start.2 = (bf16[37,48,256]{2,1,0:T(8,128)(2,1)}, bf16[37,48,256]{2,1,0:T(8,128)(2,1)S(1)}, u32[]{:S(2)}, u32[]{:S(2)}) collective-permute-start(bf16[37,48,256]{2,1,0:T(8,128)(2,1)} %get-tuple-element.41), channel_id=1, source_target_pairs={{0,4},{4,8},{8,12},{12,16},{16,20},{20,24},{24,28},{1,5},{5,9},{9,... | collective-permute-start | bytes 2727944 | tf_op jit(solution)/shard_map/ppermute | solution.py:762
  22.5 37.7 %collective-permute-start.3 = (bf16[37,48,256]{2,1,0:T(8,128)(2,1)}, bf16[37,48,256]{2,1,0:T(8,128)(2,1)}, u32[]{:S(2)}, u32[]{:S(2)}) collective-permute-start(bf16[37,48,256]{2,1,0:T(8,128)(2,1)} %get-tuple-element.42), channel_id=1, source_target_pairs={{4,0},{8,4},{12,8},{16,12},{20,16},{24,20},{28,24},{5,1},{9,5},{13... | collective-permute-start | bytes 2727944 | tf_op jit(solution)/shard_map/ppermute | solution.py:762
  23.8 35.7 %copy-start.11 = (s32[192,9]{0,1:T(8,128)S(1)}, s32[192,9]{0,1:T(8,128)}, u32[]{:S(2)}) copy-start(s32[192,9]{0,1:T(8,128)} %reshape.42) | copy-start | bytes 20740
  45.5 22.9 %collective-permute-start.4 = (bf16[37,48,256]{2,1,0:T(8,128)(2,1)}, bf16[37,48,256]{2,1,0:T(8,128)(2,1)S(1)}, u32[]{:S(2)}, u32[]{:S(2)}) collective-permute-start(bf16[37,48,256]{2,1,0:T(8,128)(2,1)} %get-tuple-element.45), channel_id=1, source_target_pairs={{0,1},{1,2},{2,3},{4,5},{5,6},{6,7},{8,9},{9,10},{10,11},{12,13},{... | collective-permute-start | bytes 2727944 | tf_op jit(solution)/shard_map/ppermute | solution.py:762
  58.1 10.3 %collective-permute-start.5 = (bf16[37,48,256]{2,1,0:T(8,128)(2,1)}, bf16[37,48,256]{2,1,0:T(8,128)(2,1)S(1)}, u32[]{:S(2)}, u32[]{:S(2)}) collective-permute-start(bf16[37,48,256]{2,1,0:T(8,128)(2,1)} %get-tuple-element.46), channel_id=1, source_target_pairs={{1,0},{2,1},{3,2},{5,4},{6,5},{7,6},{9,8},{10,9},{11,10},{13,12},{... | collective-permute-start | bytes 2727944 | tf_op jit(solution)/shard_map/ppermute | solution.py:762
  60.2 0.9 copy-start.5
  68.4 1.1 copy-start.9
  68.4 1.2 copy-start
  68.4 1.2 copy-start.1
  68.5 1.3 %copy-start.8 = (bf16[37,16,256]{2,1,0:T(8,128)(2,1)S(1)}, bf16[37,16,256]{2,1,0:T(8,128)(2,1)}, u32[]{:S(2)}) copy-start(bf16[37,16,256]{2,1,0:T(8,128)(2,1)} %get-tuple-element.50) | copy-start | bytes 909316
  70.8 47.0 %collective-permute-start.12 = (bf16[37,48,256]{2,1,0:T(8,128)(2,1)S(1)}, bf16[37,48,256]{2,1,0:T(8,128)(2,1)S(1)}, u32[]{:S(2)}, u32[]{:S(2)}) collective-permute-start(bf16[37,48,256]{2,1,0:T(8,128)(2,1)S(1)} %pad_maximum_fusion.2), channel_id=1, source_target_pairs={{4,0},{8,4},{12,8},{16,12},{20,16},{24,20},{28,24},{5,1},{9,5},{13... | collective-permute-start | bytes 2727944 | tf_op jit(solution)/shard_map/ppermute | solution.py:762
  72.1 45.8 %collective-permute-start.13 = (bf16[37,48,256]{2,1,0:T(8,128)(2,1)}, bf16[37,48,256]{2,1,0:T(8,128)(2,1)S(1)}, u32[]{:S(2)}, u32[]{:S(2)}) collective-permute-start(bf16[37,48,256]{2,1,0:T(8,128)(2,1)} %pad_maximum_fusion.3), channel_id=1, source_target_pairs={{0,4},{4,8},{8,12},{12,16},{16,20},{20,24},{24,28},{1,5},{5,9},{9,... | collective-permute-start | bytes 2727944 | tf_op jit(solution)/shard_map/ppermute | solution.py:762
  77.2 29.6 %copy-start.14 = (f32[32]{0:T(128)S(1)}, f32[32]{0:T(128)}, u32[]{:S(2)}) copy-start(f32[32]{0:T(128)} %param.9) | copy-start | bytes 388
  89.3 8.9 %collective-permute-start.7 = (f32[224,128]{1,0:T(8,128)}, f32[224,128]{1,0:T(8,128)S(1)}, u32[]{:S(2)}, u32[]{:S(2)}) collective-permute-start(f32[224,128]{1,0:T(8,128)} %wgrad.1), channel_id=1, source_target_pairs={{0,2},{1,3},{2,0},{3,1},{4,6},{5,7},{6,4},{7,5},{8,10},{9,11},{10,... | collective-permute-start | bytes 344072 | tf_op jit(solution)/shard_map/ppermute | solution.py:775
  94.3 6.7 %collective-permute-start.8 = (f32[224,128]{1,0:T(8,128)}, f32[224,128]{1,0:T(8,128)S(1)}, u32[]{:S(2)}, u32[]{:S(2)}) collective-permute-start(f32[224,128]{1,0:T(8,128)} %wgrad.1), channel_id=1, source_target_pairs={{0,3},{1,2},{2,1},{3,0},{4,7},{5,6},{6,5},{7,4},{8,11},{9,10},{10,... | collective-permute-start | bytes 344072 | tf_op jit(solution)/shard_map/ppermute | solution.py:775
  95.0 6.0 %collective-permute-start.6 = (f32[224,128]{1,0:T(8,128)}, f32[224,128]{1,0:T(8,128)S(1)}, u32[]{:S(2)}, u32[]{:S(2)}) collective-permute-start(f32[224,128]{1,0:T(8,128)} %wgrad.1), channel_id=1, source_target_pairs={{0,1},{1,0},{2,3},{3,2},{4,5},{5,4},{6,7},{7,6},{8,9},{9,8},{10,11... | collective-permute-start | bytes 344072 | tf_op jit(solution)/shard_map/ppermute | solution.py:775
  101.9 15.9 %collective-permute-start.10 = (f32[224,128]{1,0:T(8,128)S(1)}, f32[224,128]{1,0:T(8,128)S(1)}, u32[]{:S(2)}, u32[]{:S(2)}) collective-permute-start(f32[224,128]{1,0:T(8,128)S(1)} %add_add_fusion.1), channel_id=1, source_target_pairs={{0,16},{4,20},{8,24},{12,28},{16,0},{20,4},{24,8},{28,12},{1,17},{... | collective-permute-start | bytes 344072 | tf_op jit(solution)/shard_map/ppermute | solution.py:775
  105.3 12.5 %collective-permute-start.11 = (f32[224,128]{1,0:T(8,128)S(1)}, f32[224,128]{1,0:T(8,128)S(1)}, u32[]{:S(2)}, u32[]{:S(2)}) collective-permute-start(f32[224,128]{1,0:T(8,128)S(1)} %add_add_fusion.1), channel_id=1, source_target_pairs={{0,24},{4,28},{8,16},{12,20},{16,8},{20,12},{24,0},{28,4},{1,25},{... | collective-permute-start | bytes 344072 | tf_op jit(solution)/shard_map/ppermute | solution.py:775
  106.6 11.2 %collective-permute-start.9 = (f32[224,128]{1,0:T(8,128)S(1)}, f32[224,128]{1,0:T(8,128)S(1)}, u32[]{:S(2)}, u32[]{:S(2)}) collective-permute-start(f32[224,128]{1,0:T(8,128)S(1)} %add_add_fusion.1), channel_id=1, source_target_pairs={{0,8},{4,12},{8,0},{12,4},{16,24},{20,28},{24,16},{28,20},{1,9},{5... | collective-permute-start | bytes 344072 | tf_op jit(solution)/shard_map/ppermute | solution.py:775
  107.5 12.3 %copy-start.12 = (s32[1,1,8,16]{3,2,1,0:T(8,128)S(1)}, s32[1,1,8,16]{3,2,1,0:T(8,128)}, u32[]{:S(2)}) copy-start(s32[1,1,8,16]{3,2,1,0:T(8,128)} %param.12) | copy-start | bytes 1540
  117.8 2.5 %copy-start.3 = (bf16[37,48,256]{2,1,0:T(8,128)(2,1)}, bf16[37,48,256]{2,1,0:T(8,128)(2,1)S(1)}, u32[]{:S(2)}) copy-start(bf16[37,48,256]{2,1,0:T(8,128)(2,1)S(1)} %collective-permute-done.12.refs_3_) | copy-start | bytes 2727940
  117.9 2.5 %copy-start.4 = (bf16[37,48,256]{2,1,0:T(8,128)(2,1)}, bf16[37,48,256]{2,1,0:T(8,128)(2,1)S(1)}, u32[]{:S(2)}) copy-start(bf16[37,48,256]{2,1,0:T(8,128)(2,1)S(1)} %collective-permute-done.13.refs_2_) | copy-start | bytes 2727940
  117.9 8.8 %collective-permute-start.14 = (f32[224,128]{1,0:T(8,128)S(1)}, f32[224,128]{1,0:T(8,128)S(1)}, u32[]{:S(2)}, u32[]{:S(2)}) collective-permute-start(f32[224,128]{1,0:T(8,128)S(1)} %add_add_fusion), channel_id=1, source_target_pairs={{0,4},{4,0},{8,12},{12,8},{16,20},{20,16},{24,28},{28,24},{1,5},{5... | collective-permute-start | bytes 344072 | tf_op jit(solution)/shard_map/ppermute | solution.py:771

commit v4 on v3

--- a/solution.py
+++ b/solution.py
@@ -537,7 +537,7 @@
         acc[k] = dot(gm_ref[...], cols)
         return _
 
-    lax.fori_loop(0, 9, tap, 0)
+    lax.fori_loop(0, 9, tap, 0, unroll=3)
     for c in (loads[1], loads[2], loads[4]):
         c.wait()
     for s in (0, 1):

time: 129 us -> 129 us (level)
  transfers between devices with their start and end apart: 15 -> 15, of which waited for: 3 -> 4; matrix products, arithmetic and copies ran while one was open for 5% -> 5% of each run, Pallas kernels for 45% -> 44%
where the time goes in v4:
time: 129 us; the launch traced here: 128 us
  Pallas kernels  61 us (47%)
  starting transfers between devices  41.9 us (32%)
  local copies, waits for them, and re-layouts  11.5 us (9%)
  waiting for transfers between devices  7.67 us (6%)
  other arithmetic  4.65 us (4%)
  between operations  1.73 us (1%)
    ppermute x8, starting transfers between devices, shift(): lax.ppermute(value, axis, [(i, i + by) for i in range(n) if 0 <= i + by <...  28.8 us
    pallas_call x1, Pallas kernels, dgrad(): pl.pallas_call(dgrad_kernel, out_shape=[sd((64, 64, 256), F32), sd((256,...  21.7 us
    pallas_call x1, Pallas kernels, wgrad(): pl.pallas_call(wgrad_kernel, out_shape=jax.ShapeDtypeStruct((224, 128), F...  11 us
    ppermute x6, starting transfers between devices, step(): lax.ppermute(v, axis, [(i, i ^ k * by) for i in range(n)])  10.7 us
    pallas_call x1, Pallas kernels, forward(): pl.pallas_call(functools.partial(forward_kernel, first), out_shape=jax.Sh...  10.2 us
    pallas_call x1, Pallas kernels, halo(): pl.pallas_call(halo_kernel, out_shape=[sd(v, BF16) for v in edges], in_sp...  7.28 us
    pallas_call x1, Pallas kernels, finish(): pl.pallas_call(finish_kernel, out_shape=jax.ShapeDtypeStruct((64, 64, 256...  6.25 us
    ppermute x6, waiting for transfers between devices, step(): lax.ppermute(v, axis, [(i, i ^ k * by) for i in range(n)])  5.98 us
  transfers between devices with their start and end apart: 15, of which 4 were waited for; matrix products, arithmetic and copies ran while one was open for 5% of the time, Pallas kernels for 44%

profile of v4, /device:TPU:0, one launch (start us, length us, event | category | flops | bytes accessed | tf_op | source)
XLA Modules:
  0.0 128.5 jit_solution(4595873620928530446)
XLA Ops:
  1.3 1.4 %reshape_reshape_squeeze.4.slots_ref = s32[128,1]{1,0:T(8,128)} reshape(s32[1,1,8,16]{3,2,1,0:T(8,128)} %param.12) | data formatting | bytes 1024 | tf_op jit(solution)/shard_map/reshape;reshape;squeeze | solution.py:811
  2.7 4.6 %pack.1 = (bf16[64,64,256]{2,1,0:T(8,128)(2,1)}, bf16[37,48,256]{2,1,0:T(8,128)(2,1)}, bf16[37,48,256]{2,1,0:T(8,128)(2,1)}, bf16[37,16,256]{2,1,0:T(8,128)(2,1)}, bf16[37,16,256]{2,1,0:T(8,128)(2,1)}) custom-call(s32[1,1]{1,0:T(1,128)S(6)} %copy.35.count_ref, bf16[64,64,256]{2,1,0:T(8,128)(2,1)} %bitcast.35, s32[128,1]{1,0:T(8,128)} %reshape_reshape_squeeze.4.slots_ref), custom_call_target="tpu_custom_call" | custom-call | flops 5000000 | bytes 5000 | tf_op jit(solution)/shard_map/pack/pallas_call | solution.py:142
  7.3 2.4 %collective-permute-start = (bf16[37,48,256]{2,1,0:T(8,128)(2,1)}, bf16[37,48,256]{2,1,0:T(8,128)(2,1)S(1)}, u32[]{:S(2)}, u32[]{:S(2)}) collective-permute-start(bf16[37,48,256]{2,1,0:T(8,128)(2,1)} %get-tuple-element.37), channel_id=1, source_target_pairs={{0,1},{1,2},{2,3},{4,5},{5,6},{6,7},{8,9},{9,10},{10,11},{12,13},{... | collective-permute-start | bytes 2727944 | tf_op jit(solution)/shard_map/ppermute | solution.py:762
  9.7 1.3 %collective-permute-start.1 = (bf16[37,48,256]{2,1,0:T(8,128)(2,1)}, bf16[37,48,256]{2,1,0:T(8,128)(2,1)}, u32[]{:S(2)}, u32[]{:S(2)}) collective-permute-start(bf16[37,48,256]{2,1,0:T(8,128)(2,1)} %get-tuple-element.38), channel_id=1, source_target_pairs={{1,0},{2,1},{3,2},{5,4},{6,5},{7,6},{9,8},{10,9},{11,10},{13,12},{... | collective-permute-start | bytes 2727944 | tf_op jit(solution)/shard_map/ppermute | solution.py:762
  11.1 0.1 pad.15.clone
  11.1 0.1 pad_add_fusion
  11.3 0.7 reshape.42
  11.9 0.4 tile.17
  12.3 0.0 copy-start.6
  12.3 0.0 copy-start.7
  12.3 1.9 %tile.18.wt_ref = bf16[27,32,256]{2,1,0:T(8,128)(2,1)} reshape(bf16[27,32,8,32]{3,2,1,0:T(8,128)(2,1)S(1)} %tile.17) | data formatting | bytes 884736 | tf_op jit(solution)/shard_map/tile | solution.py:808
  14.3 0.7 pad_add_fusion.1.rows2_ref
  15.0 0.0 collective-permute-done.refs_0_
  15.0 1.5 %collective-permute-done.1.refs_1_ = bf16[37,48,256]{2,1,0:T(8,128)(2,1)} collective-permute-done((bf16[37,48,256]{2,1,0:T(8,128)(2,1)}, bf16[37,48,256]{2,1,0:T(8,128)(2,1)}, u32[]{:S(2)}, u32[]{:S(2)}) %collective-permute-start.1) | collective-permute-done | bytes 909344 | tf_op jit(solution)/shard_map/ppermute | solution.py:762
  16.5 1.1 fusion.2
  17.6 1.4 %pad_maximum_fusion = (bf16[37,48,256]{2,1,0:T(8,128)(2,1)}, bf16[37,48,256]{2,1,0:T(8,128)(2,1)}) fusion(bf16[37,16,256]{2,1,0:T(8,128)(2,1)S(1)} %get-tuple-element.79, bf16[37,16,256]{2,1,0:T(8,128)(2,1)S(1)} %copy-done.7, bf16[37,16,256]{2,1,0:T(8,128)(2,1)S(1)} %get-tuple-element.77, bf16[37,16,256]{2,1,0:T(8,128)(2,1)S(1)} %get-tuple-element.78, ...), kind=kLoop, calls=%fused_computation | loop fusion | flops 5455872 | bytes 3637248 | tf_op jit(solution)/shard_map/concatenate | solution.py:766
  19.0 3.5 %collective-permute-start.2 = (bf16[37,48,256]{2,1,0:T(8,128)(2,1)}, bf16[37,48,256]{2,1,0:T(8,128)(2,1)S(1)}, u32[]{:S(2)}, u32[]{:S(2)}) collective-permute-start(bf16[37,48,256]{2,1,0:T(8,128)(2,1)} %get-tuple-element.41), channel_id=1, source_target_pairs={{0,4},{4,8},{8,12},{12,16},{16,20},{20,24},{24,28},{1,5},{5,9},{9,... | collective-permute-start | bytes 2727944 | tf_op jit(solution)/shard_map/ppermute | solution.py:762
  22.5 1.3 %collective-permute-start.3 = (bf16[37,48,256]{2,1,0:T(8,128)(2,1)}, bf16[37,48,256]{2,1,0:T(8,128)(2,1)}, u32[]{:S(2)}, u32[]{:S(2)}) collective-permute-start(bf16[37,48,256]{2,1,0:T(8,128)(2,1)} %get-tuple-element.42), channel_id=1, source_target_pairs={{4,0},{8,4},{12,8},{16,12},{20,16},{24,20},{28,24},{5,1},{9,5},{13... | collective-permute-start | bytes 2727944 | tf_op jit(solution)/shard_map/ppermute | solution.py:762
  23.8 21.7 %dgrad.1 = (f32[64,64,256]{2,1,0:T(8,128)}, bf16[256,4096]{1,0:T(8,128)(2,1)}, bf16[2,256,512]{2,1,0:T(8,128)(2,1)}, bf16[9,256,256]{2,1,0:T(8,128)(2,1)}, bf16[...) custom-call(s32[1,1]{1,0:T(1,128)S(6)} %copy.35.count_ref, ...), custom_call_target="tpu_custom_call" | custom-call | flops 20000000000 | bytes 20000000 | tf_op jit(solution)/shard_map/dgrad/pallas_call | solution.py:359
  45.5 12.6 %collective-permute-start.4 = (bf16[37,48,256]{2,1,0:T(8,128)(2,1)}, bf16[37,48,256]{2,1,0:T(8,128)(2,1)S(1)}, u32[]{:S(2)}, u32[]{:S(2)}) collective-permute-start(bf16[37,48,256]{2,1,0:T(8,128)(2,1)} %get-tuple-element.45), channel_id=1, source_target_pairs={{0,1},{1,2},{2,3},{4,5},{5,6},{6,7},{8,9},{9,10},{10,11},{12,13},{... | collective-permute-start | bytes 2727944 | tf_op jit(solution)/shard_map/ppermute | solution.py:762
  58.1 1.3 %collective-permute-start.5 = (bf16[37,48,256]{2,1,0:T(8,128)(2,1)}, bf16[37,48,256]{2,1,0:T(8,128)(2,1)S(1)}, u32[]{:S(2)}, u32[]{:S(2)}) collective-permute-start(bf16[37,48,256]{2,1,0:T(8,128)(2,1)} %get-tuple-element.46), channel_id=1, source_target_pairs={{1,0},{2,1},{3,2},{5,4},{6,5},{7,6},{9,8},{10,9},{11,10},{13,12},{... | collective-permute-start | bytes 2727944 | tf_op jit(solution)/shard_map/ppermute | solution.py:762
  59.4 0.8 copy.24.cols_ref
  60.2 0.0 collective-permute-done.2.refs_2_
  60.2 0.0 collective-permute-done.3.refs_3_
  60.2 0.9 copy-done.5
  61.1 7.3 %halo.1 = (bf16[10,10,64,256]{3,2,1,0:T(8,128)(2,1)}, bf16[2,10,64,256]{3,2,1,0:T(8,128)(2,1)}, bf16[2,10,64,256]{3,2,1,0:T(8,128)(2,1)}) custom-call(bf16[64,64,256]{2,1,0:T(8,128)(2,1)} %get-tuple-element.36.fm_hbm, s32[192,9]{1,0:T(8,128)} %copy.24.cols_ref, bf16[37,48,256]{2,1,0:T(8,128)(2,1)} %copy-done.2, ...), custom_call_target="tpu_custom_call" | custom-call | flops 1000000 | bytes 1000 | tf_op jit(solution)/shard_map/halo/pallas_call | solution.py:508
  68.4 0.0 collective-permute-done.4.refs_0_
  68.4 0.0 collective-permute-done.5.refs_1_
  68.4 0.0 copy-start.1
  68.6 0.9 copy-done.9
  69.5 0.1 pad_maximum_fusion.2
  69.6 0.1 copy-done.1
  69.7 0.1 copy-done.8
  69.8 1.0 pad_maximum_fusion.3
  70.8 1.3 collective-permute-start.12
  72.1 5.1 %collective-permute-start.13 = (bf16[37,48,256]{2,1,0:T(8,128)(2,1)}, bf16[37,48,256]{2,1,0:T(8,128)(2,1)S(1)}, u32[]{:S(2)}, u32[]{:S(2)}) collective-permute-start(bf16[37,48,256]{2,1,0:T(8,128)(2,1)} %pad_maximum_fusion.3), channel_id=1, source_target_pairs={{0,4},{4,8},{8,12},{12,16},{16,20},{20,24},{24,28},{1,5},{5,9},{9,... | collective-permute-start | bytes 2727944 | tf_op jit(solution)/shard_map/ppermute | solution.py:762
  77.2 0.0 copy-start.14
  77.3 11.0 %wgrad.1 = f32[224,128]{1,0:T(8,128)} custom-call(bf16[10,10,64,256]{3,2,1,0:T(8,128)(2,1)} %get-tuple-element.52.refs_0_.vm_hbm, bf16[2,10,64,256]{3,2,1,0:T(8,128)(2,1)} %get-tuple-element.53.refs_1_.a_hbm, bf16[2,10,64,256]{3,2,1,0:T(8,128)(2,1)} %get-tuple-element.54.refs_2_.ax_hbm, bf16[256,4096]{1,0:T(8,128)(2,1)} %get-tuple-element.55.refs_3_, ...), custom_call_target="tpu_custom_call" | custom-call | flops 1000000 | bytes 1000 | tf_op jit(solution)/shard_map/wgrad/pallas_call | solution.py:590
  88.2 5.0 %collective-permute-start.7 = (f32[224,128]{1,0:T(8,128)}, f32[224,128]{1,0:T(8,128)S(1)}, u32[]{:S(2)}, u32[]{:S(2)}) collective-permute-start(f32[224,128]{1,0:T(8,128)} %wgrad.1), channel_id=1, source_target_pairs={{0,2},{1,3},{2,0},{3,1},{4,6},{5,7},{6,4},{7,5},{8,10},{9,11},{10,... | collective-permute-start | bytes 344072 | tf_op jit(solution)/shard_map/ppermute | solution.py:775
  93.2 0.7 collective-permute-start.8
  93.9 0.0 collective-permute-start.6
  93.9 3.2 %collective-permute-done.7 = f32[224,128]{1,0:T(8,128)S(1)} collective-permute-done((f32[224,128]{1,0:T(8,128)}, f32[224,128]{1,0:T(8,128)S(1)}, u32[]{:S(2)}, u32[]{:S(2)}) %collective-permute-start.7) | collective-permute-done | bytes 114720 | tf_op jit(solution)/shard_map/ppermute | solution.py:775
  97.1 2.8 %collective-permute-done.8 = f32[224,128]{1,0:T(8,128)S(1)} collective-permute-done((f32[224,128]{1,0:T(8,128)}, f32[224,128]{1,0:T(8,128)S(1)}, u32[]{:S(2)}, u32[]{:S(2)}) %collective-permute-start.8) | collective-permute-done | bytes 114720 | tf_op jit(solution)/shard_map/ppermute | solution.py:775
  99.9 0.0 collective-permute-done.6
  99.9 0.9 add_add_fusion.1
  100.8 3.4 %collective-permute-start.10 = (f32[224,128]{1,0:T(8,128)S(1)}, f32[224,128]{1,0:T(8,128)S(1)}, u32[]{:S(2)}, u32[]{:S(2)}) collective-permute-start(f32[224,128]{1,0:T(8,128)S(1)} %add_add_fusion.1), channel_id=1, source_target_pairs={{0,16},{4,20},{8,24},{12,28},{16,0},{20,4},{24,8},{28,12},{1,17},{... | collective-permute-start | bytes 344072 | tf_op jit(solution)/shard_map/ppermute | solution.py:775
  104.2 1.3 %collective-permute-start.11 = (f32[224,128]{1,0:T(8,128)S(1)}, f32[224,128]{1,0:T(8,128)S(1)}, u32[]{:S(2)}, u32[]{:S(2)}) collective-permute-start(f32[224,128]{1,0:T(8,128)S(1)} %add_add_fusion.1), channel_id=1, source_target_pairs={{0,24},{4,28},{8,16},{12,20},{16,8},{20,12},{24,0},{28,4},{1,25},{... | collective-permute-start | bytes 344072 | tf_op jit(solution)/shard_map/ppermute | solution.py:775
  105.5 0.3 collective-permute-start.9
  105.8 0.6 reshape_tile.3.bias_ref
  106.5 10.2 %forward.1 = bf16[64,64,256]{2,1,0:T(8,128)(2,1)} custom-call(s32[1,1]{1,0:T(1,128)S(6)} %copy.35.count_ref, bf16[10,10,64,256]{3,2,1,0:T(8,128)(2,1)} %get-tuple-element.52.refs_0_.vm_hbm, bf16[2,10,64,256]{3,2,1,0:T(8,128)(2,1)} %get-tuple-element.53.refs_1_.a_hbm, bf16[2,10,64,256]{3,2,1,0:T(8,128)(2,1)} %get-tuple-element.54.refs_2_.ax_hbm, ...), custom_call_target="tpu_custom_call" | custom-call | flops 1000000 | bytes 1000 | tf_op jit(solution)/shard_map/forward/pallas_call | solution.py:664
  116.7 0.0 collective-permute-done.10
  116.7 0.0 collective-permute-done.11
  116.7 0.0 collective-permute-done.9
  116.8 0.0 collective-permute-done.12.refs_3_
  116.8 0.2 collective-permute-done.13.refs_2_
  117.0 2.4 %collective-permute-start.14 = (f32[224,128]{1,0:T(8,128)S(1)}, f32[224,128]{1,0:T(8,128)S(1)}, u32[]{:S(2)}, u32[]{:S(2)}) collective-permute-start(f32[224,128]{1,0:T(8,128)S(1)} %add_add_fusion), channel_id=1, source_target_pairs={{0,4},{4,0},{8,12},{12,8},{16,20},{20,16},{24,28},{28,24},{1,5},{5... | collective-permute-start | bytes 344072 | tf_op jit(solution)/shard_map/ppermute | solution.py:771
  119.4 0.6 reshape_squeeze.7.slots_ref
  120.0 6.3 %finish.1 = bf16[64,64,256]{2,1,0:T(8,128)(2,1)} custom-call(s32[1,1]{1,0:T(1,128)S(6)} %copy.35.count_ref, f32[64,64,256]{2,1,0:T(8,128)} %get-tuple-element.64.own_hbm, s32[1,128]{1,0:T(1,128)} %reshape_squeeze.7.slots_ref, bf16[37,48,256]{2,1,0:T(8,128)(2,1)} %copy-done, bf16[37,48,256]{2,1,0:T(8,128)(2,1)} %copy-done.1, bf16[37,48,256]{2,1,0:T(8,128)(2,1)} %copy-done.4, ...), custom_call_target="tpu_custom_call" | custom-call | flops 5000000 | bytes 5000 | tf_op jit(solution)/shard_map/finish/pallas_call | solution.py:741
  126.2 0.0 collective-permute-done.14
  126.3 0.5 slice_reduce_fusion
  126.8 0.1 copy.26
  126.9 0.1 copy.27
  127.0 0.4 reshape.47
  127.4 1.0 copy.28
  (36 shorter events, 0.3 us)
Async XLA Ops:
  0.6 10.4 %copy-start.13 = (s32[1,1,64,26]{2,1,3,0:T(1,128)S(1)}, s32[1,1,64,26]{2,1,3,0:T(1,128)}, u32[]{:S(2)}) copy-start(s32[1,1,64,26]{2,1,3,0:T(1,128)} %param.13) | copy-start | bytes 19972
  0.6 11.3 %copy-start.10 = (bf16[3,3,3,32,32]{4,3,2,1,0:T(8,128)(2,1)S(1)}, bf16[3,3,3,32,32]{4,3,2,1,0:T(8,128)(2,1)}, u32[]{:S(2)}) copy-start(bf16[3,3,3,32,32]{4,3,2,1,0:T(8,128)(2,1)} %param.8) | copy-start | bytes 165892
  7.3 7.6 %collective-permute-start = (bf16[37,48,256]{2,1,0:T(8,128)(2,1)}, bf16[37,48,256]{2,1,0:T(8,128)(2,1)S(1)}, u32[]{:S(2)}, u32[]{:S(2)}) collective-permute-start(bf16[37,48,256]{2,1,0:T(8,128)(2,1)} %get-tuple-element.37), channel_id=1, source_target_pairs={{0,1},{1,2},{2,3},{4,5},{5,6},{6,7},{8,9},{9,10},{10,11},{12,13},{... | collective-permute-start | bytes 2727944 | tf_op jit(solution)/shard_map/ppermute | solution.py:762
  9.7 6.7 %collective-permute-start.1 = (bf16[37,48,256]{2,1,0:T(8,128)(2,1)}, bf16[37,48,256]{2,1,0:T(8,128)(2,1)}, u32[]{:S(2)}, u32[]{:S(2)}) collective-permute-start(bf16[37,48,256]{2,1,0:T(8,128)(2,1)} %get-tuple-element.38), channel_id=1, source_target_pairs={{1,0},{2,1},{3,2},{5,4},{6,5},{7,6},{9,8},{10,9},{11,10},{13,12},{... | collective-permute-start | bytes 2727944 | tf_op jit(solution)/shard_map/ppermute | solution.py:762
  12.3 5.3 %copy-start.6 = (bf16[37,16,256]{2,1,0:T(8,128)(2,1)S(1)}, bf16[37,16,256]{2,1,0:T(8,128)(2,1)}, u32[]{:S(2)}) copy-start(bf16[37,16,256]{2,1,0:T(8,128)(2,1)} %get-tuple-element.40) | copy-start | bytes 909316
  12.3 5.3 %copy-start.7 = (bf16[37,16,256]{2,1,0:T(8,128)(2,1)S(1)}, bf16[37,16,256]{2,1,0:T(8,128)(2,1)}, u32[]{:S(2)}) copy-start(bf16[37,16,256]{2,1,0:T(8,128)(2,1)} %get-tuple-element.39) | copy-start | bytes 909316
  15.0 4.0 %copy-start.2 = (bf16[37,48,256]{2,1,0:T(8,128)(2,1)}, bf16[37,48,256]{2,1,0:T(8,128)(2,1)S(1)}, u32[]{:S(2)}) copy-start(bf16[37,48,256]{2,1,0:T(8,128)(2,1)S(1)} %collective-permute-done.refs_0_) | copy-start | bytes 2727940
  19.0 41.2 %collective-permute-start.2 = (bf16[37,48,256]{2,1,0:T(8,128)(2,1)}, bf16[37,48,256]{2,1,0:T(8,128)(2,1)S(1)}, u32[]{:S(2)}, u32[]{:S(2)}) collective-permute-start(bf16[37,48,256]{2,1,0:T(8,128)(2,1)} %get-tuple-element.41), channel_id=1, source_target_pairs={{0,4},{4,8},{8,12},{12,16},{16,20},{20,24},{24,28},{1,5},{5,9},{9,... | collective-permute-start | bytes 2727944 | tf_op jit(solution)/shard_map/ppermute | solution.py:762
  22.5 37.7 %collective-permute-start.3 = (bf16[37,48,256]{2,1,0:T(8,128)(2,1)}, bf16[37,48,256]{2,1,0:T(8,128)(2,1)}, u32[]{:S(2)}, u32[]{:S(2)}) collective-permute-start(bf16[37,48,256]{2,1,0:T(8,128)(2,1)} %get-tuple-element.42), channel_id=1, source_target_pairs={{4,0},{8,4},{12,8},{16,12},{20,16},{24,20},{28,24},{5,1},{9,5},{13... | collective-permute-start | bytes 2727944 | tf_op jit(solution)/shard_map/ppermute | solution.py:762
  23.8 35.7 %copy-start.11 = (s32[192,9]{0,1:T(8,128)S(1)}, s32[192,9]{0,1:T(8,128)}, u32[]{:S(2)}) copy-start(s32[192,9]{0,1:T(8,128)} %reshape.42) | copy-start | bytes 20740
  45.5 22.9 %collective-permute-start.4 = (bf16[37,48,256]{2,1,0:T(8,128)(2,1)}, bf16[37,48,256]{2,1,0:T(8,128)(2,1)S(1)}, u32[]{:S(2)}, u32[]{:S(2)}) collective-permute-start(bf16[37,48,256]{2,1,0:T(8,128)(2,1)} %get-tuple-element.45), channel_id=1, source_target_pairs={{0,1},{1,2},{2,3},{4,5},{5,6},{6,7},{8,9},{9,10},{10,11},{12,13},{... | collective-permute-start | bytes 2727944 | tf_op jit(solution)/shard_map/ppermute | solution.py:762
  58.1 10.3 %collective-permute-start.5 = (bf16[37,48,256]{2,1,0:T(8,128)(2,1)}, bf16[37,48,256]{2,1,0:T(8,128)(2,1)S(1)}, u32[]{:S(2)}, u32[]{:S(2)}) collective-permute-start(bf16[37,48,256]{2,1,0:T(8,128)(2,1)} %get-tuple-element.46), channel_id=1, source_target_pairs={{1,0},{2,1},{3,2},{5,4},{6,5},{7,6},{9,8},{10,9},{11,10},{13,12},{... | collective-permute-start | bytes 2727944 | tf_op jit(solution)/shard_map/ppermute | solution.py:762
  60.2 0.9 copy-start.5
  68.4 1.1 copy-start.9
  68.4 1.2 copy-start
  68.4 1.2 copy-start.1
  68.5 1.3 %copy-start.8 = (bf16[37,16,256]{2,1,0:T(8,128)(2,1)S(1)}, bf16[37,16,256]{2,1,0:T(8,128)(2,1)}, u32[]{:S(2)}) copy-start(bf16[37,16,256]{2,1,0:T(8,128)(2,1)} %get-tuple-element.50) | copy-start | bytes 909316
  70.8 46.0 %collective-permute-start.12 = (bf16[37,48,256]{2,1,0:T(8,128)(2,1)S(1)}, bf16[37,48,256]{2,1,0:T(8,128)(2,1)S(1)}, u32[]{:S(2)}, u32[]{:S(2)}) collective-permute-start(bf16[37,48,256]{2,1,0:T(8,128)(2,1)S(1)} %pad_maximum_fusion.2), channel_id=1, source_target_pairs={{4,0},{8,4},{12,8},{16,12},{20,16},{24,20},{28,24},{5,1},{9,5},{13... | collective-permute-start | bytes 2727944 | tf_op jit(solution)/shard_map/ppermute | solution.py:762
  72.1 44.9 %collective-permute-start.13 = (bf16[37,48,256]{2,1,0:T(8,128)(2,1)}, bf16[37,48,256]{2,1,0:T(8,128)(2,1)S(1)}, u32[]{:S(2)}, u32[]{:S(2)}) collective-permute-start(bf16[37,48,256]{2,1,0:T(8,128)(2,1)} %pad_maximum_fusion.3), channel_id=1, source_target_pairs={{0,4},{4,8},{8,12},{12,16},{16,20},{20,24},{24,28},{1,5},{5,9},{9,... | collective-permute-start | bytes 2727944 | tf_op jit(solution)/shard_map/ppermute | solution.py:762
  77.2 28.6 %copy-start.14 = (f32[32]{0:T(128)S(1)}, f32[32]{0:T(128)}, u32[]{:S(2)}) copy-start(f32[32]{0:T(128)} %param.9) | copy-start | bytes 388
  88.2 8.9 %collective-permute-start.7 = (f32[224,128]{1,0:T(8,128)}, f32[224,128]{1,0:T(8,128)S(1)}, u32[]{:S(2)}, u32[]{:S(2)}) collective-permute-start(f32[224,128]{1,0:T(8,128)} %wgrad.1), channel_id=1, source_target_pairs={{0,2},{1,3},{2,0},{3,1},{4,6},{5,7},{6,4},{7,5},{8,10},{9,11},{10,... | collective-permute-start | bytes 344072 | tf_op jit(solution)/shard_map/ppermute | solution.py:775
  93.2 6.7 %collective-permute-start.8 = (f32[224,128]{1,0:T(8,128)}, f32[224,128]{1,0:T(8,128)S(1)}, u32[]{:S(2)}, u32[]{:S(2)}) collective-permute-start(f32[224,128]{1,0:T(8,128)} %wgrad.1), channel_id=1, source_target_pairs={{0,3},{1,2},{2,1},{3,0},{4,7},{5,6},{6,5},{7,4},{8,11},{9,10},{10,... | collective-permute-start | bytes 344072 | tf_op jit(solution)/shard_map/ppermute | solution.py:775
  93.9 6.0 %collective-permute-start.6 = (f32[224,128]{1,0:T(8,128)}, f32[224,128]{1,0:T(8,128)S(1)}, u32[]{:S(2)}, u32[]{:S(2)}) collective-permute-start(f32[224,128]{1,0:T(8,128)} %wgrad.1), channel_id=1, source_target_pairs={{0,1},{1,0},{2,3},{3,2},{4,5},{5,4},{6,7},{7,6},{8,9},{9,8},{10,11... | collective-permute-start | bytes 344072 | tf_op jit(solution)/shard_map/ppermute | solution.py:775
  100.8 15.9 %collective-permute-start.10 = (f32[224,128]{1,0:T(8,128)S(1)}, f32[224,128]{1,0:T(8,128)S(1)}, u32[]{:S(2)}, u32[]{:S(2)}) collective-permute-start(f32[224,128]{1,0:T(8,128)S(1)} %add_add_fusion.1), channel_id=1, source_target_pairs={{0,16},{4,20},{8,24},{12,28},{16,0},{20,4},{24,8},{28,12},{1,17},{... | collective-permute-start | bytes 344072 | tf_op jit(solution)/shard_map/ppermute | solution.py:775
  104.2 12.5 %collective-permute-start.11 = (f32[224,128]{1,0:T(8,128)S(1)}, f32[224,128]{1,0:T(8,128)S(1)}, u32[]{:S(2)}, u32[]{:S(2)}) collective-permute-start(f32[224,128]{1,0:T(8,128)S(1)} %add_add_fusion.1), channel_id=1, source_target_pairs={{0,24},{4,28},{8,16},{12,20},{16,8},{20,12},{24,0},{28,4},{1,25},{... | collective-permute-start | bytes 344072 | tf_op jit(solution)/shard_map/ppermute | solution.py:775
  105.5 11.2 %collective-permute-start.9 = (f32[224,128]{1,0:T(8,128)S(1)}, f32[224,128]{1,0:T(8,128)S(1)}, u32[]{:S(2)}, u32[]{:S(2)}) collective-permute-start(f32[224,128]{1,0:T(8,128)S(1)} %add_add_fusion.1), channel_id=1, source_target_pairs={{0,8},{4,12},{8,0},{12,4},{16,24},{20,28},{24,16},{28,20},{1,9},{5... | collective-permute-start | bytes 344072 | tf_op jit(solution)/shard_map/ppermute | solution.py:775
  106.5 12.9 %copy-start.12 = (s32[1,1,8,16]{3,2,1,0:T(8,128)S(1)}, s32[1,1,8,16]{3,2,1,0:T(8,128)}, u32[]{:S(2)}) copy-start(s32[1,1,8,16]{3,2,1,0:T(8,128)} %param.12) | copy-start | bytes 1540
  116.8 3.2 %copy-start.3 = (bf16[37,48,256]{2,1,0:T(8,128)(2,1)}, bf16[37,48,256]{2,1,0:T(8,128)(2,1)S(1)}, u32[]{:S(2)}) copy-start(bf16[37,48,256]{2,1,0:T(8,128)(2,1)S(1)} %collective-permute-done.12.refs_3_) | copy-start | bytes 2727940
  117.0 3.0 %copy-start.4 = (bf16[37,48,256]{2,1,0:T(8,128)(2,1)}, bf16[37,48,256]{2,1,0:T(8,128)(2,1)S(1)}, u32[]{:S(2)}) copy-start(bf16[37,48,256]{2,1,0:T(8,128)(2,1)S(1)} %collective-permute-done.13.refs_2_) | copy-start | bytes 2727940
  117.0 9.2 %collective-permute-start.14 = (f32[224,128]{1,0:T(8,128)S(1)}, f32[224,128]{1,0:T(8,128)S(1)}, u32[]{:S(2)}, u32[]{:S(2)}) collective-permute-start(f32[224,128]{1,0:T(8,128)S(1)} %add_add_fusion), channel_id=1, source_target_pairs={{0,4},{4,0},{8,12},{12,8},{16,20},{20,16},{24,28},{28,24},{1,5},{5... | collective-permute-start | bytes 344072 | tf_op jit(solution)/shard_map/ppermute | solution.py:771
